TPU v7x, 1024 devices: a whole 8x8x8 slice. The times are simulated.
1024 devices in a mesh: blk: 256 (over z, x_hi, y), grp: 4 (over x_lo, core).
Axes of the slice: x: 8 (x_hi: 4, x_lo: 2; x = x_hi * 2 + x_lo), y: 8, z: 8, core: 2. Of those that a mesh axis runs over, the one named last changes fastest.
Arguments:
- queries: bfloat16 [131072, 4096], P(('blk', 'grp')), may hold values from -0.1875 to 0.1875
- passages: bfloat16 [2048, 4096], P(('blk', 'grp')), may hold values from -5 to 5
- pool: bfloat16 [131072, 4096], P(('blk', 'grp')), may hold values from -5 to 5
- positive_ids: int32 [131072], P(('blk', 'grp')), may hold values from 0 to 511
- request_lists: int32 [1024, 4, 32], P(('blk', 'grp')), may hold values from 0 to 127, as said below
- hard_refs: int32 [131072, 30], P(('blk', 'grp')), may hold values from 0 to 127, as said below
- hard_count: int32 [131072], P(('blk', 'grp')), may hold values from 1 to 30
Outputs:
- query_grad: bfloat16 [131072, 4096], P(('blk', 'grp'))
- query_loss: float32 [131072], P(('blk', 'grp'))
Inputs may be any that keep to these rules, and one draw needn't show every extreme that they name: `request_lists`: entries of one list are distinct rows of that owner's 128 pool rows. `hard_refs`: the first hard_count entries of a row are distinct; later entries are padding and unused.
All inputs are finite; a program needn't handle non-finite values.
Results may differ from a plain program's by a relative error of at most 0.0034.
Values may be sent and summed in bfloat16 or wider, within the bound.
No kernel may reach another device: no remote copies, remote signals or barrier semaphores. Data moves between devices by JAX's collectives and lax.ppermute only.
A program may use at most 32 MiB of HBM per device.

v0:
```python
import jax
import jax.numpy as jnp
from jax import lax
from jax.sharding import PartitionSpec as P


def hard_mask(refs, count, span):
    table_iota = jnp.arange(span, dtype=jnp.int32)
    order = jnp.arange(refs.shape[1], dtype=jnp.int32)
    live = order[None, :] < count[:, None]
    hits = (refs[:, :, None] == table_iota[None, None, :]) & live[:, :, None]
    return jnp.sum(hits.astype(jnp.float32), axis=1)


def body(queries, passages, pool, positive_ids, request_lists, hard_refs, hard_count):
    owners = request_lists.shape[1]
    slot_count = request_lists.shape[2]
    gathered = lax.all_gather(pool, "grp", axis=0, tiled=True)
    pool_depth = pool.shape[0]
    owner_base = jnp.arange(owners, dtype=jnp.int32)[:, None] * pool_depth
    row_index = (owner_base + request_lists[0]).reshape(owners * slot_count)
    hard_table = gathered[row_index]
    hard_logits = jnp.dot(queries, hard_table.T, preferred_element_type=jnp.float32)
    present = hard_mask(hard_refs, hard_count, owners * slot_count)
    hard_peak = jnp.max(jnp.where(present > 0, hard_logits, -jnp.inf), axis=1)
    cycle_rows = lax.all_gather(passages, "blk", axis=0, tiled=True)
    cycle_logits = jnp.dot(queries, cycle_rows.T, preferred_element_type=jnp.float32)
    peak_value = jnp.maximum(hard_peak, jnp.max(cycle_logits, axis=1))
    cycle_exp = jnp.exp(cycle_logits - peak_value[:, None])
    hard_exp = present * jnp.exp(hard_logits - peak_value[:, None])
    denominator = jnp.sum(cycle_exp, axis=1) + jnp.sum(hard_exp, axis=1)
    cycle_iota = jnp.arange(cycle_rows.shape[0], dtype=jnp.int32)
    onehot = (cycle_iota[None, :] == positive_ids[:, None]).astype(jnp.float32)
    chosen = jnp.sum(cycle_logits * onehot, axis=1)
    cycle_weights = (cycle_exp / denominator[:, None] - onehot).astype(jnp.bfloat16)
    cycle_part = jnp.dot(cycle_weights, cycle_rows, preferred_element_type=jnp.float32)
    hard_weights = (hard_exp / denominator[:, None]).astype(jnp.bfloat16)
    gradient = cycle_part + jnp.dot(hard_weights, hard_table, preferred_element_type=jnp.float32)
    query_loss = jnp.log(denominator) + peak_value - chosen
    return (gradient.astype(jnp.bfloat16), query_loss)


def solution(mesh):
    return jax.shard_map(
        body,
        mesh=mesh,
        in_specs=(
            P(("blk", "grp"), None),
            P(("blk", "grp"), None),
            P(("blk", "grp"), None),
            P(("blk", "grp")),
            P(("blk", "grp"), None, None),
            P(("blk", "grp"), None),
            P(("blk", "grp")),
        ),
        out_specs=(P(("blk", "grp"), None), P(("blk", "grp"))),
        check_vma=False,
    )
```

profile of v0, /device:TPU:1, one launch (start us, length us, event | category | flops | bytes accessed | tf_op | source)
XLA Modules:
  0.0 244.0 jit_solution(918667819417339015)
XLA Ops:
  7.2 0.0 copy-start
  7.2 0.0 all-gather.4.cloned.1.call-start
  7.2 0.7 all-gather.4.cloned.1.call-update
  7.9 0.0 all-gather.6.cloned.1.call-start
  8.0 0.7 all-gather.6.cloned.1.call-update
  8.7 0.8 squeeze.3
  9.4 0.1 add.44
  9.5 0.1 add.45
  9.6 0.7 iota_compare_fusion.2
  10.3 3.1 %convert_reduce_fusion = f32[128,128]{1,0:T(8,128)S(1)} fusion(s32[128,30]{0,1:T(8,128)} %param.12, pred[128,30]{0,1:T(8,128)(4,1)S(1)} %iota_compare_fusion.2), kind=kLoop, calls=%fused_computation.3 | loop fusion | flops 1949696 | bytes 84736 | tf_op jit(solution)/shard_map/reduce_sum | solution.py:12
  13.4 0.1 copy.11
  13.5 64.3 %all-gather.4.cloned.1.call-done = bf16[512,4096]{1,0:T(8,128)(2,1)} async-done(((bf16[128,4096]{1,0:T(8,128)(2,1)}), bf16[512,4096]{1,0:T(8,128)(2,1)}) %all-gather.4.cloned.1.call-update) | async-done | bytes 4194320 | tf_op jit(solution)/shard_map/all_gather | solution.py:18
  77.8 4.9 %gather_fusion = bf16[128,4096]{1,0:T(8,128)(2,1)S(1)} fusion(bf16[512,4096]{1,0:T(8,128)(2,1)} %all-gather.4.cloned.1.call-done, s32[1024]{0:T(1024)S(1)} %pad_clamp_fusion), kind=kCustom, calls=%fused_computation | custom fusion | bytes 2097664 | tf_op jit(solution)/shard_map/gather | solution.py:22
  82.7 0.0 copy-done
  82.7 0.5 select_reduce_fusion.1
  83.2 139.7 %all-gather.6.cloned.1.call-done = bf16[256,2,4096]{2,1,0:T(2,128)(2,1)} async-done(((bf16[1,2,4096]{2,1,0:T(2,128)(2,1)}), bf16[256,2,4096]{2,1,0:T(2,128)(2,1)}) %all-gather.6.cloned.1.call-update) | async-done | bytes 4194320 | tf_op jit(solution)/shard_map/all_gather | solution.py:26
  222.9 7.2 %reshape.80 = bf16[512,4096]{1,0:T(8,128)(2,1)} reshape(bf16[256,2,4096]{2,1,0:T(2,128)(2,1)} %all-gather.6.cloned.1.call-done) | data formatting | bytes 8388608
  230.1 0.0 copy-start.2
  230.1 0.0 copy-start.1
  230.1 3.9 %fusion.10 = (f32[128]{0:T(128)S(1)}, f32[128,512]{1,0:T(8,128)S(1)}) fusion(bf16[128,4096]{1,0:T(8,128)(2,1)S(1)} %copy-done, bf16[512,4096]{1,0:T(8,128)(2,1)} %reshape.80), kind=kOutput, calls=%fused_computation.27 | convolution fusion | flops 536936320 | bytes 5505536 | tf_op jit(solution)/shard_map/dot_general | solution.py:27
  234.1 0.0 copy-done.2
  234.1 0.2 select_reduce_fusion
  234.3 0.5 add_subtract_fusion
  234.9 0.0 copy-done.1
  234.9 0.8 fusion.3
  235.7 1.5 fusion
  (5 shorter events, 0.1 us)
Async XLA Ops:
  7.2 75.6 %copy-start = (bf16[128,4096]{1,0:T(8,128)(2,1)S(1)}, bf16[128,4096]{1,0:T(8,128)(2,1)}, u32[]{:S(2)}) copy-start(bf16[128,4096]{1,0:T(8,128)(2,1)} %param.7) | copy-start | bytes 3145732
  7.2 70.6 %all-gather.4.cloned.1.call-start = ((), (), s32[]{:S(2)}) async-start(), calls=%async_computation | async-start | bytes 5242880 | tf_op jit(solution)/shard_map/all_gather | solution.py:18
  7.9 215.0 %all-gather.6.cloned.1.call-start = ((), (), s32[]{:S(2)}) async-start(), calls=%async_computation.1 | async-start | bytes 4210688 | tf_op jit(solution)/shard_map/all_gather | solution.py:26
  230.1 4.0 %copy-start.2 = (s32[128]{0:T(128)S(1)}, s32[128]{0:T(128)}, u32[]{:S(2)}) copy-start(s32[128]{0:T(128)} %param.10) | copy-start | bytes 1540
  230.1 4.8 %copy-start.1 = (bf16[512,4096]{1,0:T(8,128)(2,1)S(1)}, bf16[512,4096]{1,0:T(8,128)(2,1)}, u32[]{:S(2)}) copy-start(bf16[512,4096]{1,0:T(8,128)(2,1)} %reshape.80) | copy-start | bytes 12582916
Sparse Core Ops, SparseCore 0:
  10.7 67.0 all-gather.3
  83.6 139.2 all-gather.5
where the time goes:
time: 246 us; the launch traced here: 244 us
  waiting for transfers between devices  205 us (83%)
  between operations  14.1 us (6%)
  local copies, waits for them, and re-layouts  13.2 us (5%)
  matrix products  6.64 us (3%)
  other arithmetic  4.62 us (2%)
    all_gather x1, waiting for transfers between devices, body(): cycle_rows = lax.all_gather(passages, 'blk', axis=0, tiled=True)  140 us
    all_gather x1, waiting for transfers between devices, body(): gathered = lax.all_gather(pool, 'grp', axis=0, tiled=True)  64.3 us
    unnamed x7, local copies, waits for them, and re-layouts  7.22 us
    gather x1, local copies, waits for them, and re-layouts, body(): hard_table = gathered[row_index]  4.93 us
  transfers between devices with their start and end apart: 2, of which 2 were waited for; matrix products, arithmetic and copies ran while one was open for 4% of the time, Pallas kernels for 0%

commit v1 on v0

v1 whole, which is shorter than its diff:
```python
import jax
import jax.numpy as jnp
from jax import lax
from jax.sharding import Mesh, PartitionSpec as P

AXES = ("z", "xh", "y", "xl", "c")
SIZES = (8, 4, 8, 2, 2)
WIDE = 3328


def hard_mask(refs, count, span):
    table_iota = jnp.arange(span, dtype=jnp.int32)
    order = jnp.arange(refs.shape[1], dtype=jnp.int32)
    live = order[None, :] < count[:, None]
    hits = (refs[:, :, None] == table_iota[None, None, :]) & live[:, :, None]
    return jnp.sum(hits.astype(jnp.float32), axis=1)


def spread(block, axes, members):
    copies = jnp.broadcast_to(block[None], (members,) + block.shape)
    return lax.all_to_all(copies, axes, 0, 0, tiled=True)


def dots(a, b):
    return lax.dot_general(a, b, (((1,), (1,)), ((), ())), preferred_element_type=jnp.float32)


def body(queries, passages, pool, positive_ids, request_lists, hard_refs, hard_count):
    depth = pool.shape[0]
    width = passages.shape[1]
    rest = width - WIDE
    slots = request_lists.shape[1] * request_lists.shape[2]

    with jax.named_scope("near_wide"):
        near_a = spread(passages[:, :WIDE], ("xh", "y"), 32).reshape(64, WIDE)
    with jax.named_scope("far_wide"):
        rows_a = lax.all_gather(near_a, "z", axis=0, tiled=True)
    tail, near_a = lax.optimization_barrier((passages[:, WIDE:], near_a))
    with jax.named_scope("near_rest"):
        near_b = spread(tail, ("z", "xh"), 32).reshape(64, rest)
    near_b, pool = lax.optimization_barrier((near_b, pool))
    with jax.named_scope("pool_x"):
        pool_x = lax.ppermute(pool, "xl", [(0, 1), (1, 0)])
        pool_c = lax.ppermute(pool, "c", [(0, 1), (1, 0)])
    with jax.named_scope("far_rest"):
        far_b = spread(near_b, "y", 8)
        rows_b = far_b.reshape(8, 32, 2, rest).transpose(1, 0, 2, 3).reshape(512, rest)
    with jax.named_scope("pool_xc"):
        pool_xc = lax.ppermute(pool_x, "c", [(0, 1), (1, 0)])

    with jax.named_scope("hard_logits"):
        present = hard_mask(hard_refs, hard_count, slots)
        xl, c = lax.axis_index("xl"), lax.axis_index("c")
        holders = jnp.stack([xl * 2 + c, xl * 2 + 1 - c, (1 - xl) * 2 + c, (1 - xl) * 2 + 1 - c])
        slot_owner = jnp.arange(slots, dtype=jnp.int32) // request_lists.shape[2]
        slot_row = request_lists.reshape(slots)
        place = jnp.arange(4 * depth, dtype=jnp.int32)
        match = (slot_owner[:, None] == jnp.repeat(holders, depth)[None, :]) & (
            slot_row[:, None] == (place % depth)[None, :]
        )
        present = jnp.dot(
            present.astype(jnp.bfloat16), match.astype(jnp.bfloat16), preferred_element_type=jnp.float32
        )
        pools = (pool, pool_c, pool_x, pool_xc)
        hard_logits = jnp.concatenate([dots(queries, p) for p in pools], axis=1)
        hard_peak = jnp.max(jnp.where(present > 0, hard_logits, -jnp.inf), axis=1)
    with jax.named_scope("cycle_logits"):
        logits_b = dots(queries[:, WIDE:], rows_b)
        cycle_logits = dots(queries[:, :WIDE], rows_a) + logits_b
        peak_value = jnp.maximum(hard_peak, jnp.max(cycle_logits, axis=1))
        cycle_exp = jnp.exp(cycle_logits - peak_value[:, None])
        hard_exp = jnp.where(present > 0, present * jnp.exp(hard_logits - peak_value[:, None]), 0.0)
        denominator = jnp.sum(cycle_exp, axis=1) + jnp.sum(hard_exp, axis=1)
        cycle_iota = jnp.arange(512, dtype=jnp.int32)
        onehot = (cycle_iota[None, :] == positive_ids[:, None]).astype(jnp.float32)
        chosen = jnp.sum(cycle_logits * onehot, axis=1)
    with jax.named_scope("gradient"):
        cycle_weights = (cycle_exp / denominator[:, None] - onehot).astype(jnp.bfloat16)
        hard_weights = (hard_exp / denominator[:, None]).astype(jnp.bfloat16)
        hard_part = sum(
            jnp.dot(hard_weights[:, i * depth : (i + 1) * depth], p, preferred_element_type=jnp.float32)
            for i, p in enumerate(pools)
        )
        part_a = jnp.dot(cycle_weights, rows_a, preferred_element_type=jnp.float32)
        part_b = jnp.dot(cycle_weights, rows_b, preferred_element_type=jnp.float32)
        gradient = jnp.concatenate([part_a + hard_part[:, :WIDE], part_b + hard_part[:, WIDE:]], axis=1)
        query_loss = jnp.log(denominator) + peak_value - chosen
    return (gradient.astype(jnp.bfloat16), query_loss)


def solution(mesh):
    grid = Mesh(mesh.devices.reshape(SIZES), AXES)
    return jax.shard_map(
        body,
        mesh=grid,
        in_specs=(
            P(AXES, None),
            P(AXES, None),
            P(AXES, None),
            P(AXES),
            P(AXES, None, None),
            P(AXES, None),
            P(AXES),
        ),
        out_specs=(P(AXES, None), P(AXES)),
        check_vma=False,
    )
```

time: 246 us -> 134 us (0.54)
  waiting for transfers between devices: 205 us -> 12.9 us
  blocking collectives: 0 us -> 60.6 us
  starting transfers between devices: 0.08 us -> 16.1 us
  matrix products: 6.64 us -> 14.3 us
  local copies, waits for them, and re-layouts: 13.2 us -> 9.95 us
    all_gather x2 -> x1, waiting for transfers between devices: 204 us -> 0.02 us  [body(): rows_a = lax.all_gather(near_a, 'z', axis=0, tiled=True)]
    all_to_all x0 -> x2, blocking collectives: none -> 60.6 us  [spread(): return lax.all_to_all(copies, axes, 0, 0, tiled=True)]
    ppermute x0 -> x3, starting transfers between devices: none -> 11.8 us  [the longest x1 5.2 us: body(): pool_xc = lax.ppermute(pool_x, 'c', [(0, 1), (1, 0)])]
    ppermute x0 -> x3, waiting for transfers between devices: none -> 9.44 us  [the longest x1 9.43 us: body(): pool_x = lax.ppermute(pool, 'xl', [(0, 1), (1, 0)])]
    dot_general x4 -> x13, matrix products: 6.64 us -> 14.3 us  [the longest x6 8.6 us: dots(): lax.dot_general(a, b, (((1,), (1,)), ((), ())), preferred_element_type=jn...]
    unnamed x7 -> x28, local copies, waits for them, and re-layouts: 7.22 us -> 0.79 us
    gather x1 -> x0, local copies, waits for them, and re-layouts: 4.93 us -> none  [body(): hard_table = gathered[row_index]]
    all_to_all x0 -> x1, starting transfers between devices: none -> 4.21 us  [spread(): return lax.all_to_all(copies, axes, 0, 0, tiled=True)]
  transfers between devices with their start and end apart: 2 -> 5, of which waited for: 2 -> 2; matrix products, arithmetic and copies ran while one was open for 4% -> 11% of each run, Pallas kernels for 0% -> 0%
where the time goes in v1:
time: 134 us; the launch traced here: 133 us
  blocking collectives  60.6 us (45%)
  starting transfers between devices  16.1 us (12%)
  matrix products  14.3 us (11%)
  between operations  14.3 us (11%)
  waiting for transfers between devices  12.9 us (10%)
  local copies, waits for them, and re-layouts  9.95 us (7%)
  other arithmetic  4.79 us (4%)
    all_to_all x2, blocking collectives, spread(): return lax.all_to_all(copies, axes, 0, 0, tiled=True)  60.6 us
    ppermute x1, waiting for transfers between devices, body(): pool_x = lax.ppermute(pool, 'xl', [(0, 1), (1, 0)])  9.43 us
    dot_general x6, matrix products, dots(): lax.dot_general(a, b, (((1,), (1,)), ((), ())), preferred_element_type=jn...  8.6 us
    ppermute x1, starting transfers between devices, body(): pool_xc = lax.ppermute(pool_x, 'c', [(0, 1), (1, 0)])  5.2 us
    ppermute x1, starting transfers between devices, body(): pool_c = lax.ppermute(pool, 'c', [(0, 1), (1, 0)])  4.35 us
    dot_general x4, matrix products, body(): jnp.dot(hard_weights[:, i * depth:(i + 1) * depth], p, preferred_element_...  4.28 us
    all_to_all x1, starting transfers between devices, spread(): return lax.all_to_all(copies, axes, 0, 0, tiled=True)  4.21 us
    all_to_all x1, waiting for transfers between devices, spread(): return lax.all_to_all(copies, axes, 0, 0, tiled=True)  3.43 us
  transfers between devices with their start and end apart: 5, of which 2 were waited for; matrix products, arithmetic and copies ran while one was open for 11% of the time, Pallas kernels for 0%

profile of v1, /device:TPU:1, one launch (start us, length us, event | category | flops | bytes accessed | tf_op | source)
XLA Modules:
  0.0 133.0 jit_solution(3974166810218337069)
XLA Ops:
  7.2 0.0 slice-start
  7.2 0.0 copy-start.2
  7.2 0.0 copy-start.12
  7.2 0.0 all-gather.2.cloned.1.call-start
  7.2 0.8 slice.31
  8.0 0.2 broadcast_in_dim.12
  8.3 28.8 %all_to_all.15 = bf16[32,2,3328]{2,1,0:T(2,128)(2,1)S(1)} all-to-all(bf16[32,2,3328]{2,1,0:T(2,128)(2,1)S(1)} %broadcast_in_dim.12), channel_id=1, replica_groups=mesh['z'=8,'xh'=4,'y'=8,'xl'=2,'c'=2] {'xh','y'}, dimensions={0} | all-to-all | bytes 851968 | tf_op jit(solution)/shard_map/near_wide/all_to_all | solution.py:21
  37.1 0.9 reshape.78
  38.0 0.0 all-gather.2.cloned.1.call-update
  38.0 0.0 slice-done
  38.1 0.1 broadcast_in_dim.13
  38.1 31.8 %all_to_all.16 = bf16[32,2,768]{2,1,0:T(2,128)(2,1)S(1)} all-to-all(bf16[32,2,768]{2,1,0:T(2,128)(2,1)S(1)} %broadcast_in_dim.13), channel_id=1, replica_groups=mesh['z'=8,'xh'=4,'y'=8,'xl'=2,'c'=2] {'z','xh'}, dimensions={0} | all-to-all | bytes 196608 | tf_op jit(solution)/shard_map/near_rest/all_to_all | solution.py:21
  70.0 0.0 copy-done.2
  70.0 2.3 %collective-permute-start.1 = (bf16[128,4096]{1,0:T(8,128)(2,1)S(1)}, bf16[128,4096]{1,0:T(8,128)(2,1)S(1)}, u32[]{:S(2)}, u32[]{:S(2)}) collective-permute-start(bf16[128,4096]{1,0:T(8,128)(2,1)S(1)} %copy-done.2), channel_id=1, source_target_pairs={{0,2},{2,0},{1,3},{3,1},{4,6},{6,4},{5,7},{7,5},{8,10},{10,8},{9,1... | collective-permute-start | bytes 3145736 | tf_op jit(solution)/shard_map/pool_x/ppermute | solution.py:43
  72.3 0.6 and_select_fusion
  72.9 0.0 copy-done.12
  72.9 4.3 %collective-permute-start = (bf16[128,4096]{1,0:T(8,128)(2,1)S(1)}, bf16[128,4096]{1,0:T(8,128)(2,1)}, u32[]{:S(2)}, u32[]{:S(2)}) collective-permute-start(bf16[128,4096]{1,0:T(8,128)(2,1)S(1)} %copy-done.2), channel_id=1, source_target_pairs={{0,1},{1,0},{2,3},{3,2},{4,5},{5,4},{6,7},{7,6},{8,9},{9,8},{10,11... | collective-permute-start | bytes 3145736 | tf_op jit(solution)/shard_map/pool_x/ppermute | solution.py:44
  77.2 0.9 broadcast_in_dim.14
  78.2 4.2 %all-to-all-start.2 = ((bf16[8,64,768]{2,1,0:T(8,128)(2,1)}), bf16[8,64,768]{2,1,0:T(8,128)(2,1)}, u32[]{:S(2)}, u32[]{:S(2)}) async-start(bf16[8,64,768]{2,1,0:T(8,128)(2,1)} %broadcast_in_dim.14), calls=%async_computation.2 | async-start | bytes 1572864 | tf_op jit(solution)/shard_map/far_rest/all_to_all | solution.py:21
  82.4 0.1 pad_add_fusion
  82.5 0.0 copy-done.10
  82.5 0.1 eq.65
  82.6 0.0 copy-done.9
  82.6 2.1 %convert_reduce_fusion = bf16[128,128]{1,0:T(8,128)(2,1)} fusion(s32[128,30]{0,1:T(8,128)S(1)} %copy-done.9, pred[128,30]{0,1:T(8,128)(4,1)S(1)} %iota_compare_fusion.2), kind=kLoop, calls=%fused_computation.3 | loop fusion | flops 1949696 | bytes 51968 | tf_op jit(solution)/shard_map/hard_logits/reduce_sum | solution.py:16
  84.7 9.4 %collective-permute-done.1 = bf16[128,4096]{1,0:T(8,128)(2,1)S(1)} collective-permute-done((bf16[128,4096]{1,0:T(8,128)(2,1)S(1)}, bf16[128,4096]{1,0:T(8,128)(2,1)S(1)}, u32[]{:S(2)}, u32[]{:S(2)}) %collective-permute-start.1) | collective-permute-done | bytes 1048608 | tf_op jit(solution)/shard_map/pool_x/ppermute | solution.py:43
  94.1 5.2 %collective-permute-start.2 = (bf16[128,4096]{1,0:T(8,128)(2,1)S(1)}, bf16[128,4096]{1,0:T(8,128)(2,1)}, u32[]{:S(2)}, u32[]{:S(2)}) collective-permute-start(bf16[128,4096]{1,0:T(8,128)(2,1)S(1)} %collective-permute-done.1), channel_id=1, source_target_pairs={{0,1},{1,0},{2,3},{3,2},{4,5},{5,4},{6,7},{7,6},{8,9},{9,8},{10,11... | collective-permute-start | bytes 3145736 | tf_op jit(solution)/shard_map/pool_xc/ppermute | solution.py:49
  99.4 0.1 broadcast_bitcast_fusion
  99.4 0.0 copy-done
  99.4 0.4 convolution_bitcast_fusion.4
  99.9 0.4 convolution_bitcast_fusion.2
  100.3 0.0 collective-permute-done
  100.3 2.3 %convolution_bitcast_fusion.3 = f32[128,128]{1,0:T(8,128)} fusion(bf16[128,4096]{1,0:T(8,128)(2,1)} %collective-permute-done, bf16[128,4096]{1,0:T(8,128)(2,1)S(1)} %copy-done), kind=kOutput, calls=%fused_computation.12 | convolution fusion | flops 134217728 | bytes 2162688 | tf_op jit(solution)/shard_map/hard_logits/dot_general | solution.py:25
  102.6 3.4 %all-to-all-done.2 = bf16[8,64,768]{2,1,0:T(8,128)(2,1)} async-done(((bf16[8,64,768]{2,1,0:T(8,128)(2,1)}), bf16[8,64,768]{2,1,0:T(8,128)(2,1)}, u32[]{:S(2)}, u32[]{:S(2)}) %all-to-all-start.2) | async-done | bytes 786464 | tf_op jit(solution)/shard_map/far_rest/all_to_all | solution.py:21
  106.1 1.6 %copy.36 = bf16[8,64,768]{2,0,1:T(8,128)(2,1)S(1)} copy(bf16[8,64,768]{2,1,0:T(8,128)(2,1)} %all-to-all-done.2) | data formatting | bytes 1572864 | tf_op jit(solution)/shard_map/far_rest/all_to_all | solution.py:21
  107.6 1.5 %copy.37 = bf16[32,8,2,768]{3,2,1,0:T(2,128)(2,1)} copy(bf16[32,8,2,768]{3,1,2,0:T(8,128)(2,1)S(1)} %bitcast.38) | data formatting | bytes 1572864 | tf_op jit(solution)/shard_map/far_rest/transpose | solution.py:47
  109.1 2.9 %reshape.81 = bf16[512,768]{1,0:T(8,128)(2,1)} reshape(bf16[32,8,2,768]{3,2,1,0:T(2,128)(2,1)} %copy.37) | data formatting | bytes 1572864 | tf_op jit(solution)/shard_map/far_rest/reshape | solution.py:47
  112.1 0.0 collective-permute-done.2
  112.1 1.7 %convolution_bitcast_fusion.1 = f32[128,128]{1,0:T(8,128)S(1)} fusion(bf16[128,4096]{1,0:T(8,128)(2,1)} %collective-permute-done.2, bf16[128,4096]{1,0:T(8,128)(2,1)S(1)} %copy-done), kind=kOutput, calls=%fused_computation.10 | convolution fusion | flops 134217728 | bytes 2162688 | tf_op jit(solution)/shard_map/hard_logits/dot_general | solution.py:25
  113.8 0.0 copy-start.6
  113.8 0.6 copy-done.6
  114.4 0.0 copy-done.4
  114.4 0.0 copy-done.8
  114.4 0.0 copy-done.13
  114.4 0.4 select_reduce_fusion.1
  114.8 0.0 copy-start.11
  114.8 0.0 all-gather.2.cloned.1.call-done
  114.8 0.0 copy-start.3
  114.8 0.0 copy-start.5
  114.8 0.0 copy-start.7
  114.8 3.3 %fusion.3 = f32[128,512]{1,0:T(8,128)S(1)} fusion(bf16[512,3328]{1,0:T(8,128)(2,1)} %all-gather.2.cloned.1.call-done, bf16[128,4096]{1,0:T(8,128)(2,1)S(1)} %copy-done), kind=kOutput, calls=%fused_computation.15 | convolution fusion | flops 436207616 | bytes 4521984 | tf_op jit(solution)/shard_map/cycle_logits/dot_general | solution.py:25
  118.1 0.0 copy-done.3
  118.1 0.5 fusion.28
  118.6 0.3 select_reduce_fusion
  118.9 0.5 add_subtract_fusion
  119.5 0.1 divide_convert_fusion
  119.6 0.4 fusion.19
  120.0 1.6 %convolution_add_fusion.2 = f32[128,4096]{1,0:T(8,128)S(1)} fusion(f32[128,4096]{1,0:T(8,128)S(1)} %fusion.19, bf16[128,4096]{1,0:T(8,128)(2,1)} %collective-permute-done, bf16[128,512]{1,0:T(8,128)(2,1)S(1)} %divide_convert_fusion), kind=kOutput, calls=%fused_computation.2 | convolution fusion | flops 134742016 | bytes 5275648 | tf_op jit(solution)/shard_map/gradient/dot_general | solution.py:81
  121.6 0.4 convolution_add_fusion.1
  122.1 0.0 copy-start.1
  122.1 1.8 %convolution_add_fusion = f32[128,4096]{1,0:T(8,128)S(1)} fusion(f32[128,4096]{1,0:T(8,128)S(1)} %convolution_add_fusion.1, bf16[128,4096]{1,0:T(8,128)(2,1)} %collective-permute-done.2, bf16[128,512]{1,0:T(8,128)(2,1)S(1)} %divide_convert_fusion), kind=kOutput, calls=%fused_computation | convolution fusion | flops 134742016 | bytes 5275648 | tf_op jit(solution)/shard_map/gradient/dot_general | solution.py:81
  123.9 0.3 fusion.5
  124.2 0.1 copy-done.1
  124.3 0.7 fusion.1
  125.1 1.1 pad_maximum_fusion
  (13 shorter events, 0.1 us)
Async XLA Ops:
  7.2 30.9 %slice-start = ((bf16[2,4096]{1,0:T(2,128)(2,1)}), bf16[2,768]{1,0:T(2,128)(2,1)S(1)}, s32[]{:S(2)}) async-start(bf16[2,4096]{1,0:T(2,128)(2,1)} %param.8), calls=%async_computation.4 | async-start | bytes 6144 | tf_op jit(solution)/shard_map/slice | solution.py:38
  7.2 62.8 %copy-start.2 = (bf16[128,4096]{1,0:T(8,128)(2,1)S(1)}, bf16[128,4096]{1,0:T(8,128)(2,1)}, u32[]{:S(2)}) copy-start(bf16[128,4096]{1,0:T(8,128)(2,1)} %param.9) | copy-start | bytes 3145732
  7.2 65.7 %copy-start.12 = (s32[128]{0:T(128)S(1)}, s32[128]{0:T(128)}, u32[]{:S(2)}) copy-start(s32[128]{0:T(128)} %param.13) | copy-start | bytes 1540
  7.2 107.6 %all-gather.2.cloned.1.call-start = ((), (), s32[]{:S(2)}) async-start(), calls=%async_computation.3 | async-start | bytes 3833856 | tf_op jit(solution)/shard_map/far_wide/all_gather | solution.py:37
  37.1 45.4 %copy-start.10 = (s32[1,4,32]{2,1,0:T(4,128)S(1)}, s32[1,4,32]{2,1,0:T(4,128)}, u32[]{:S(2)}) copy-start(s32[1,4,32]{2,1,0:T(4,128)} %param.11) | copy-start | bytes 1540
  37.1 45.5 %copy-start.9 = (s32[128,30]{0,1:T(8,128)S(1)}, s32[128,30]{0,1:T(8,128)}, u32[]{:S(2)}) copy-start(s32[128,30]{0,1:T(8,128)} %param.12) | copy-start | bytes 46084
  37.1 62.3 %copy-start = (bf16[128,4096]{1,0:T(8,128)(2,1)S(1)}, bf16[128,4096]{1,0:T(8,128)(2,1)}, u32[]{:S(2)}) copy-start(bf16[128,4096]{1,0:T(8,128)(2,1)} %param.7) | copy-start | bytes 3145732
  70.0 24.2 %collective-permute-start.1 = (bf16[128,4096]{1,0:T(8,128)(2,1)S(1)}, bf16[128,4096]{1,0:T(8,128)(2,1)S(1)}, u32[]{:S(2)}, u32[]{:S(2)}) collective-permute-start(bf16[128,4096]{1,0:T(8,128)(2,1)S(1)} %copy-done.2), channel_id=1, source_target_pairs={{0,2},{2,0},{1,3},{3,1},{4,6},{6,4},{5,7},{7,5},{8,10},{10,8},{9,1... | collective-permute-start | bytes 3145736 | tf_op jit(solution)/shard_map/pool_x/ppermute | solution.py:43
  72.9 27.4 %collective-permute-start = (bf16[128,4096]{1,0:T(8,128)(2,1)S(1)}, bf16[128,4096]{1,0:T(8,128)(2,1)}, u32[]{:S(2)}, u32[]{:S(2)}) collective-permute-start(bf16[128,4096]{1,0:T(8,128)(2,1)S(1)} %copy-done.2), channel_id=1, source_target_pairs={{0,1},{1,0},{2,3},{3,2},{4,5},{5,4},{6,7},{7,6},{8,9},{9,8},{10,11... | collective-permute-start | bytes 3145736 | tf_op jit(solution)/shard_map/pool_x/ppermute | solution.py:44
  78.2 27.9 %all-to-all-start.2 = ((bf16[8,64,768]{2,1,0:T(8,128)(2,1)}), bf16[8,64,768]{2,1,0:T(8,128)(2,1)}, u32[]{:S(2)}, u32[]{:S(2)}) async-start(bf16[8,64,768]{2,1,0:T(8,128)(2,1)} %broadcast_in_dim.14), calls=%async_computation.2 | async-start | bytes 1572864 | tf_op jit(solution)/shard_map/far_rest/all_to_all | solution.py:21
  94.1 17.9 %collective-permute-start.2 = (bf16[128,4096]{1,0:T(8,128)(2,1)S(1)}, bf16[128,4096]{1,0:T(8,128)(2,1)}, u32[]{:S(2)}, u32[]{:S(2)}) collective-permute-start(bf16[128,4096]{1,0:T(8,128)(2,1)S(1)} %collective-permute-done.1), channel_id=1, source_target_pairs={{0,1},{1,0},{2,3},{3,2},{4,5},{5,4},{6,7},{7,6},{8,9},{9,8},{10,11... | collective-permute-start | bytes 3145736 | tf_op jit(solution)/shard_map/pool_xc/ppermute | solution.py:49
  112.1 2.3 %copy-start.4 = (f32[128,128]{1,0:T(8,128)S(1)}, f32[128,128]{1,0:T(8,128)}, u32[]{:S(2)}) copy-start(f32[128,128]{1,0:T(8,128)} %convolution_bitcast_fusion.3) | copy-start | bytes 196612
  112.1 2.3 %copy-start.8 = (bf16[128,128]{1,0:T(8,128)(2,1)S(1)}, bf16[128,128]{1,0:T(8,128)(2,1)}, u32[]{:S(2)}) copy-start(bf16[128,128]{1,0:T(8,128)(2,1)} %convert_reduce_fusion) | copy-start | bytes 98308
  112.1 2.3 %copy-start.13 = (s32[128]{0:T(128)S(1)}, s32[128]{0:T(128)}, u32[]{:S(2)}) copy-start(s32[128]{0:T(128)} %and_select_fusion) | copy-start | bytes 1540
  113.8 0.6 copy-start.6
  114.8 3.8 %copy-start.11 = (s32[128]{0:T(128)S(1)}, s32[128]{0:T(128)}, u32[]{:S(2)}) copy-start(s32[128]{0:T(128)} %param.10) | copy-start | bytes 1540
  114.8 3.3 %copy-start.3 = (bf16[512,768]{1,0:T(8,128)(2,1)S(1)}, bf16[512,768]{1,0:T(8,128)(2,1)}, u32[]{:S(2)}) copy-start(bf16[512,768]{1,0:T(8,128)(2,1)} %reshape.81) | copy-start | bytes 2359300
  114.8 3.8 %copy-start.5 = (f32[128,128]{1,0:T(8,128)S(1)}, f32[128,128]{1,0:T(8,128)}, u32[]{:S(2)}) copy-start(f32[128,128]{1,0:T(8,128)} %convolution_bitcast_fusion.3) | copy-start | bytes 196612
  114.8 3.8 %copy-start.7 = (f32[128,128]{1,0:T(8,128)S(1)}, f32[128,128]{1,0:T(8,128)}, u32[]{:S(2)}) copy-start(f32[128,128]{1,0:T(8,128)} %copy-done.6) | copy-start | bytes 196612
  122.1 2.3 %copy-start.1 = (bf16[512,3328]{1,0:T(8,128)(2,1)S(1)}, bf16[512,3328]{1,0:T(8,128)(2,1)}, u32[]{:S(2)}) copy-start(bf16[512,3328]{1,0:T(8,128)(2,1)} %all-gather.2.cloned.1.call-done) | copy-start | bytes 10223620
Sparse Core Ops, SparseCore 0:
  38.2 62.1 all-gather.1

commit v2 on v1

v2 whole, which is shorter than its diff:
```python
import jax
import jax.numpy as jnp
import numpy as np
from jax import lax
from jax.sharding import Mesh, PartitionSpec as P

DEVICES = np.arange(1024).reshape(8, 4, 8, 2, 2)


def lines(order):
    return DEVICES.transpose(order)


ALONG_Y = lines((0, 1, 3, 4, 2))
ALONG_Z = lines((1, 2, 3, 4, 0))
CROSS = lines((0, 2, 3, 1, 4)).reshape(-1, 8).tolist()
NEAR = np.concatenate([ALONG_Y[:, :, :, 0].reshape(-1, 8), ALONG_Z[:, :, :, 1].reshape(-1, 8)]).tolist()
FAR = np.concatenate([ALONG_Z[:, :, :, 0].reshape(-1, 8), ALONG_Y[:, :, :, 1].reshape(-1, 8)]).tolist()
OTHER_CORE = [(i, i ^ 1) for i in range(1024)]
OTHER_CHIP = [(i, i ^ 2) for i in range(1024)]


def hard_mask(refs, count, span):
    table_iota = jnp.arange(span, dtype=jnp.int32)
    order = jnp.arange(refs.shape[1], dtype=jnp.int32)
    live = order[None, :] < count[:, None]
    hits = (refs[:, :, None] == table_iota[None, None, :]) & live[:, :, None]
    return jnp.sum(hits.astype(jnp.float32), axis=1)


def dots(a, b):
    return lax.dot_general(a, b, (((1,), (1,)), ((), ())), preferred_element_type=jnp.float32)


def body(queries, passages, pool, positive_ids, request_lists, hard_refs, hard_count):
    depth = pool.shape[0]
    half = passages.shape[1] // 2
    slots = request_lists.shape[1] * request_lists.shape[2]
    device = lax.axis_index("d")
    core = device % 2
    chip = (device // 2) % 2

    with jax.named_scope("cross"):
        halves = passages.reshape(2, 2, half).transpose(1, 0, 2)
        sent = jnp.broadcast_to(halves[None], (4, 2, 2, half)).reshape(8, 2, half)
        got = lax.all_to_all(sent, "d", 0, 0, axis_index_groups=CROSS, tiled=True)
        got = got.reshape(4, 2, 2, half).transpose(1, 0, 2, 3).reshape(2, 8, half)
        got = jnp.where(core == 0, got, got[::-1])
    with jax.named_scope("near"):
        sent = jnp.broadcast_to(got.reshape(1, 16, half), (8, 16, half))
        near = lax.all_to_all(sent, "d", 0, 0, axis_index_groups=NEAR, tiled=True)
        near = near.reshape(8, 2, 8, half).transpose(1, 0, 2, 3).reshape(128, half)
    with jax.named_scope("far"):
        far = lax.all_gather(near, "d", axis_index_groups=FAR, axis=0, tiled=True).reshape(8, 2, 64, half)
    near, pool = lax.optimization_barrier((near, pool))
    with jax.named_scope("pools"):
        pool_x = lax.ppermute(pool, "d", OTHER_CHIP)
        pool_c = lax.ppermute(pool, "d", OTHER_CORE)
        pool_xc = lax.ppermute(pool_x, "d", OTHER_CORE)

    with jax.named_scope("hard_logits"):
        present = hard_mask(hard_refs, hard_count, slots)
        own = chip * 2 + core
        holders = jnp.stack([own, own ^ 1, own ^ 2, own ^ 3])
        slot_owner = jnp.arange(slots, dtype=jnp.int32) // request_lists.shape[2]
        slot_row = request_lists.reshape(slots)
        place = jnp.arange(4 * depth, dtype=jnp.int32)
        match = (slot_owner[:, None] == jnp.repeat(holders, depth)[None, :]) & (
            slot_row[:, None] == (place % depth)[None, :]
        )
        present = jnp.dot(
            present.astype(jnp.bfloat16), match.astype(jnp.bfloat16), preferred_element_type=jnp.float32
        )
        pools = (pool, pool_c, pool_x, pool_xc)
        hard_logits = jnp.concatenate([dots(queries, p) for p in pools], axis=1)
        hard_peak = jnp.max(jnp.where(present > 0, hard_logits, -jnp.inf), axis=1)

    far, hard_logits, present, hard_peak, pool_xc = lax.optimization_barrier(
        (far, hard_logits, present, hard_peak, pool_xc)
    )
    with jax.named_scope("swap"):
        swapped = far[:, 1].reshape(8, 8, 8, half).transpose(1, 0, 2, 3).reshape(512, half)
        swapped = lax.ppermute(swapped, "d", OTHER_CORE)
        rows_own = far[:, 0].reshape(512, half)
    with jax.named_scope("cycle_logits"):
        queries_own = lax.dynamic_slice_in_dim(queries, core * half, half, 1)
        queries_swap = lax.dynamic_slice_in_dim(queries, (1 - core) * half, half, 1)
        cycle_logits = dots(queries_own, rows_own) + dots(queries_swap, swapped)
        peak_value = jnp.maximum(hard_peak, jnp.max(cycle_logits, axis=1))
        cycle_exp = jnp.exp(cycle_logits - peak_value[:, None])
        hard_exp = jnp.where(present > 0, present * jnp.exp(hard_logits - peak_value[:, None]), 0.0)
        denominator = jnp.sum(cycle_exp, axis=1) + jnp.sum(hard_exp, axis=1)
        place = jnp.arange(512, dtype=jnp.int32)
        outer, inner, hi, row = place // 64, (place // 8) % 8, (place // 2) % 4, place % 2
        far_z, far_y = jnp.where(core == 0, outer, inner), jnp.where(core == 0, inner, outer)
        index = ((far_z * 4 + hi) * 8 + far_y) * 2 + row
        onehot = (index[None, :] == positive_ids[:, None]).astype(jnp.float32)
        chosen = jnp.sum(cycle_logits * onehot, axis=1)
    with jax.named_scope("gradient"):
        cycle_weights = (cycle_exp / denominator[:, None] - onehot).astype(jnp.bfloat16)
        hard_weights = (hard_exp / denominator[:, None]).astype(jnp.bfloat16)
        hard_part = sum(
            jnp.dot(hard_weights[:, i * depth : (i + 1) * depth], p, preferred_element_type=jnp.float32)
            for i, p in enumerate((pool, pool_c, pool_x, pool_xc))
        )
        part_own = jnp.dot(cycle_weights, rows_own, preferred_element_type=jnp.float32)
        part_swap = jnp.dot(cycle_weights, swapped, preferred_element_type=jnp.float32)
        low = jnp.where(core == 0, part_own, part_swap)
        high = jnp.where(core == 0, part_swap, part_own)
        gradient = jnp.concatenate([low, high], axis=1) + hard_part
        query_loss = jnp.log(denominator) + peak_value - chosen
    return (gradient.astype(jnp.bfloat16), query_loss)


def solution(mesh):
    flat = Mesh(mesh.devices.reshape(1024), ("d",))
    return jax.shard_map(
        body,
        mesh=flat,
        in_specs=(P("d", None), P("d", None), P("d", None), P("d"), P("d", None, None), P("d", None), P("d")),
        out_specs=(P("d", None), P("d")),
        check_vma=False,
    )
```

time: 134 us -> 127 us (0.948)
  blocking collectives: 60.6 us -> 19.2 us
  waiting for transfers between devices: 12.9 us -> 31.3 us
  starting transfers between devices: 16.1 us -> 31.7 us
  other arithmetic: 4.79 us -> 3.23 us
  matrix products: 14.3 us -> 15.8 us
    all_to_all x2 -> x1, blocking collectives: 60.6 us -> 19.2 us  [body(): near = lax.all_to_all(sent, 'd', 0, 0, axis_index_groups=NEAR, tiled=True)]
    all_to_all x1, starting transfers between devices: 4.21 us -> 17.4 us  [body(): got = lax.all_to_all(sent, 'd', 0, 0, axis_index_groups=CROSS, tiled=True)]
    ppermute x3 -> x4, waiting for transfers between devices: 9.44 us -> 19.7 us  [the longest x1 18.9 us: body(): pool_x = lax.ppermute(pool, 'd', OTHER_CHIP)]
    all_gather x1, waiting for transfers between devices: 0.02 us -> 4.17 us  [body(): lax.all_gather(near, 'd', axis_index_groups=FAR, axis=0, tiled=True)]
    all_to_all x1, waiting for transfers between devices: 3.43 us -> 7.47 us  [body(): got = lax.all_to_all(sent, 'd', 0, 0, axis_index_groups=CROSS, tiled=True)]
    reshape x3 -> x1, local copies, waits for them, and re-layouts: 3.93 us -> 0.88 us  [body(): halves = passages.reshape(2, 2, half).transpose(1, 0, 2)]
    transpose x1 -> x5, local copies, waits for them, and re-layouts: 1.49 us -> 4.13 us  [the longest x2 3.22 us: body(): far[:, 1].reshape(8, 8, 8, half).transpose(1, 0, 2, 3).reshape(512, half)]
    ppermute x3 -> x4, starting transfers between devices: 11.8 us -> 14.3 us  [the longest x1 8.24 us: body(): swapped = lax.ppermute(swapped, 'd', OTHER_CORE)]
  transfers between devices with their start and end apart: 5 -> 6, of which waited for: 2 -> 4; matrix products, arithmetic and copies ran while one was open for 11% -> 9% of each run, Pallas kernels for 0% -> 0%
where the time goes in v2:
time: 127 us; the launch traced here: 126 us
  starting transfers between devices  31.7 us (25%)
  waiting for transfers between devices  31.3 us (25%)
  blocking collectives  19.2 us (15%)
  matrix products  15.8 us (12%)
  between operations  14.4 us (11%)
  local copies, waits for them, and re-layouts  10.7 us (8%)
  other arithmetic  3.23 us (3%)
    all_to_all x1, blocking collectives, body(): near = lax.all_to_all(sent, 'd', 0, 0, axis_index_groups=NEAR, tiled=True)  19.2 us
    ppermute x1, waiting for transfers between devices, body(): pool_x = lax.ppermute(pool, 'd', OTHER_CHIP)  18.9 us
    all_to_all x1, starting transfers between devices, body(): got = lax.all_to_all(sent, 'd', 0, 0, axis_index_groups=CROSS, tiled=True)  17.4 us
    ppermute x1, starting transfers between devices, body(): swapped = lax.ppermute(swapped, 'd', OTHER_CORE)  8.24 us
    all_to_all x1, waiting for transfers between devices, body(): got = lax.all_to_all(sent, 'd', 0, 0, axis_index_groups=CROSS, tiled=True)  7.47 us
    dot_general x6, matrix products, dots(): lax.dot_general(a, b, (((1,), (1,)), ((), ())), preferred_element_type=jn...  7.32 us
    dot_general x4, matrix products, body(): jnp.dot(hard_weights[:, i * depth:(i + 1) * depth], p, preferred_element_...  5.41 us
    all_gather x1, waiting for transfers between devices, body(): lax.all_gather(near, 'd', axis_index_groups=FAR, axis=0, tiled=True)  4.17 us
  transfers between devices with their start and end apart: 6, of which 4 were waited for; matrix products, arithmetic and copies ran while one was open for 9% of the time, Pallas kernels for 0%

profile of v2, /device:TPU:1, one launch (start us, length us, event | category | flops | bytes accessed | tf_op | source)
XLA Modules:
  0.0 126.3 jit_solution(17746207480572314615)
XLA Ops:
  7.2 0.0 copy-start
  7.2 0.0 copy-start.1
  7.2 0.0 copy-start.11
  7.2 0.0 copy-start.8
  7.2 0.9 reshape.152
  8.1 0.0 copy-start.10
  8.1 0.7 broadcast_in_dim.12
  8.8 17.4 %all-to-all-start = ((bf16[8,2,2048]{2,1,0:T(2,128)(2,1)}), bf16[8,2,2048]{2,1,0:T(2,128)(2,1)S(1)}, u32[]{:S(2)}, u32[]{:S(2)}) async-start(bf16[8,2,2048]{2,1,0:T(2,128)(2,1)} %bitcast.1), calls=%async_computation | async-start | bytes 131072 | tf_op jit(solution)/shard_map/cross/all_to_all | solution.py:46
  26.2 0.0 all-gather.2.cloned.1.call-start
  26.2 7.5 %all-to-all-done = bf16[8,2,2048]{2,1,0:T(2,128)(2,1)S(1)} async-done(((bf16[8,2,2048]{2,1,0:T(2,128)(2,1)}), bf16[8,2,2048]{2,1,0:T(2,128)(2,1)S(1)}, u32[]{:S(2)}, u32[]{:S(2)}) %all-to-all-start) | async-done | bytes 65568 | tf_op jit(solution)/shard_map/cross/all_to_all | solution.py:46
  33.7 0.1 copy.47
  33.7 0.7 rev.3
  34.4 0.1 broadcast_select_fusion.2
  34.6 19.2 %all_to_all.10 = bf16[8,16,2048]{2,1,0:T(8,128)(2,1)S(1)} all-to-all(bf16[8,16,2048]{2,1,0:T(8,128)(2,1)S(1)} %broadcast_in_dim.14), channel_id=1, replica_groups={{0,4,8,12,16,20,24,28},{2,6,10,14,18,22,26,30},{32,36,40,44,48,52,56,60..., dimensions={0} | all-to-all | bytes 1048576 | tf_op jit(solution)/shard_map/near/all_to_all | solution.py:51
  53.8 0.8 copy.49
  54.6 0.0 all-gather.2.cloned.1.call-update
  54.6 0.0 copy-done.1
  54.7 2.2 %collective-permute-start.1 = (bf16[128,4096]{1,0:T(8,128)(2,1)S(1)}, bf16[128,4096]{1,0:T(8,128)(2,1)S(1)}, u32[]{:S(2)}, u32[]{:S(2)}) collective-permute-start(bf16[128,4096]{1,0:T(8,128)(2,1)S(1)} %copy-done.1), channel_id=1, source_target_pairs={{0,2},{1,3},{2,0},{3,1},{4,6},{5,7},{6,4},{7,5},{8,10},{9,11},{10,... | collective-permute-start | bytes 3145736 | tf_op jit(solution)/shard_map/pools/ppermute | solution.py:57
  57.0 0.0 copy-done.11
  57.0 0.0 copy-done.8
  57.0 1.5 %convert_reduce_fusion = bf16[128,128]{1,0:T(8,128)(2,1)S(1)} fusion(s32[128,30]{0,1:T(8,128)S(1)} %copy-done.8, pred[128,30]{0,1:T(8,128)(4,1)S(1)} %iota_compare_fusion.1), kind=kLoop, calls=%fused_computation.6 | loop fusion | flops 1949696 | bytes 51968 | tf_op jit(solution)/shard_map/hard_logits/reduce_sum | solution.py:28
  58.5 1.9 %collective-permute-start = (bf16[128,4096]{1,0:T(8,128)(2,1)S(1)}, bf16[128,4096]{1,0:T(8,128)(2,1)}, u32[]{:S(2)}, u32[]{:S(2)}) collective-permute-start(bf16[128,4096]{1,0:T(8,128)(2,1)S(1)} %copy-done.1), channel_id=1, source_target_pairs={{0,1},{1,0},{2,3},{3,2},{4,5},{5,4},{6,7},{7,6},{8,9},{9,8},{10,11... | collective-permute-start | bytes 3145736 | tf_op jit(solution)/shard_map/pools/ppermute | solution.py:58
  60.5 0.1 pad_add_fusion
  60.5 0.0 copy-done.10
  60.6 0.1 eq.79
  60.6 0.1 broadcast_bitcast_fusion
  60.7 18.9 %collective-permute-done.1 = bf16[128,4096]{1,0:T(8,128)(2,1)S(1)} collective-permute-done((bf16[128,4096]{1,0:T(8,128)(2,1)S(1)}, bf16[128,4096]{1,0:T(8,128)(2,1)S(1)}, u32[]{:S(2)}, u32[]{:S(2)}) %collective-permute-start.1) | collective-permute-done | bytes 1048608 | tf_op jit(solution)/shard_map/pools/ppermute | solution.py:57
  79.6 1.9 %collective-permute-start.2 = (bf16[128,4096]{1,0:T(8,128)(2,1)S(1)}, bf16[128,4096]{1,0:T(8,128)(2,1)}, u32[]{:S(2)}, u32[]{:S(2)}) collective-permute-start(bf16[128,4096]{1,0:T(8,128)(2,1)S(1)} %collective-permute-done.1), channel_id=1, source_target_pairs={{0,1},{1,0},{2,3},{3,2},{4,5},{5,4},{6,7},{7,6},{8,9},{9,8},{10,11... | collective-permute-start | bytes 3145736 | tf_op jit(solution)/shard_map/pools/ppermute | solution.py:59
  81.5 0.3 fusion.9
  81.8 0.9 copy.50
  82.7 0.0 copy-done
  82.7 0.4 convolution_bitcast_fusion.3
  83.1 0.4 convolution_bitcast_fusion.1
  83.5 0.0 copy-done.3
  83.6 0.0 copy-start.7
  83.6 0.0 collective-permute-done
  83.6 1.7 %convolution_bitcast_fusion.2 = f32[128,128]{0,1:T(8,128)S(1)} fusion(bf16[128,4096]{1,0:T(8,128)(2,1)} %collective-permute-done, bf16[128,4096]{1,0:T(8,128)(2,1)S(1)} %copy-done), kind=kOutput, calls=%fused_computation.12 | convolution fusion | flops 134217728 | bytes 2162688 | tf_op jit(solution)/shard_map/hard_logits/dot_general | solution.py:32
  85.3 0.0 collective-permute-done.2
  85.3 1.7 %convolution_bitcast_fusion = f32[128,128]{0,1:T(8,128)S(1)} fusion(bf16[128,4096]{1,0:T(8,128)(2,1)} %collective-permute-done.2, bf16[128,4096]{1,0:T(8,128)(2,1)S(1)} %copy-done), kind=kOutput, calls=%fused_computation.10 | convolution fusion | flops 134217728 | bytes 2162688 | tf_op jit(solution)/shard_map/hard_logits/dot_general | solution.py:32
  87.0 0.7 select_reduce_fusion
  87.7 4.2 %all-gather.2.cloned.1.call-done = bf16[1024,2048]{1,0:T(8,128)(2,1)} async-done(((bf16[128,2048]{1,0:T(8,128)(2,1)}), bf16[1024,2048]{1,0:T(8,128)(2,1)}) %all-gather.2.cloned.1.call-update) | async-done | bytes 4194320 | tf_op jit(solution)/shard_map/far/all_gather | solution.py:54
  91.9 1.7 %slice_bitcast_fusion = bf16[8,8,8,2048]{3,2,0,1:T(8,128)(2,1)S(1)} fusion(bf16[8,2,64,2048]{3,2,1,0:T(8,128)(2,1)} %bitcast.54), kind=kLoop, calls=%fused_computation.5 | loop fusion | bytes 4194304 | tf_op jit(solution)/shard_map/swap/transpose | solution.py:82
  93.6 1.5 %copy.52 = bf16[8,8,8,2048]{3,2,1,0:T(8,128)(2,1)} copy(bf16[8,8,8,2048]{3,2,0,1:T(8,128)(2,1)S(1)} %slice_bitcast_fusion) | data formatting | bytes 4194304 | tf_op jit(solution)/shard_map/swap/transpose | solution.py:82
  95.1 8.2 %collective-permute-start.3 = (bf16[512,2048]{1,0:T(8,128)(2,1)}, bf16[512,2048]{1,0:T(8,128)(2,1)}, u32[]{:S(2)}, u32[]{:S(2)}) collective-permute-start(bf16[512,2048]{1,0:T(8,128)(2,1)} %bitcast.22), channel_id=1, source_target_pairs={{0,1},{1,0},{2,3},{3,2},{4,5},{5,4},{6,7},{7,6},{8,9},{9,8},{10,11... | collective-permute-start | bytes 6291464 | tf_op jit(solution)/shard_map/swap/ppermute | solution.py:83
  103.4 1.7 %slice.18 = bf16[8,1,64,2048]{3,2,1,0:T(8,128)(2,1)S(1)} slice(bf16[8,2,64,2048]{3,2,1,0:T(8,128)(2,1)} %bitcast.55), slice={[0:8], [0:1], [0:64], [0:2048]} | slice | bytes 4194304 | tf_op jit(solution)/shard_map/swap/slice | solution.py:84
  105.1 0.8 copy.55
  106.0 0.7 fusion.4
  106.7 0.0 copy-start.5
  106.7 0.0 copy-start.6
  106.7 0.0 copy-start.9
  106.7 0.8 collective-permute-done.3
  107.5 2.3 %fusion.52 = (f32[128]{0:T(128)S(1)}, f32[128,512]{0,1:T(8,128)S(1)}) fusion(f32[128,512]{0,1:T(8,128)S(1)} %fusion.4, bf16[512,2048]{1,0:T(8,128)(2,1)} %collective-permute-done.3, bf16[128,4096]{1,0:T(8,128)(2,1)S(1)} %copy-done, s32[]{:T(128)S(6)} %select_n.150), kind=kOutput, calls=%fused_computation.99 | convolution fusion | flops 268566400 | bytes 3146244 | tf_op jit(solution)/shard_map/cycle_logits/dot_general | solution.py:32
  109.9 0.2 fusion.8
  110.0 0.5 add_subtract_fusion
  110.6 0.1 divide_convert_fusion
  110.6 2.2 %fusion.48 = f32[128,2048]{1,0:T(8,128)S(1)} fusion(bf16[512,2048]{1,0:T(8,128)(2,1)} %collective-permute-done.3, f32[128,512]{0,1:T(8,128)S(1)} %get-tuple-element.24, s32[128]{0:T(128)S(1)} %copy-done.9, f32[128]{0:T(128)S(1)} %get-tuple-element.18, f32[128]{0:T(128)S(1)} %max.3, s32[512]{0:T(512)S(1)} %fusion.34), kind=kOutput, calls=%fused_computation.97 | convolution fusion | flops 268828672 | bytes 3411456 | tf_op jit(solution)/shard_map/gradient/dot_general | solution.py:107
  112.8 0.0 copy-start.2
  112.8 0.6 broadcast_select_fusion.1
  113.5 0.6 copy-done.2
  114.1 0.5 fusion.22
  114.5 0.0 copy-start.4
  114.5 1.8 %convolution_add_fusion.2 = f32[128,4096]{1,0:T(8,128)S(1)} fusion(f32[128,4096]{1,0:T(8,128)S(1)} %fusion.22, bf16[128,4096]{1,0:T(8,128)(2,1)} %collective-permute-done, bf16[128,512]{0,1:T(8,128)(2,1)S(1)} %divide_convert_fusion), kind=kOutput, calls=%fused_computation.3 | convolution fusion | flops 134742016 | bytes 5275648 | tf_op jit(solution)/shard_map/gradient/dot_general | solution.py:103
  116.3 0.5 convolution_add_fusion.1
  116.8 2.7 %fusion.1 = bf16[128,4096]{1,0:T(8,128)(2,1)} fusion(f32[128,4096]{1,0:T(8,128)S(1)} %convolution_add_fusion.1, bf16[128,4096]{1,0:T(8,128)(2,1)} %collective-permute-done.2, f32[128,2048]{1,0:T(8,128)S(1)} %get-tuple-element.20, f32[128,2048]{1,0:T(8,128)S(1)} %get-tuple-element.19, bf16[128,512]{0,1:T(8,128)(2,1)S(1)} %divide_convert_fusion), kind=kOutput, calls=%fused_computation.4 | convolution fusion | flops 136314880 | bytes 6324224 | tf_op jit(solution)/shard_map/gradient/dot_general | solution.py:103
  (14 shorter events, 0.1 us)
Async XLA Ops:
  7.2 75.5 %copy-start = (bf16[128,4096]{1,0:T(8,128)(2,1)S(1)}, bf16[128,4096]{1,0:T(8,128)(2,1)}, u32[]{:S(2)}) copy-start(bf16[128,4096]{1,0:T(8,128)(2,1)} %param.7) | copy-start | bytes 3145732
  7.2 47.5 %copy-start.1 = (bf16[128,4096]{1,0:T(8,128)(2,1)S(1)}, bf16[128,4096]{1,0:T(8,128)(2,1)}, u32[]{:S(2)}) copy-start(bf16[128,4096]{1,0:T(8,128)(2,1)} %param.9) | copy-start | bytes 3145732
  7.2 49.8 %copy-start.11 = (s32[128]{0:T(128)S(1)}, s32[128]{0:T(128)}, u32[]{:S(2)}) copy-start(s32[128]{0:T(128)} %param.13) | copy-start | bytes 1540
  7.2 49.8 %copy-start.8 = (s32[128,30]{0,1:T(8,128)S(1)}, s32[128,30]{0,1:T(8,128)}, u32[]{:S(2)}) copy-start(s32[128,30]{0,1:T(8,128)} %param.12) | copy-start | bytes 46084
  8.1 52.4 %copy-start.10 = (s32[1,4,32]{2,1,0:T(4,128)S(1)}, s32[1,4,32]{2,1,0:T(4,128)}, u32[]{:S(2)}) copy-start(s32[1,4,32]{2,1,0:T(4,128)} %param.11) | copy-start | bytes 1540
  8.8 24.9 %all-to-all-start = ((bf16[8,2,2048]{2,1,0:T(2,128)(2,1)}), bf16[8,2,2048]{2,1,0:T(2,128)(2,1)S(1)}, u32[]{:S(2)}, u32[]{:S(2)}) async-start(bf16[8,2,2048]{2,1,0:T(2,128)(2,1)} %bitcast.1), calls=%async_computation | async-start | bytes 131072 | tf_op jit(solution)/shard_map/cross/all_to_all | solution.py:46
  26.2 65.7 %all-gather.2.cloned.1.call-start = ((), (), s32[]{:S(2)}) async-start(), calls=%async_computation.2 | async-start | bytes 4718592 | tf_op jit(solution)/shard_map/far/all_gather | solution.py:54
  54.7 24.9 %collective-permute-start.1 = (bf16[128,4096]{1,0:T(8,128)(2,1)S(1)}, bf16[128,4096]{1,0:T(8,128)(2,1)S(1)}, u32[]{:S(2)}, u32[]{:S(2)}) collective-permute-start(bf16[128,4096]{1,0:T(8,128)(2,1)S(1)} %copy-done.1), channel_id=1, source_target_pairs={{0,2},{1,3},{2,0},{3,1},{4,6},{5,7},{6,4},{7,5},{8,10},{9,11},{10,... | collective-permute-start | bytes 3145736 | tf_op jit(solution)/shard_map/pools/ppermute | solution.py:57
  58.5 25.0 %collective-permute-start = (bf16[128,4096]{1,0:T(8,128)(2,1)S(1)}, bf16[128,4096]{1,0:T(8,128)(2,1)}, u32[]{:S(2)}, u32[]{:S(2)}) collective-permute-start(bf16[128,4096]{1,0:T(8,128)(2,1)S(1)} %copy-done.1), channel_id=1, source_target_pairs={{0,1},{1,0},{2,3},{3,2},{4,5},{5,4},{6,7},{7,6},{8,9},{9,8},{10,11... | collective-permute-start | bytes 3145736 | tf_op jit(solution)/shard_map/pools/ppermute | solution.py:58
  79.6 3.9 %copy-start.3 = (bf16[128,4096]{1,0:T(8,128)(2,1)}, bf16[128,4096]{1,0:T(8,128)(2,1)S(1)}, u32[]{:S(2)}) copy-start(bf16[128,4096]{1,0:T(8,128)(2,1)S(1)} %collective-permute-done.1) | copy-start | bytes 3145732
  79.6 5.7 %collective-permute-start.2 = (bf16[128,4096]{1,0:T(8,128)(2,1)S(1)}, bf16[128,4096]{1,0:T(8,128)(2,1)}, u32[]{:S(2)}, u32[]{:S(2)}) collective-permute-start(bf16[128,4096]{1,0:T(8,128)(2,1)S(1)} %collective-permute-done.1), channel_id=1, source_target_pairs={{0,1},{1,0},{2,3},{3,2},{4,5},{5,4},{6,7},{7,6},{8,9},{9,8},{10,11... | collective-permute-start | bytes 3145736 | tf_op jit(solution)/shard_map/pools/ppermute | solution.py:59
  83.6 3.4 %copy-start.7 = (f32[128,512]{0,1:T(8,128)S(1)}, f32[128,512]{0,1:T(8,128)}, u32[]{:S(2)}) copy-start(f32[128,512]{0,1:T(8,128)} %copy.50) | copy-start | bytes 786436
  95.1 12.4 %collective-permute-start.3 = (bf16[512,2048]{1,0:T(8,128)(2,1)}, bf16[512,2048]{1,0:T(8,128)(2,1)}, u32[]{:S(2)}, u32[]{:S(2)}) collective-permute-start(bf16[512,2048]{1,0:T(8,128)(2,1)} %bitcast.22), channel_id=1, source_target_pairs={{0,1},{1,0},{2,3},{3,2},{4,5},{5,4},{6,7},{7,6},{8,9},{9,8},{10,11... | collective-permute-start | bytes 6291464 | tf_op jit(solution)/shard_map/swap/ppermute | solution.py:83
  106.7 3.1 %copy-start.5 = (f32[128,512]{0,1:T(8,128)S(1)}, f32[128,512]{0,1:T(8,128)}, u32[]{:S(2)}) copy-start(f32[128,512]{0,1:T(8,128)} %copy.55) | copy-start | bytes 786436
  106.7 3.1 %copy-start.6 = (f32[128,512]{0,1:T(8,128)S(1)}, f32[128,512]{0,1:T(8,128)}, u32[]{:S(2)}) copy-start(f32[128,512]{0,1:T(8,128)} %get-tuple-element.12) | copy-start | bytes 786436
  106.7 3.1 %copy-start.9 = (s32[128]{0:T(128)S(1)}, s32[128]{0:T(128)}, u32[]{:S(2)}) copy-start(s32[128]{0:T(128)} %param.10) | copy-start | bytes 1540
  112.8 1.2 copy-start.2
  114.5 1.8 %copy-start.4 = (bf16[128,4096]{1,0:T(8,128)(2,1)S(1)}, bf16[128,4096]{1,0:T(8,128)(2,1)}, u32[]{:S(2)}) copy-start(bf16[128,4096]{1,0:T(8,128)(2,1)} %copy-done.3) | copy-start | bytes 3145732
Sparse Core Ops, SparseCore 0:
  54.8 37.0 all-gather.1

commit v3 on v2

v3 whole, which is shorter than its diff:
```python
import functools

import jax
import jax.numpy as jnp
import numpy as np
from jax import lax
from jax.experimental import pallas as pl
from jax.experimental.pallas import tpu as pltpu
from jax.sharding import Mesh, PartitionSpec as P

DEVICES = np.arange(1024).reshape(8, 4, 8, 2, 2)


def lines(order):
    return DEVICES.transpose(order)


ALONG_Y = lines((0, 1, 3, 4, 2))
ALONG_Z = lines((1, 2, 3, 4, 0))
CROSS = lines((0, 2, 3, 1, 4)).reshape(-1, 8).tolist()
NEAR = np.concatenate([ALONG_Y[:, :, :, 0].reshape(-1, 8), ALONG_Z[:, :, :, 1].reshape(-1, 8)]).tolist()
RINGS = np.concatenate([ALONG_Z[:, :, :, 0].reshape(-1, 8), ALONG_Y[:, :, :, 1].reshape(-1, 8)]).tolist()
UP = [(g[i], g[(i + 1) % 8]) for g in RINGS for i in range(8)]
DOWN = [(g[i], g[i - 1]) for g in RINGS for i in range(8)]
DOWN_OTHER_CORE = [(a, b ^ 1) for a, b in DOWN]
OTHER_CORE = [(i, i ^ 1) for i in range(1024)]
OTHER_CHIP = [(i, i ^ 2) for i in range(1024)]
BLOCK = 64


def dots(a, b):
    return lax.dot_general(a, b, (((1,), (1,)), ((), ())), preferred_element_type=jnp.float32)


def hard_kernel(place_ref, refs_ref, count_ref, list_ref, q_ref, p0, p1, p2, p3, out_ref):
    rows, most = refs_ref.shape
    span = list_ref.shape[0]
    slots = span // 4
    own = place_ref[3]
    column = lax.broadcasted_iota(jnp.int32, (rows, span), 1)
    refs = refs_ref[...]
    live = lax.broadcasted_iota(jnp.int32, refs.shape, 1) < count_ref[...]
    refs = jnp.where(live, refs, -1)
    present = jnp.zeros((rows, span), jnp.float32)
    for i in range(most):
        present = present + jnp.where(refs[:, i : i + 1] == column, 1.0, 0.0)
    present = present.astype(jnp.bfloat16)
    slot = lax.broadcasted_iota(jnp.int32, (span, span), 0)
    row = lax.broadcasted_iota(jnp.int32, (span, span), 1)
    same = list_ref[...] == row
    for i, pool in enumerate((p0, p1, p2, p3)):
        match = jnp.where(same & (lax.div(slot, slots) == (own ^ i)), 1.0, 0.0).astype(jnp.bfloat16)
        used = jnp.dot(present, match, preferred_element_type=jnp.float32)
        out_ref[:, i * span : (i + 1) * span] = jnp.where(used > 0, dots(q_ref[...], pool[...]), -jnp.inf)


def passage(shape, dim, place, ring_is_z):
    at = lax.broadcasted_iota(jnp.int32, shape, dim)
    block, inner, hi, row = at >> 6, (at >> 3) & 7, (at >> 1) & 3, at & 1
    step = (block + 1) >> 1
    shift = jnp.where((block & 1) == 1, 8 - step, step)
    ring_z, ring_y = (place[0] + shift) & 7, (place[1] + shift) & 7
    z = jnp.where(ring_is_z, ring_z, inner)
    y = jnp.where(ring_is_z, inner, ring_y)
    return ((z * 4 + hi) * 8 + y) * 2 + row


def tail_kernel(place_ref, pos_ref, hard_ref, q_ref, *rest):
    blocks, (p0, p1, p2, p3), (grad_ref, loss_ref, own_ref, swap_ref) = rest[:13], rest[13:17], rest[17:]
    near, l1, r1, l2, r2, l3, r3, last, cnear, c1, c2, c3, clast = blocks
    core = place_ref[2]
    half = own_ref.shape[1]
    total = own_ref.shape[0]
    for i, part in enumerate((near, l1, r1, l2, r2, l3, r3)):
        own_ref[i * BLOCK : (i + 1) * BLOCK, :] = part[0]
    own_ref[7 * BLOCK :, :] = last[...]
    swap_ref[:BLOCK, :] = cnear[...]
    for i, part in enumerate((c1, c2, c3)):
        for j in range(2):
            at = (2 * i + j + 1) * BLOCK
            swap_ref[at : at + BLOCK, :] = part[j]
    swap_ref[7 * BLOCK :, :] = clast[...]

    place = (place_ref[0], place_ref[1])
    q_own = q_ref[:, pl.ds(pl.multiple_of(core * half, 128), half)]
    q_swap = q_ref[:, pl.ds(pl.multiple_of((1 - core) * half, 128), half)]
    own_index = passage((1, total), 1, place, core == 0)
    swap_index = passage((total, 1), 0, place, core == 1)
    order = jnp.where(swap_index == own_index, 1.0, 0.0).astype(jnp.bfloat16)
    swap_logits = dots(q_swap, swap_ref[...])
    high = swap_logits.astype(jnp.bfloat16)
    left = swap_logits - high.astype(jnp.float32)
    middle = left.astype(jnp.bfloat16)
    low = (left - middle.astype(jnp.float32)).astype(jnp.bfloat16)
    moved = jnp.dot(low, order, preferred_element_type=jnp.float32)
    moved = moved + jnp.dot(middle, order, preferred_element_type=jnp.float32)
    moved = moved + jnp.dot(high, order, preferred_element_type=jnp.float32)
    logits = dots(q_own, own_ref[...]) + moved

    hard = hard_ref[...]
    peak = jnp.maximum(jnp.max(logits, axis=1, keepdims=True), jnp.max(hard, axis=1, keepdims=True))
    cycle_exp = jnp.exp(logits - peak)
    hard_exp = jnp.exp(hard - peak)
    denominator = jnp.sum(cycle_exp, axis=1, keepdims=True) + jnp.sum(hard_exp, axis=1, keepdims=True)
    positive = own_index == pos_ref[...]
    chosen = jnp.sum(jnp.where(positive, logits, 0.0), axis=1, keepdims=True)
    loss_ref[...] = jnp.log(denominator) + peak - chosen
    weights = (cycle_exp / denominator - jnp.where(positive, 1.0, 0.0)).astype(jnp.bfloat16)
    hard_weights = (hard_exp / denominator).astype(jnp.bfloat16)
    swap_weights = dots(weights, order).astype(jnp.bfloat16)

    depth = p0.shape[0]
    for mine, w, rows in ((core, weights, own_ref), (1 - core, swap_weights, swap_ref)):
        for chunk in range(0, half, 512):
            at = pl.ds(pl.multiple_of(mine * half + chunk, 128), 512)
            total_grad = jnp.dot(w, rows[:, chunk : chunk + 512], preferred_element_type=jnp.float32)
            for i, pool in enumerate((p0, p1, p2, p3)):
                part = hard_weights[:, i * depth : (i + 1) * depth]
                total_grad += jnp.dot(part, pool[:, at], preferred_element_type=jnp.float32)
            grad_ref[:, at] = total_grad.astype(jnp.bfloat16)


VMEM = functools.partial(pl.BlockSpec, memory_space=pltpu.VMEM)
SMEM = functools.partial(pl.BlockSpec, memory_space=pltpu.SMEM)


def hard_call(place, refs, count, lists, queries, pools):
    rows = queries.shape[0]
    span = lists.size
    return pl.pallas_call(
        hard_kernel,
        out_shape=jax.ShapeDtypeStruct((rows, 4 * span), jnp.float32),
        in_specs=[SMEM()] + [VMEM()] * 8,
        out_specs=VMEM(),
        compiler_params=pltpu.CompilerParams(vmem_limit_bytes=8 * 2**20),
        cost_estimate=pl.CostEstimate(flops=2**29, bytes_accessed=6 * 2**20, transcendentals=0),
        name="hard",
    )(place, refs, count.reshape(rows, 1), lists.reshape(span, 1), queries, *pools)


def tail_call(place, positive, hard, queries, blocks, pools):
    rows, width = queries.shape
    half = width // 2
    return pl.pallas_call(
        tail_kernel,
        out_shape=(
            jax.ShapeDtypeStruct((rows, width), jnp.bfloat16),
            jax.ShapeDtypeStruct((rows, 1), jnp.float32),
        ),
        in_specs=[SMEM()] + [VMEM()] * (3 + len(blocks) + len(pools)),
        out_specs=(VMEM(), VMEM()),
        scratch_shapes=[pltpu.VMEM((8 * BLOCK, half), jnp.bfloat16), pltpu.VMEM((8 * BLOCK, half), jnp.bfloat16)],
        compiler_params=pltpu.CompilerParams(vmem_limit_bytes=16 * 2**20),
        cost_estimate=pl.CostEstimate(flops=2**31, bytes_accessed=12 * 2**20, transcendentals=2**17),
        name="tail",
    )(place, positive.reshape(rows, 1), hard, queries, *blocks, *pools)


def body(queries, passages, pool, positive_ids, request_lists, hard_refs, hard_count):
    half = passages.shape[1] // 2
    device = lax.axis_index("d")
    core = device & 1
    place = jnp.stack([device >> 7, (device >> 2) & 7, core, device & 3]).astype(jnp.int32)

    with jax.named_scope("cross"):
        halves = passages.reshape(2, 2, half).transpose(1, 0, 2)
        sent = jnp.broadcast_to(halves[None], (4, 2, 2, half)).reshape(8, 2, half)
        got = lax.all_to_all(sent, "d", 0, 0, axis_index_groups=CROSS, tiled=True)
        got = got.reshape(4, 2, 2, half).transpose(1, 0, 2, 3).reshape(2, 8, half)
        got = jnp.where(core == 0, got, got[::-1])
    with jax.named_scope("near"):
        sent = jnp.broadcast_to(got.reshape(1, 16, half), (8, 16, half))
        near = lax.all_to_all(sent, "d", 0, 0, axis_index_groups=NEAR, tiled=True)
        near = near.reshape(8, 2, 8, half).transpose(1, 0, 2, 3).reshape(2, BLOCK, half)
    with jax.named_scope("ring"):
        up, down, handed = near, near, [lax.ppermute(near[1], "d", OTHER_CORE)]
        own = [near]
        for _ in range(3):
            up, down = lax.ppermute(up, "d", UP), lax.ppermute(down, "d", DOWN)
            own += [up, down]
            handed.append(lax.ppermute(jnp.stack([up[1], down[1]]), "d", OTHER_CORE))
        own.append(lax.ppermute(up[0], "d", UP))
        handed.append(lax.ppermute(down[1], "d", DOWN_OTHER_CORE))
    with jax.named_scope("pools"):
        near, pool = lax.optimization_barrier((near, pool))
        pool_x = lax.ppermute(pool, "d", OTHER_CHIP)
        pool_c = lax.ppermute(pool, "d", OTHER_CORE)
        pool_xc = lax.ppermute(pool_x, "d", OTHER_CORE)
        pools = (pool, pool_c, pool_x, pool_xc)
    hard = hard_call(place, hard_refs, hard_count, request_lists, queries, pools)
    grad, loss = tail_call(place, positive_ids, hard, queries, own + handed, pools)
    return grad, loss.reshape(-1)


def solution(mesh):
    flat = Mesh(mesh.devices.reshape(1024), ("d",))
    return jax.shard_map(
        body,
        mesh=flat,
        in_specs=(P("d", None), P("d", None), P("d", None), P("d"), P("d", None, None), P("d", None), P("d")),
        out_specs=(P("d", None), P("d")),
        check_vma=False,
    )
```

time: 127 us -> 131 us (1.031)
  starting transfers between devices: 31.7 us -> 70.2 us
  waiting for transfers between devices: 31.3 us -> 12.7 us
  matrix products: 15.8 us -> 0 us
  between operations: 14.4 us -> 1.16 us
  Pallas kernels: 0 us -> 9.27 us
  local copies, waits for them, and re-layouts: 10.7 us -> 13.8 us
    ppermute x1 -> x12, starting transfers between devices: 8.24 us -> 40.9 us  [the longest x6 21.8 us: body(): up, down = (lax.ppermute(up, 'd', UP), lax.ppermute(down, 'd', DOWN))]
    ppermute x1, waiting for transfers between devices: 18.9 us -> 0.01 us  [body(): pool_x = lax.ppermute(pool, 'd', OTHER_CHIP)]
    dot_general x13 -> x0, matrix products: 15.8 us -> none  [the longest x6 7.32 us: dots(): lax.dot_general(a, b, (((1,), (1,)), ((), ())), preferred_element_type=jn...]
    pallas_call x0 -> x2, Pallas kernels: none -> 9.27 us  [the longest x1 6.51 us: tail_call(): pl.pallas_call(tail_kernel, out_shape=(jax.ShapeDtypeStruct((rows, width)...]
    unnamed x24 -> x57, local copies, waits for them, and re-layouts: 0.67 us -> 9.62 us
    ppermute x1, starting transfers between devices: 1.92 us -> 7.47 us  [body(): pool_c = lax.ppermute(pool, 'd', OTHER_CORE)]
    ppermute x1 -> x12, waiting for transfers between devices: 0.76 us -> 5.19 us  [the longest x6 5.18 us: body(): up, down = (lax.ppermute(up, 'd', UP), lax.ppermute(down, 'd', DOWN))]
    all_gather x1 -> x0, waiting for transfers between devices: 4.17 us -> none  [body(): lax.all_gather(near, 'd', axis_index_groups=FAR, axis=0, tiled=True)]
  transfers between devices with their start and end apart: 6 -> 16, of which waited for: 4 -> 4; matrix products, arithmetic and copies ran while one was open for 9% -> 4% of each run, Pallas kernels for 0% -> 2%
where the time goes in v3:
time: 131 us; the launch traced here: 130 us
  starting transfers between devices  70.2 us (54%)
  blocking collectives  19.3 us (15%)
  local copies, waits for them, and re-layouts  13.8 us (11%)
  waiting for transfers between devices  12.7 us (10%)
  Pallas kernels  9.27 us (7%)
  other arithmetic  3.33 us (3%)
    ppermute x6, starting transfers between devices, body(): up, down = (lax.ppermute(up, 'd', UP), lax.ppermute(down, 'd', DOWN))  21.8 us
    all_to_all x1, blocking collectives, body(): near = lax.all_to_all(sent, 'd', 0, 0, axis_index_groups=NEAR, tiled=True)  19.3 us
    all_to_all x1, starting transfers between devices, body(): got = lax.all_to_all(sent, 'd', 0, 0, axis_index_groups=CROSS, tiled=True)  17.4 us
    ppermute x3, starting transfers between devices, body(): handed.append(lax.ppermute(jnp.stack([up[1], down[1]]), 'd', OTHER_CORE))  10.6 us
    unnamed x57, local copies, waits for them, and re-layouts  9.62 us
    ppermute x1, starting transfers between devices, body(): pool_c = lax.ppermute(pool, 'd', OTHER_CORE)  7.47 us
    all_to_all x1, waiting for transfers between devices, body(): got = lax.all_to_all(sent, 'd', 0, 0, axis_index_groups=CROSS, tiled=True)  7.47 us
    pallas_call x1, Pallas kernels, tail_call(): pl.pallas_call(tail_kernel, out_shape=(jax.ShapeDtypeStruct((rows, width)...  6.51 us
  transfers between devices with their start and end apart: 16, of which 4 were waited for; matrix products, arithmetic and copies ran while one was open for 4% of the time, Pallas kernels for 2%

profile of v3, /device:TPU:1, one launch (start us, length us, event | category | flops | bytes accessed | tf_op | source)
XLA Modules:
  0.0 129.7 jit_solution(7781561250598494636)
XLA Ops:
  0.6 0.7 reshape.42
  1.4 0.7 broadcast_in_dim.6
  2.1 17.4 %all-to-all-start = ((bf16[8,2,2048]{2,1,0:T(2,128)(2,1)}), bf16[8,2,2048]{2,1,0:T(2,128)(2,1)S(1)}, u32[]{:S(2)}, u32[]{:S(2)}) async-start(bf16[8,2,2048]{2,1,0:T(2,128)(2,1)} %bitcast.7), calls=%async_computation | async-start | bytes 131072 | tf_op jit(solution)/shard_map/cross/all_to_all | solution.py:168
  19.5 7.5 %all-to-all-done = bf16[8,2,2048]{2,1,0:T(2,128)(2,1)S(1)} async-done(((bf16[8,2,2048]{2,1,0:T(2,128)(2,1)}), bf16[8,2,2048]{2,1,0:T(2,128)(2,1)S(1)}, u32[]{:S(2)}, u32[]{:S(2)}) %all-to-all-start) | async-done | bytes 65568 | tf_op jit(solution)/shard_map/cross/all_to_all | solution.py:168
  26.9 0.1 copy.28
  27.0 0.7 rev.3
  27.7 0.1 broadcast_select_fusion
  27.9 0.0 copy-start.1
  27.9 19.3 %all_to_all.10 = bf16[8,16,2048]{2,1,0:T(8,128)(2,1)S(1)} all-to-all(bf16[8,16,2048]{2,1,0:T(8,128)(2,1)S(1)} %broadcast_in_dim.15), channel_id=1, replica_groups={{0,4,8,12,16,20,24,28},{2,6,10,14,18,22,26,30},{32,36,40,44,48,52,56,60..., dimensions={0} | all-to-all | bytes 1048576 | tf_op jit(solution)/shard_map/near/all_to_all | solution.py:173
  47.2 6.0 %collective-permute-start.4 = (bf16[2,64,2048]{2,1,0:T(8,128)(2,1)S(1)}, bf16[2,64,2048]{2,1,0:T(8,128)(2,1)S(1)}, u32[]{:S(2)}, u32[]{:S(2)}) collective-permute-start(bf16[2,64,2048]{2,1,0:T(8,128)(2,1)S(1)} %copy_bitcast_fusion.rest_0_), channel_id=1, source_target_pairs={{0,896},{128,0},{256,128},{384,256},{512,384},{640,512},{768,640},... | collective-permute-start | bytes 1572872 | tf_op jit(solution)/shard_map/ring/ppermute | solution.py:179
  53.3 1.9 %collective-permute-start.3 = (bf16[2,64,2048]{2,1,0:T(8,128)(2,1)S(1)}, bf16[2,64,2048]{2,1,0:T(8,128)(2,1)S(1)}, u32[]{:S(2)}, u32[]{:S(2)}) collective-permute-start(bf16[2,64,2048]{2,1,0:T(8,128)(2,1)S(1)} %copy_bitcast_fusion.rest_0_), channel_id=1, source_target_pairs={{0,128},{128,256},{256,384},{384,512},{512,640},{640,768},{768,896... | collective-permute-start | bytes 1572872 | tf_op jit(solution)/shard_map/ring/ppermute | solution.py:179
  55.2 4.2 %collective-permute-done.4.rest_2_ = bf16[2,64,2048]{2,1,0:T(8,128)(2,1)S(1)} collective-permute-done((bf16[2,64,2048]{2,1,0:T(8,128)(2,1)S(1)}, bf16[2,64,2048]{2,1,0:T(8,128)(2,1)S(1)}, u32[]{:S(2)}, u32[]{:S(2)}) %collective-permute-start.4) | collective-permute-done | bytes 524320 | tf_op jit(solution)/shard_map/ring/ppermute | solution.py:179
  59.4 5.3 %collective-permute-start.6 = (bf16[2,64,2048]{2,1,0:T(8,128)(2,1)S(1)}, bf16[2,64,2048]{2,1,0:T(8,128)(2,1)S(1)}, u32[]{:S(2)}, u32[]{:S(2)}) collective-permute-start(bf16[2,64,2048]{2,1,0:T(8,128)(2,1)S(1)} %collective-permute-done.4.rest_2_), channel_id=1, source_target_pairs={{0,896},{128,0},{256,128},{384,256},{512,384},{640,512},{768,640},... | collective-permute-start | bytes 1572872 | tf_op jit(solution)/shard_map/ring/ppermute | solution.py:179
  64.7 2.5 %collective-permute-start.1 = (bf16[128,4096]{1,0:T(8,128)(2,1)S(1)}, bf16[128,4096]{1,0:T(8,128)(2,1)S(1)}, u32[]{:S(2)}, u32[]{:S(2)}) collective-permute-start(bf16[128,4096]{1,0:T(8,128)(2,1)S(1)} %copy-done.1), channel_id=1, source_target_pairs={{0,2},{1,3},{2,0},{3,1},{4,6},{5,7},{6,4},{7,5},{8,10},{9,11},{10,... | collective-permute-start | bytes 3145736 | tf_op jit(solution)/shard_map/pools/ppermute | solution.py:186
  67.2 7.5 %collective-permute-start = (bf16[128,4096]{1,0:T(8,128)(2,1)S(1)}, bf16[128,4096]{1,0:T(8,128)(2,1)S(1)}, u32[]{:S(2)}, u32[]{:S(2)}) collective-permute-start(bf16[128,4096]{1,0:T(8,128)(2,1)S(1)} %copy-done.1), channel_id=1, source_target_pairs={{0,1},{1,0},{2,3},{3,2},{4,5},{5,4},{6,7},{7,6},{8,9},{9,8},{10,11... | collective-permute-start | bytes 3145736 | tf_op jit(solution)/shard_map/pools/ppermute | solution.py:187
  74.7 0.0 collective-permute-done.3.rest_1_
  74.7 2.3 %collective-permute-start.5 = (bf16[2,64,2048]{2,1,0:T(8,128)(2,1)S(1)}, bf16[2,64,2048]{2,1,0:T(8,128)(2,1)S(1)}, u32[]{:S(2)}, u32[]{:S(2)}) collective-permute-start(bf16[2,64,2048]{2,1,0:T(8,128)(2,1)S(1)} %collective-permute-done.3.rest_1_), channel_id=1, source_target_pairs={{0,128},{128,256},{256,384},{384,512},{512,640},{640,768},{768,896... | collective-permute-start | bytes 1572872 | tf_op jit(solution)/shard_map/ring/ppermute | solution.py:179
  77.0 0.0 collective-permute-done.6.rest_4_
  77.0 4.2 %collective-permute-start.8 = (bf16[2,64,2048]{2,1,0:T(8,128)(2,1)S(1)}, bf16[2,64,2048]{2,1,0:T(8,128)(2,1)S(1)}, u32[]{:S(2)}, u32[]{:S(2)}) collective-permute-start(bf16[2,64,2048]{2,1,0:T(8,128)(2,1)S(1)} %collective-permute-done.6.rest_4_), channel_id=1, source_target_pairs={{0,896},{128,0},{256,128},{384,256},{512,384},{640,512},{768,640},... | collective-permute-start | bytes 1572872 | tf_op jit(solution)/shard_map/ring/ppermute | solution.py:179
  81.2 2.9 %collective-permute-start.10 = (bf16[64,2048]{1,0:T(8,128)(2,1)S(1)}, bf16[64,2048]{1,0:T(8,128)(2,1)S(1)}, u32[]{:S(2)}, u32[]{:S(2)}) collective-permute-start(bf16[64,2048]{1,0:T(8,128)(2,1)S(1)} %slice_bitcast_fusion), channel_id=1, source_target_pairs={{0,1},{1,0},{2,3},{3,2},{4,5},{5,4},{6,7},{7,6},{8,9},{9,8},{10,11... | collective-permute-start | bytes 786440 | tf_op jit(solution)/shard_map/ring/ppermute | solution.py:176
  84.2 0.8 copy-done.16
  85.0 0.8 pad_maximum_fusion
  85.9 0.2 collective-permute-done.5.rest_3_
  86.1 2.0 %collective-permute-start.7 = (bf16[2,64,2048]{2,1,0:T(8,128)(2,1)S(1)}, bf16[2,64,2048]{2,1,0:T(8,128)(2,1)S(1)}, u32[]{:S(2)}, u32[]{:S(2)}) collective-permute-start(bf16[2,64,2048]{2,1,0:T(8,128)(2,1)S(1)} %collective-permute-done.5.rest_3_), channel_id=1, source_target_pairs={{0,128},{128,256},{256,384},{384,512},{512,640},{640,768},{768,896... | collective-permute-start | bytes 1572872 | tf_op jit(solution)/shard_map/ring/ppermute | solution.py:179
  88.2 0.8 pad_maximum_fusion.1
  89.0 0.0 collective-permute-done.1.p2.rest_15_
  89.0 5.1 %collective-permute-start.11 = (bf16[2,64,2048]{2,1,0:T(8,128)(2,1)}, bf16[2,64,2048]{2,1,0:T(8,128)(2,1)}, u32[]{:S(2)}, u32[]{:S(2)}) collective-permute-start(bf16[2,64,2048]{2,1,0:T(8,128)(2,1)} %pad_maximum_fusion), channel_id=1, source_target_pairs={{0,1},{1,0},{2,3},{3,2},{4,5},{5,4},{6,7},{7,6},{8,9},{9,8},{10,11... | collective-permute-start | bytes 1572872 | tf_op jit(solution)/shard_map/ring/ppermute | solution.py:181
  94.1 0.0 collective-permute-done.8.rest_6_
  94.1 1.9 %collective-permute-start.2 = (bf16[128,4096]{1,0:T(8,128)(2,1)S(1)}, bf16[128,4096]{1,0:T(8,128)(2,1)S(1)}, u32[]{:S(2)}, u32[]{:S(2)}) collective-permute-start(bf16[128,4096]{1,0:T(8,128)(2,1)S(1)} %collective-permute-done.1.p2.rest_15_), channel_id=1, source_target_pairs={{0,1},{1,0},{2,3},{3,2},{4,5},{5,4},{6,7},{7,6},{8,9},{9,8},{10,11... | collective-permute-start | bytes 3145736 | tf_op jit(solution)/shard_map/pools/ppermute | solution.py:188
  96.0 0.8 slice_bitcast_fusion.2
  96.8 0.8 collective-permute-done.7.rest_5_
  97.6 3.6 %collective-permute-start.12 = (bf16[2,64,2048]{2,1,0:T(8,128)(2,1)}, bf16[2,64,2048]{2,1,0:T(8,128)(2,1)}, u32[]{:S(2)}, u32[]{:S(2)}) collective-permute-start(bf16[2,64,2048]{2,1,0:T(8,128)(2,1)} %pad_maximum_fusion.1), channel_id=1, source_target_pairs={{0,1},{1,0},{2,3},{3,2},{4,5},{5,4},{6,7},{7,6},{8,9},{9,8},{10,11... | collective-permute-start | bytes 1572872 | tf_op jit(solution)/shard_map/ring/ppermute | solution.py:181
  101.2 0.7 fusion
  101.9 0.9 pad_maximum_fusion.2
  102.8 0.0 collective-permute-done.10.rest_8_
  102.8 0.7 copy-done.22
  103.6 1.9 %collective-permute-start.13 = (bf16[2,64,2048]{2,1,0:T(8,128)(2,1)}, bf16[2,64,2048]{2,1,0:T(8,128)(2,1)}, u32[]{:S(2)}, u32[]{:S(2)}) collective-permute-start(bf16[2,64,2048]{2,1,0:T(8,128)(2,1)} %pad_maximum_fusion.2), channel_id=1, source_target_pairs={{0,1},{1,0},{2,3},{3,2},{4,5},{5,4},{6,7},{7,6},{8,9},{9,8},{10,11... | collective-permute-start | bytes 1572872 | tf_op jit(solution)/shard_map/ring/ppermute | solution.py:181
  105.5 0.0 collective-permute-done.p1.rest_14_
  105.5 0.0 copy-start.2
  105.5 1.0 copy-done.2
  106.5 1.9 %collective-permute-start.14 = (bf16[64,2048]{1,0:T(8,128)(2,1)}, bf16[64,2048]{1,0:T(8,128)(2,1)}, u32[]{:S(2)}, u32[]{:S(2)}) collective-permute-start(bf16[64,2048]{1,0:T(8,128)(2,1)} %get-tuple-element.8), channel_id=1, source_target_pairs={{0,897},{128,1},{256,129},{384,257},{512,385},{640,513},{768,641},... | collective-permute-start | bytes 786440 | tf_op jit(solution)/shard_map/ring/ppermute | solution.py:183
  108.4 0.0 collective-permute-done.2.p3.rest_16_
  108.4 1.0 copy-done.5
  109.4 3.7 %collective-permute-start.9 = (bf16[64,2048]{1,0:T(8,128)(2,1)}, bf16[64,2048]{1,0:T(8,128)(2,1)}, u32[]{:S(2)}, u32[]{:S(2)}) collective-permute-start(bf16[64,2048]{1,0:T(8,128)(2,1)} %get-tuple-element.11), channel_id=1, source_target_pairs={{0,128},{128,256},{256,384},{384,512},{512,640},{640,768},{768,896... | collective-permute-start | bytes 786440 | tf_op jit(solution)/shard_map/ring/ppermute | solution.py:182
  113.1 0.0 copy-start.26
  113.1 0.6 copy-done.26
  113.8 0.1 copy.34.pos_ref
  113.9 0.6 copy-done.25
  114.5 0.1 reshape.49.list_ref
  114.6 0.6 copy-done.24
  115.2 0.1 copy.31.refs_ref
  115.3 0.7 copy-done.27
  115.9 0.1 copy.32.count_ref
  116.1 0.1 pad_add_fusion.place_ref
  116.1 1.2 copy-done.3
  117.4 1.2 copy-done.6
  118.7 2.8 %hard.1.hard_ref = f32[128,512]{1,0:T(8,128)S(1)} custom-call(s32[4]{0:T(128)S(1)} %pad_add_fusion.place_ref, s32[128,30]{1,0:T(8,128)S(1)} %copy.31.refs_ref, s32[128,1]{1,0:T(8,128)S(1)} %copy.32.count_ref, s32[128,1]{1,0:T(8,128)S(1)} %reshape.49.list_ref, bf16[128,4096]{1,0:T(8,128)(2,1)S(1)} %copy-done, bf16[128,4096]{1,0:T(8,128)(2,1)S(1)} %copy-done.1, ...), custom_call_target="tpu_custom_call" | custom-call | flops 536870912 | bytes 6291456 | tf_op jit(solution)/shard_map/hard/pallas_call | solution.py:130
  121.4 0.0 collective-permute-done.11.rest_9_
  121.4 0.0 collective-permute-done.12.rest_10_
  121.5 0.0 collective-permute-done.9.rest_7_
  121.5 0.0 collective-permute-done.13.rest_11_
  121.6 1.0 copy-done.21
  122.6 6.5 %tail.1 = (bf16[128,4096]{1,0:T(8,128)(2,1)}, f32[128,1]{1,0:T(8,128)S(1)}) custom-call(s32[4]{0:T(128)S(1)} %pad_add_fusion.place_ref, s32[128,1]{1,0:T(8,128)S(1)} %copy.34.pos_ref, f32[128,512]{1,0:T(8,128)S(1)} %hard.1.hard_ref, bf16[128,4096]{1,0:T(8,128)(2,1)S(1)} %copy-done, bf16[2,64,2048]{2,1,0:T(8,128)(2,1)S(1)} %copy-done.9, ...), custom_call_target="tpu_custom_call" | custom-call | flops 2147483648 | bytes 12582912 | tf_op jit(solution)/shard_map/tail/pallas_call | solution.py:144
  129.1 0.6 reduce
  (52 shorter events, 0.3 us)
Async XLA Ops:
  2.1 24.9 %all-to-all-start = ((bf16[8,2,2048]{2,1,0:T(2,128)(2,1)}), bf16[8,2,2048]{2,1,0:T(2,128)(2,1)S(1)}, u32[]{:S(2)}, u32[]{:S(2)}) async-start(bf16[8,2,2048]{2,1,0:T(2,128)(2,1)} %bitcast.7), calls=%async_computation | async-start | bytes 131072 | tf_op jit(solution)/shard_map/cross/all_to_all | solution.py:168
  27.9 36.8 %copy-start.1 = (bf16[128,4096]{1,0:T(8,128)(2,1)S(1)}, bf16[128,4096]{1,0:T(8,128)(2,1)}, u32[]{:S(2)}) copy-start(bf16[128,4096]{1,0:T(8,128)(2,1)} %rest_13_) | copy-start | bytes 3145732
  47.2 36.9 %copy-start.8 = (bf16[2,64,2048]{2,1,0:T(8,128)(2,1)}, bf16[2,64,2048]{2,1,0:T(8,128)(2,1)S(1)}, u32[]{:S(2)}) copy-start(bf16[2,64,2048]{2,1,0:T(8,128)(2,1)S(1)} %copy_bitcast_fusion.rest_0_) | copy-start | bytes 1572868
  47.2 12.1 %collective-permute-start.4 = (bf16[2,64,2048]{2,1,0:T(8,128)(2,1)S(1)}, bf16[2,64,2048]{2,1,0:T(8,128)(2,1)S(1)}, u32[]{:S(2)}, u32[]{:S(2)}) collective-permute-start(bf16[2,64,2048]{2,1,0:T(8,128)(2,1)S(1)} %copy_bitcast_fusion.rest_0_), channel_id=1, source_target_pairs={{0,896},{128,0},{256,128},{384,256},{512,384},{640,512},{768,640},... | collective-permute-start | bytes 1572872 | tf_op jit(solution)/shard_map/ring/ppermute | solution.py:179
  53.3 21.4 %collective-permute-start.3 = (bf16[2,64,2048]{2,1,0:T(8,128)(2,1)S(1)}, bf16[2,64,2048]{2,1,0:T(8,128)(2,1)S(1)}, u32[]{:S(2)}, u32[]{:S(2)}) collective-permute-start(bf16[2,64,2048]{2,1,0:T(8,128)(2,1)S(1)} %copy_bitcast_fusion.rest_0_), channel_id=1, source_target_pairs={{0,128},{128,256},{256,384},{384,512},{512,640},{640,768},{768,896... | collective-permute-start | bytes 1572872 | tf_op jit(solution)/shard_map/ring/ppermute | solution.py:179
  59.4 24.8 %copy-start.14 = (bf16[2,64,2048]{2,1,0:T(8,128)(2,1)}, bf16[2,64,2048]{2,1,0:T(8,128)(2,1)S(1)}, u32[]{:S(2)}) copy-start(bf16[2,64,2048]{2,1,0:T(8,128)(2,1)S(1)} %collective-permute-done.4.rest_2_) | copy-start | bytes 1572868
  59.4 17.6 %collective-permute-start.6 = (bf16[2,64,2048]{2,1,0:T(8,128)(2,1)S(1)}, bf16[2,64,2048]{2,1,0:T(8,128)(2,1)S(1)}, u32[]{:S(2)}, u32[]{:S(2)}) collective-permute-start(bf16[2,64,2048]{2,1,0:T(8,128)(2,1)S(1)} %collective-permute-done.4.rest_2_), channel_id=1, source_target_pairs={{0,896},{128,0},{256,128},{384,256},{512,384},{640,512},{768,640},... | collective-permute-start | bytes 1572872 | tf_op jit(solution)/shard_map/ring/ppermute | solution.py:179
  64.7 24.3 %collective-permute-start.1 = (bf16[128,4096]{1,0:T(8,128)(2,1)S(1)}, bf16[128,4096]{1,0:T(8,128)(2,1)S(1)}, u32[]{:S(2)}, u32[]{:S(2)}) collective-permute-start(bf16[128,4096]{1,0:T(8,128)(2,1)S(1)} %copy-done.1), channel_id=1, source_target_pairs={{0,2},{1,3},{2,0},{3,1},{4,6},{5,7},{6,4},{7,5},{8,10},{9,11},{10,... | collective-permute-start | bytes 3145736 | tf_op jit(solution)/shard_map/pools/ppermute | solution.py:186
  67.2 38.3 %collective-permute-start = (bf16[128,4096]{1,0:T(8,128)(2,1)S(1)}, bf16[128,4096]{1,0:T(8,128)(2,1)S(1)}, u32[]{:S(2)}, u32[]{:S(2)}) collective-permute-start(bf16[128,4096]{1,0:T(8,128)(2,1)S(1)} %copy-done.1), channel_id=1, source_target_pairs={{0,1},{1,0},{2,3},{3,2},{4,5},{5,4},{6,7},{7,6},{8,9},{9,8},{10,11... | collective-permute-start | bytes 3145736 | tf_op jit(solution)/shard_map/pools/ppermute | solution.py:187
  74.7 11.4 %collective-permute-start.5 = (bf16[2,64,2048]{2,1,0:T(8,128)(2,1)S(1)}, bf16[2,64,2048]{2,1,0:T(8,128)(2,1)S(1)}, u32[]{:S(2)}, u32[]{:S(2)}) collective-permute-start(bf16[2,64,2048]{2,1,0:T(8,128)(2,1)S(1)} %collective-permute-done.3.rest_1_), channel_id=1, source_target_pairs={{0,128},{128,256},{256,384},{384,512},{512,640},{640,768},{768,896... | collective-permute-start | bytes 1572872 | tf_op jit(solution)/shard_map/ring/ppermute | solution.py:179
  77.0 8.9 %copy-start.18 = (bf16[2,64,2048]{2,1,0:T(8,128)(2,1)}, bf16[2,64,2048]{2,1,0:T(8,128)(2,1)S(1)}, u32[]{:S(2)}) copy-start(bf16[2,64,2048]{2,1,0:T(8,128)(2,1)S(1)} %collective-permute-done.6.rest_4_) | copy-start | bytes 1572868
  77.0 17.1 %collective-permute-start.8 = (bf16[2,64,2048]{2,1,0:T(8,128)(2,1)S(1)}, bf16[2,64,2048]{2,1,0:T(8,128)(2,1)S(1)}, u32[]{:S(2)}, u32[]{:S(2)}) collective-permute-start(bf16[2,64,2048]{2,1,0:T(8,128)(2,1)S(1)} %collective-permute-done.6.rest_4_), channel_id=1, source_target_pairs={{0,896},{128,0},{256,128},{384,256},{512,384},{640,512},{768,640},... | collective-permute-start | bytes 1572872 | tf_op jit(solution)/shard_map/ring/ppermute | solution.py:179
  81.2 21.6 %collective-permute-start.10 = (bf16[64,2048]{1,0:T(8,128)(2,1)S(1)}, bf16[64,2048]{1,0:T(8,128)(2,1)S(1)}, u32[]{:S(2)}, u32[]{:S(2)}) collective-permute-start(bf16[64,2048]{1,0:T(8,128)(2,1)S(1)} %slice_bitcast_fusion), channel_id=1, source_target_pairs={{0,1},{1,0},{2,3},{3,2},{4,5},{5,4},{6,7},{7,6},{8,9},{9,8},{10,11... | collective-permute-start | bytes 786440 | tf_op jit(solution)/shard_map/ring/ppermute | solution.py:176
  84.2 0.8 copy-start.16
  86.1 2.9 %copy-start.20 = (bf16[2,64,2048]{2,1,0:T(8,128)(2,1)}, bf16[2,64,2048]{2,1,0:T(8,128)(2,1)S(1)}, u32[]{:S(2)}) copy-start(bf16[2,64,2048]{2,1,0:T(8,128)(2,1)S(1)} %collective-permute-done.5.rest_3_) | copy-start | bytes 1572868
  86.1 11.4 %collective-permute-start.7 = (bf16[2,64,2048]{2,1,0:T(8,128)(2,1)S(1)}, bf16[2,64,2048]{2,1,0:T(8,128)(2,1)S(1)}, u32[]{:S(2)}, u32[]{:S(2)}) collective-permute-start(bf16[2,64,2048]{2,1,0:T(8,128)(2,1)S(1)} %collective-permute-done.5.rest_3_), channel_id=1, source_target_pairs={{0,128},{128,256},{256,384},{384,512},{512,640},{640,768},{768,896... | collective-permute-start | bytes 1572872 | tf_op jit(solution)/shard_map/ring/ppermute | solution.py:179
  89.0 32.4 %collective-permute-start.11 = (bf16[2,64,2048]{2,1,0:T(8,128)(2,1)}, bf16[2,64,2048]{2,1,0:T(8,128)(2,1)}, u32[]{:S(2)}, u32[]{:S(2)}) collective-permute-start(bf16[2,64,2048]{2,1,0:T(8,128)(2,1)} %pad_maximum_fusion), channel_id=1, source_target_pairs={{0,1},{1,0},{2,3},{3,2},{4,5},{5,4},{6,7},{7,6},{8,9},{9,8},{10,11... | collective-permute-start | bytes 1572872 | tf_op jit(solution)/shard_map/ring/ppermute | solution.py:181
  94.1 7.8 %copy-start.12 = (bf16[2,64,2048]{2,1,0:T(8,128)(2,1)}, bf16[2,64,2048]{2,1,0:T(8,128)(2,1)S(1)}, u32[]{:S(2)}) copy-start(bf16[2,64,2048]{2,1,0:T(8,128)(2,1)S(1)} %collective-permute-done.8.rest_6_) | copy-start | bytes 1572868
  94.1 14.3 %collective-permute-start.2 = (bf16[128,4096]{1,0:T(8,128)(2,1)S(1)}, bf16[128,4096]{1,0:T(8,128)(2,1)S(1)}, u32[]{:S(2)}, u32[]{:S(2)}) collective-permute-start(bf16[128,4096]{1,0:T(8,128)(2,1)S(1)} %collective-permute-done.1.p2.rest_15_), channel_id=1, source_target_pairs={{0,1},{1,0},{2,3},{3,2},{4,5},{5,4},{6,7},{7,6},{8,9},{9,8},{10,11... | collective-permute-start | bytes 3145736 | tf_op jit(solution)/shard_map/pools/ppermute | solution.py:188
  96.8 19.3 %copy-start = (bf16[128,4096]{1,0:T(8,128)(2,1)S(1)}, bf16[128,4096]{1,0:T(8,128)(2,1)}, u32[]{:S(2)}) copy-start(bf16[128,4096]{1,0:T(8,128)(2,1)} %q_ref.3) | copy-start | bytes 3145732
  97.6 4.4 %copy-start.10 = (bf16[2,64,2048]{2,1,0:T(8,128)(2,1)}, bf16[2,64,2048]{2,1,0:T(8,128)(2,1)S(1)}, u32[]{:S(2)}) copy-start(bf16[2,64,2048]{2,1,0:T(8,128)(2,1)S(1)} %collective-permute-done.7.rest_5_) | copy-start | bytes 1572868
  97.6 23.9 %collective-permute-start.12 = (bf16[2,64,2048]{2,1,0:T(8,128)(2,1)}, bf16[2,64,2048]{2,1,0:T(8,128)(2,1)}, u32[]{:S(2)}, u32[]{:S(2)}) collective-permute-start(bf16[2,64,2048]{2,1,0:T(8,128)(2,1)} %pad_maximum_fusion.1), channel_id=1, source_target_pairs={{0,1},{1,0},{2,3},{3,2},{4,5},{5,4},{6,7},{7,6},{8,9},{9,8},{10,11... | collective-permute-start | bytes 1572872 | tf_op jit(solution)/shard_map/ring/ppermute | solution.py:181
  102.8 0.7 copy-start.22
  103.6 17.9 %collective-permute-start.13 = (bf16[2,64,2048]{2,1,0:T(8,128)(2,1)}, bf16[2,64,2048]{2,1,0:T(8,128)(2,1)}, u32[]{:S(2)}, u32[]{:S(2)}) collective-permute-start(bf16[2,64,2048]{2,1,0:T(8,128)(2,1)} %pad_maximum_fusion.2), channel_id=1, source_target_pairs={{0,1},{1,0},{2,3},{3,2},{4,5},{5,4},{6,7},{7,6},{8,9},{9,8},{10,11... | collective-permute-start | bytes 1572872 | tf_op jit(solution)/shard_map/ring/ppermute | solution.py:181
  105.5 1.0 copy-start.2
  106.5 15.0 %collective-permute-start.14 = (bf16[64,2048]{1,0:T(8,128)(2,1)}, bf16[64,2048]{1,0:T(8,128)(2,1)}, u32[]{:S(2)}, u32[]{:S(2)}) collective-permute-start(bf16[64,2048]{1,0:T(8,128)(2,1)} %get-tuple-element.8), channel_id=1, source_target_pairs={{0,897},{128,1},{256,129},{384,257},{512,385},{640,513},{768,641},... | collective-permute-start | bytes 786440 | tf_op jit(solution)/shard_map/ring/ppermute | solution.py:183
  108.4 1.0 copy-start.5
  109.4 12.1 %collective-permute-start.9 = (bf16[64,2048]{1,0:T(8,128)(2,1)}, bf16[64,2048]{1,0:T(8,128)(2,1)}, u32[]{:S(2)}, u32[]{:S(2)}) collective-permute-start(bf16[64,2048]{1,0:T(8,128)(2,1)} %get-tuple-element.11), channel_id=1, source_target_pairs={{0,128},{128,256},{256,384},{384,512},{512,640},{640,768},{768,896... | collective-permute-start | bytes 786440 | tf_op jit(solution)/shard_map/ring/ppermute | solution.py:182
  113.1 0.7 copy-start.26
  113.8 0.7 copy-start.25
  114.5 0.7 copy-start.24
  115.3 0.7 copy-start.27
  116.1 1.2 copy-start.3
  117.4 1.2 copy-start.6
  118.6 2.9 %copy-start.4 = (bf16[128,4096]{1,0:T(8,128)(2,1)S(1)}, bf16[128,4096]{1,0:T(8,128)(2,1)}, u32[]{:S(2)}) copy-start(bf16[128,4096]{1,0:T(8,128)(2,1)} %copy-done.2) | copy-start | bytes 3145732
  118.6 2.9 %copy-start.7 = (bf16[128,4096]{1,0:T(8,128)(2,1)S(1)}, bf16[128,4096]{1,0:T(8,128)(2,1)}, u32[]{:S(2)}) copy-start(bf16[128,4096]{1,0:T(8,128)(2,1)} %copy-done.5) | copy-start | bytes 3145732
  118.6 2.9 %copy-start.9 = (bf16[2,64,2048]{2,1,0:T(8,128)(2,1)S(1)}, bf16[2,64,2048]{2,1,0:T(8,128)(2,1)}, u32[]{:S(2)}) copy-start(bf16[2,64,2048]{2,1,0:T(8,128)(2,1)} %copy-done.8) | copy-start | bytes 1572868
  118.6 2.9 %copy-start.11 = (bf16[2,64,2048]{2,1,0:T(8,128)(2,1)S(1)}, bf16[2,64,2048]{2,1,0:T(8,128)(2,1)}, u32[]{:S(2)}) copy-start(bf16[2,64,2048]{2,1,0:T(8,128)(2,1)} %copy-done.10) | copy-start | bytes 1572868
  118.6 2.9 %copy-start.13 = (bf16[2,64,2048]{2,1,0:T(8,128)(2,1)S(1)}, bf16[2,64,2048]{2,1,0:T(8,128)(2,1)}, u32[]{:S(2)}) copy-start(bf16[2,64,2048]{2,1,0:T(8,128)(2,1)} %copy-done.12) | copy-start | bytes 1572868
  118.6 2.9 %copy-start.15 = (bf16[2,64,2048]{2,1,0:T(8,128)(2,1)S(1)}, bf16[2,64,2048]{2,1,0:T(8,128)(2,1)}, u32[]{:S(2)}) copy-start(bf16[2,64,2048]{2,1,0:T(8,128)(2,1)} %copy-done.14) | copy-start | bytes 1572868
  118.6 2.9 %copy-start.17 = (bf16[2,64,2048]{2,1,0:T(8,128)(2,1)S(1)}, bf16[2,64,2048]{2,1,0:T(8,128)(2,1)}, u32[]{:S(2)}) copy-start(bf16[2,64,2048]{2,1,0:T(8,128)(2,1)} %copy-done.16) | copy-start | bytes 1572868
  118.6 2.9 %copy-start.19 = (bf16[2,64,2048]{2,1,0:T(8,128)(2,1)S(1)}, bf16[2,64,2048]{2,1,0:T(8,128)(2,1)}, u32[]{:S(2)}) copy-start(bf16[2,64,2048]{2,1,0:T(8,128)(2,1)} %copy-done.18) | copy-start | bytes 1572868
  118.6 2.9 %copy-start.23 = (bf16[64,2048]{1,0:T(8,128)(2,1)S(1)}, bf16[64,2048]{1,0:T(8,128)(2,1)}, u32[]{:S(2)}) copy-start(bf16[64,2048]{1,0:T(8,128)(2,1)} %copy-done.22) | copy-start | bytes 786436
  121.6 1.0 copy-start.21

commit v4 on v3

--- a/solution.py
+++ b/solution.py
@@ -33,24 +33,24 @@
 
 
 def hard_kernel(place_ref, refs_ref, count_ref, list_ref, q_ref, p0, p1, p2, p3, out_ref):
-    rows, most = refs_ref.shape
-    span = list_ref.shape[0]
-    slots = span // 4
+    most, rows = refs_ref.shape
+    owners, slots = list_ref.shape
+    span = owners * slots
     own = place_ref[3]
-    column = lax.broadcasted_iota(jnp.int32, (rows, span), 1)
-    refs = refs_ref[...]
-    live = lax.broadcasted_iota(jnp.int32, refs.shape, 1) < count_ref[...]
-    refs = jnp.where(live, refs, -1)
-    present = jnp.zeros((rows, span), jnp.float32)
+    at = lax.broadcasted_iota(jnp.int32, (span, rows), 0)
+    live = lax.broadcasted_iota(jnp.int32, (most, rows), 0) < count_ref[...]
+    refs = jnp.where(live, refs_ref[...], -1)
+    present = jnp.zeros((span, rows), jnp.float32)
     for i in range(most):
-        present = present + jnp.where(refs[:, i : i + 1] == column, 1.0, 0.0)
+        present = present + jnp.where(refs[i : i + 1, :] == at, 1.0, 0.0)
     present = present.astype(jnp.bfloat16)
-    slot = lax.broadcasted_iota(jnp.int32, (span, span), 0)
-    row = lax.broadcasted_iota(jnp.int32, (span, span), 1)
-    same = list_ref[...] == row
+    row = lax.broadcasted_iota(jnp.int32, (span, span), 0)
+    owner = lax.broadcasted_iota(jnp.int32, (span, span), 1) // slots
+    lists = jnp.concatenate([list_ref[i : i + 1, :] for i in range(owners)], axis=1)
+    same = lists == row
     for i, pool in enumerate((p0, p1, p2, p3)):
-        match = jnp.where(same & (lax.div(slot, slots) == (own ^ i)), 1.0, 0.0).astype(jnp.bfloat16)
-        used = jnp.dot(present, match, preferred_element_type=jnp.float32)
+        match = jnp.where(same & (owner == (own ^ i)), 1.0, 0.0).astype(jnp.bfloat16)
+        used = lax.dot_general(present, match, (((0,), (1,)), ((), ())), preferred_element_type=jnp.float32)
         out_ref[:, i * span : (i + 1) * span] = jnp.where(used > 0, dots(q_ref[...], pool[...]), -jnp.inf)
 
 
@@ -65,21 +65,24 @@
     return ((z * 4 + hi) * 8 + y) * 2 + row
 
 
+def hand_kernel(*refs):
+    (keep_ref, give_ref), blocks = refs[-2:], refs[:-2]
+    for i, block in enumerate(blocks):
+        keep_ref[i] = block[0]
+        give_ref[i] = block[1]
+
+
 def tail_kernel(place_ref, pos_ref, hard_ref, q_ref, *rest):
-    blocks, (p0, p1, p2, p3), (grad_ref, loss_ref, own_ref, swap_ref) = rest[:13], rest[13:17], rest[17:]
-    near, l1, r1, l2, r2, l3, r3, last, cnear, c1, c2, c3, clast = blocks
+    blocks, (p0, p1, p2, p3), (grad_ref, loss_ref, own_ref, swap_ref) = rest[:8], rest[8:12], rest[12:]
     core = place_ref[2]
     half = own_ref.shape[1]
     total = own_ref.shape[0]
-    for i, part in enumerate((near, l1, r1, l2, r2, l3, r3)):
-        own_ref[i * BLOCK : (i + 1) * BLOCK, :] = part[0]
-    own_ref[7 * BLOCK :, :] = last[...]
-    swap_ref[:BLOCK, :] = cnear[...]
-    for i, part in enumerate((c1, c2, c3)):
-        for j in range(2):
-            at = (2 * i + j + 1) * BLOCK
-            swap_ref[at : at + BLOCK, :] = part[j]
-    swap_ref[7 * BLOCK :, :] = clast[...]
+    for parts, rows_ref in ((blocks[:4], own_ref), (blocks[4:], swap_ref)):
+        at = 0
+        for part in parts:
+            for i in range(part.shape[0]):
+                rows_ref[at : at + BLOCK, :] = part[i]
+                at += BLOCK
 
     place = (place_ref[0], place_ref[1])
     q_own = q_ref[:, pl.ds(pl.multiple_of(core * half, 128), half)]
@@ -102,22 +105,24 @@
     cycle_exp = jnp.exp(logits - peak)
     hard_exp = jnp.exp(hard - peak)
     denominator = jnp.sum(cycle_exp, axis=1, keepdims=True) + jnp.sum(hard_exp, axis=1, keepdims=True)
-    positive = own_index == pos_ref[...]
+    rows = q_ref.shape[0]
+    eye = lax.broadcasted_iota(jnp.int32, (rows, rows), 0) == lax.broadcasted_iota(jnp.int32, (rows, rows), 1)
+    positives = jnp.sum(jnp.where(eye, pos_ref[...].astype(jnp.float32), 0.0), axis=1, keepdims=True)
+    positive = own_index == positives.astype(jnp.int32)
     chosen = jnp.sum(jnp.where(positive, logits, 0.0), axis=1, keepdims=True)
-    loss_ref[...] = jnp.log(denominator) + peak - chosen
+    loss = jnp.log(denominator) + peak - chosen
+    loss_ref[...] = jnp.sum(jnp.where(eye, loss, 0.0), axis=0, keepdims=True)
     weights = (cycle_exp / denominator - jnp.where(positive, 1.0, 0.0)).astype(jnp.bfloat16)
     hard_weights = (hard_exp / denominator).astype(jnp.bfloat16)
     swap_weights = dots(weights, order).astype(jnp.bfloat16)
 
-    depth = p0.shape[0]
-    for mine, w, rows in ((core, weights, own_ref), (1 - core, swap_weights, swap_ref)):
+    for mine, w, rows_ref in ((core, weights, own_ref), (1 - core, swap_weights, swap_ref)):
+        all_weights = jnp.concatenate([w, hard_weights], axis=1)
         for chunk in range(0, half, 512):
             at = pl.ds(pl.multiple_of(mine * half + chunk, 128), 512)
-            total_grad = jnp.dot(w, rows[:, chunk : chunk + 512], preferred_element_type=jnp.float32)
-            for i, pool in enumerate((p0, p1, p2, p3)):
-                part = hard_weights[:, i * depth : (i + 1) * depth]
-                total_grad += jnp.dot(part, pool[:, at], preferred_element_type=jnp.float32)
-            grad_ref[:, at] = total_grad.astype(jnp.bfloat16)
+            all_rows = [rows_ref[:, chunk : chunk + 512]] + [pool[:, at] for pool in (p0, p1, p2, p3)]
+            grad = jnp.dot(all_weights, jnp.concatenate(all_rows, axis=0), preferred_element_type=jnp.float32)
+            grad_ref[:, at] = grad.astype(jnp.bfloat16)
 
 
 VMEM = functools.partial(pl.BlockSpec, memory_space=pltpu.VMEM)
@@ -127,15 +132,29 @@
 def hard_call(place, refs, count, lists, queries, pools):
     rows = queries.shape[0]
     span = lists.size
+    refs, count = refs.T, count.reshape(1, rows)
     return pl.pallas_call(
         hard_kernel,
         out_shape=jax.ShapeDtypeStruct((rows, 4 * span), jnp.float32),
         in_specs=[SMEM()] + [VMEM()] * 8,
         out_specs=VMEM(),
         compiler_params=pltpu.CompilerParams(vmem_limit_bytes=8 * 2**20),
-        cost_estimate=pl.CostEstimate(flops=2**29, bytes_accessed=6 * 2**20, transcendentals=0),
+        cost_estimate=pl.CostEstimate(flops=2**33, bytes_accessed=6 * 2**20, transcendentals=0),
         name="hard",
-    )(place, refs, count.reshape(rows, 1), lists.reshape(span, 1), queries, *pools)
+    )(place, refs, count, lists[0], queries, *pools)
+
+
+def hand_call(*blocks):
+    out = jax.ShapeDtypeStruct((len(blocks),) + blocks[0].shape[1:], blocks[0].dtype)
+    return pl.pallas_call(
+        hand_kernel,
+        out_shape=(out, out),
+        in_specs=[VMEM()] * len(blocks),
+        out_specs=(VMEM(), VMEM()),
+        compiler_params=pltpu.CompilerParams(vmem_limit_bytes=8 * 2**20),
+        cost_estimate=pl.CostEstimate(flops=2**33, bytes_accessed=4 * 2**20, transcendentals=0),
+        name="hand",
+    )(*blocks)
 
 
 def tail_call(place, positive, hard, queries, blocks, pools):
@@ -145,7 +164,7 @@
         tail_kernel,
         out_shape=(
             jax.ShapeDtypeStruct((rows, width), jnp.bfloat16),
-            jax.ShapeDtypeStruct((rows, 1), jnp.float32),
+            jax.ShapeDtypeStruct((1, rows), jnp.float32),
         ),
         in_specs=[SMEM()] + [VMEM()] * (3 + len(blocks) + len(pools)),
         out_specs=(VMEM(), VMEM()),
@@ -153,7 +172,7 @@
         compiler_params=pltpu.CompilerParams(vmem_limit_bytes=16 * 2**20),
         cost_estimate=pl.CostEstimate(flops=2**31, bytes_accessed=12 * 2**20, transcendentals=2**17),
         name="tail",
-    )(place, positive.reshape(rows, 1), hard, queries, *blocks, *pools)
+    )(place, positive.reshape(1, rows), hard, queries, *blocks, *pools)
 
 
 def body(queries, passages, pool, positive_ids, request_lists, hard_refs, hard_count):
@@ -173,14 +192,17 @@
         near = lax.all_to_all(sent, "d", 0, 0, axis_index_groups=NEAR, tiled=True)
         near = near.reshape(8, 2, 8, half).transpose(1, 0, 2, 3).reshape(2, BLOCK, half)
     with jax.named_scope("ring"):
-        up, down, handed = near, near, [lax.ppermute(near[1], "d", OTHER_CORE)]
-        own = [near]
-        for _ in range(3):
+        up, down, held, kept, handed = near, near, [near], [], []
+        for step in range(3):
             up, down = lax.ppermute(up, "d", UP), lax.ppermute(down, "d", DOWN)
-            own += [up, down]
-            handed.append(lax.ppermute(jnp.stack([up[1], down[1]]), "d", OTHER_CORE))
-        own.append(lax.ppermute(up[0], "d", UP))
-        handed.append(lax.ppermute(down[1], "d", DOWN_OTHER_CORE))
+            if step == 2:
+                up, down, *handed = lax.optimization_barrier((up, down, *handed))
+            keep, give = hand_call(*held, up, down)
+            kept.append(keep)
+            handed.append(lax.ppermute(give, "d", OTHER_CORE))
+            held = []
+        kept.append(lax.ppermute(up[:1], "d", UP))
+        handed.append(lax.ppermute(down[1:], "d", DOWN_OTHER_CORE))
     with jax.named_scope("pools"):
         near, pool = lax.optimization_barrier((near, pool))
         pool_x = lax.ppermute(pool, "d", OTHER_CHIP)
@@ -188,7 +210,7 @@
         pool_xc = lax.ppermute(pool_x, "d", OTHER_CORE)
         pools = (pool, pool_c, pool_x, pool_xc)
     hard = hard_call(place, hard_refs, hard_count, request_lists, queries, pools)
-    grad, loss = tail_call(place, positive_ids, hard, queries, own + handed, pools)
+    grad, loss = tail_call(place, positive_ids, hard, queries, kept + handed, pools)
     return grad, loss.reshape(-1)
 
 

time: 131 us -> 121 us (0.924)
  local copies, waits for them, and re-layouts: 13.8 us -> 8.08 us
  starting transfers between devices: 70.2 us -> 66.2 us
  other arithmetic: 3.33 us -> 0.16 us
  Pallas kernels: 9.27 us -> 12.3 us
    unnamed x57 -> x24, local copies, waits for them, and re-layouts: 9.62 us -> 3.86 us
    ppermute x1, starting transfers between devices: 7.47 us -> 1.92 us  [body(): pool_c = lax.ppermute(pool, 'd', OTHER_CORE)]
    ppermute x6 -> x5, starting transfers between devices: 19.1 us -> 22.7 us  [the longest x3 16.5 us: body(): handed.append(lax.ppermute(give, 'd', OTHER_CORE))]
    pallas_call x0 -> x3, Pallas kernels: none -> 3.41 us  [hand_call(): pl.pallas_call(hand_kernel, out_shape=(out, out), in_specs=[VMEM()] * len...]
    another operation x3 -> x0, other arithmetic: 2.55 us -> none  [body(): handed.append(lax.ppermute(jnp.stack([up[1], down[1]]), 'd', OTHER_CORE))]
    ppermute x6, starting transfers between devices: 21.8 us -> 19.3 us  [body(): up, down = (lax.ppermute(up, 'd', UP), lax.ppermute(down, 'd', DOWN))]
  transfers between devices with their start and end apart: 16 -> 15, of which waited for: 4 -> 3; matrix products, arithmetic and copies ran while one was open for 4% -> 2% of each run, Pallas kernels for 2% -> 5%
where the time goes in v4:
time: 121 us; the launch traced here: 120 us
  starting transfers between devices  66.2 us (55%)
  blocking collectives  19.3 us (16%)
  waiting for transfers between devices  13.4 us (11%)
  Pallas kernels  12.3 us (10%)
  local copies, waits for them, and re-layouts  8.08 us (7%)
    ppermute x6, starting transfers between devices, body(): up, down = (lax.ppermute(up, 'd', UP), lax.ppermute(down, 'd', DOWN))  19.3 us
    all_to_all x1, blocking collectives, body(): near = lax.all_to_all(sent, 'd', 0, 0, axis_index_groups=NEAR, tiled=True)  19.3 us
    all_to_all x1, starting transfers between devices, body(): got = lax.all_to_all(sent, 'd', 0, 0, axis_index_groups=CROSS, tiled=True)  17.4 us
    ppermute x3, starting transfers between devices, body(): handed.append(lax.ppermute(give, 'd', OTHER_CORE))  16.5 us
    all_to_all x1, waiting for transfers between devices, body(): got = lax.all_to_all(sent, 'd', 0, 0, axis_index_groups=CROSS, tiled=True)  7.47 us
    pallas_call x1, Pallas kernels, tail_call(): pl.pallas_call(tail_kernel, out_shape=(jax.ShapeDtypeStruct((rows, width)...  5.95 us
    ppermute x6, waiting for transfers between devices, body(): up, down = (lax.ppermute(up, 'd', UP), lax.ppermute(down, 'd', DOWN))  5.88 us
    ppermute x1, starting transfers between devices, body(): kept.append(lax.ppermute(up[:1], 'd', UP))  4.11 us
  transfers between devices with their start and end apart: 15, of which 3 were waited for; matrix products, arithmetic and copies ran while one was open for 2% of the time, Pallas kernels for 5%

profile of v4, /device:TPU:1, one launch (start us, length us, event | category | flops | bytes accessed | tf_op | source)
XLA Modules:
  0.0 120.5 jit_solution(10522489128507132621)
XLA Ops:
  0.6 0.7 reshape.36
  1.4 0.7 broadcast_in_dim.6
  2.1 17.4 %all-to-all-start = ((bf16[8,2,2048]{2,1,0:T(2,128)(2,1)}), bf16[8,2,2048]{2,1,0:T(2,128)(2,1)S(1)}, u32[]{:S(2)}, u32[]{:S(2)}) async-start(bf16[8,2,2048]{2,1,0:T(2,128)(2,1)} %bitcast.9), calls=%async_computation | async-start | bytes 131072 | tf_op jit(solution)/shard_map/cross/all_to_all | solution.py:187
  19.5 7.5 %all-to-all-done = bf16[8,2,2048]{2,1,0:T(2,128)(2,1)S(1)} async-done(((bf16[8,2,2048]{2,1,0:T(2,128)(2,1)}), bf16[8,2,2048]{2,1,0:T(2,128)(2,1)S(1)}, u32[]{:S(2)}, u32[]{:S(2)}) %all-to-all-start) | async-done | bytes 65568 | tf_op jit(solution)/shard_map/cross/all_to_all | solution.py:187
  26.9 0.1 copy.16
  27.0 0.7 rev.3
  27.7 0.1 broadcast_select_fusion
  27.9 0.0 copy-start.1
  27.9 19.3 %all_to_all.10 = bf16[8,16,2048]{2,1,0:T(8,128)(2,1)S(1)} all-to-all(bf16[8,16,2048]{2,1,0:T(8,128)(2,1)S(1)} %broadcast_in_dim.15), channel_id=1, replica_groups={{0,4,8,12,16,20,24,28},{2,6,10,14,18,22,26,30},{32,36,40,44,48,52,56,60..., dimensions={0} | all-to-all | bytes 1048576 | tf_op jit(solution)/shard_map/near/all_to_all | solution.py:192
  47.2 6.0 %collective-permute-start.4 = (bf16[2,64,2048]{2,1,0:T(8,128)(2,1)S(1)}, bf16[2,64,2048]{2,1,0:T(8,128)(2,1)S(1)}, u32[]{:S(2)}, u32[]{:S(2)}) collective-permute-start(bf16[2,64,2048]{2,1,0:T(8,128)(2,1)S(1)} %copy_bitcast_fusion.refs_0_), channel_id=1, source_target_pairs={{0,896},{128,0},{256,128},{384,256},{512,384},{640,512},{768,640},... | collective-permute-start | bytes 1572872 | tf_op jit(solution)/shard_map/ring/ppermute | solution.py:197
  53.3 1.9 %collective-permute-start.3 = (bf16[2,64,2048]{2,1,0:T(8,128)(2,1)S(1)}, bf16[2,64,2048]{2,1,0:T(8,128)(2,1)S(1)}, u32[]{:S(2)}, u32[]{:S(2)}) collective-permute-start(bf16[2,64,2048]{2,1,0:T(8,128)(2,1)S(1)} %copy_bitcast_fusion.refs_0_), channel_id=1, source_target_pairs={{0,128},{128,256},{256,384},{384,512},{512,640},{640,768},{768,896... | collective-permute-start | bytes 1572872 | tf_op jit(solution)/shard_map/ring/ppermute | solution.py:197
  55.2 0.0 copy-done.1
  55.2 2.5 %collective-permute-start.1 = (bf16[128,4096]{1,0:T(8,128)(2,1)S(1)}, bf16[128,4096]{1,0:T(8,128)(2,1)S(1)}, u32[]{:S(2)}, u32[]{:S(2)}) collective-permute-start(bf16[128,4096]{1,0:T(8,128)(2,1)S(1)} %copy-done.1), channel_id=1, source_target_pairs={{0,2},{1,3},{2,0},{3,1},{4,6},{5,7},{6,4},{7,5},{8,10},{9,11},{10,... | collective-permute-start | bytes 3145736 | tf_op jit(solution)/shard_map/pools/ppermute | solution.py:208
  57.7 1.7 %collective-permute-done.4.refs_2_ = bf16[2,64,2048]{2,1,0:T(8,128)(2,1)S(1)} collective-permute-done((bf16[2,64,2048]{2,1,0:T(8,128)(2,1)S(1)}, bf16[2,64,2048]{2,1,0:T(8,128)(2,1)S(1)}, u32[]{:S(2)}, u32[]{:S(2)}) %collective-permute-start.4) | collective-permute-done | bytes 524320 | tf_op jit(solution)/shard_map/ring/ppermute | solution.py:197
  59.4 5.3 %collective-permute-start.6 = (bf16[2,64,2048]{2,1,0:T(8,128)(2,1)S(1)}, bf16[2,64,2048]{2,1,0:T(8,128)(2,1)}, u32[]{:S(2)}, u32[]{:S(2)}) collective-permute-start(bf16[2,64,2048]{2,1,0:T(8,128)(2,1)S(1)} %collective-permute-done.4.refs_2_), channel_id=1, source_target_pairs={{0,896},{128,0},{256,128},{384,256},{512,384},{640,512},{768,640},... | collective-permute-start | bytes 1572872 | tf_op jit(solution)/shard_map/ring/ppermute | solution.py:197
  64.7 0.0 collective-permute-done.3.refs_1_
  64.7 1.9 %collective-permute-start.5 = (bf16[2,64,2048]{2,1,0:T(8,128)(2,1)S(1)}, bf16[2,64,2048]{2,1,0:T(8,128)(2,1)}, u32[]{:S(2)}, u32[]{:S(2)}) collective-permute-start(bf16[2,64,2048]{2,1,0:T(8,128)(2,1)S(1)} %collective-permute-done.3.refs_1_), channel_id=1, source_target_pairs={{0,128},{128,256},{256,384},{384,512},{512,640},{640,768},{768,896... | collective-permute-start | bytes 1572872 | tf_op jit(solution)/shard_map/ring/ppermute | solution.py:197
  66.6 0.1 hand.3
  66.7 0.0 copy-start.2
  66.8 0.9 copy-done.2
  67.6 7.1 %collective-permute-start.9 = (bf16[3,64,2048]{2,1,0:T(8,128)(2,1)S(1)}, bf16[3,64,2048]{2,1,0:T(8,128)(2,1)S(1)}, u32[]{:S(2)}, u32[]{:S(2)}) collective-permute-start(bf16[3,64,2048]{2,1,0:T(8,128)(2,1)S(1)} %get-tuple-element.18), channel_id=1, source_target_pairs={{0,1},{1,0},{2,3},{3,2},{4,5},{5,4},{6,7},{7,6},{8,9},{9,8},{10,11... | collective-permute-start | bytes 2359304 | tf_op jit(solution)/shard_map/ring/ppermute | solution.py:202
  74.7 0.0 collective-permute-done.6.refs_1_
  74.8 1.9 %collective-permute-start.8 = (bf16[2,64,2048]{2,1,0:T(8,128)(2,1)}, bf16[2,64,2048]{2,1,0:T(8,128)(2,1)}, u32[]{:S(2)}, u32[]{:S(2)}) collective-permute-start(bf16[2,64,2048]{2,1,0:T(8,128)(2,1)} %collective-permute-done.6.refs_1_), channel_id=1, source_target_pairs={{0,896},{128,0},{256,128},{384,256},{512,384},{640,512},{768,640},... | collective-permute-start | bytes 1572872 | tf_op jit(solution)/shard_map/ring/ppermute | solution.py:197
  76.7 0.0 collective-permute-done.5.refs_0_
  76.7 2.0 %hand.4 = (bf16[2,64,2048]{2,1,0:T(8,128)(2,1)S(1)}, bf16[2,64,2048]{2,1,0:T(8,128)(2,1)}) custom-call(bf16[2,64,2048]{2,1,0:T(8,128)(2,1)} %collective-permute-done.5.refs_0_, bf16[2,64,2048]{2,1,0:T(8,128)(2,1)} %collective-permute-done.6.refs_1_), custom_call_target="tpu_custom_call" | custom-call | flops 8589934592 | bytes 4194304 | tf_op jit(solution)/shard_map/ring/hand/pallas_call | solution.py:149
  78.7 0.8 copy-done.6
  79.5 7.5 %collective-permute-start.10 = (bf16[2,64,2048]{2,1,0:T(8,128)(2,1)}, bf16[2,64,2048]{2,1,0:T(8,128)(2,1)}, u32[]{:S(2)}, u32[]{:S(2)}) collective-permute-start(bf16[2,64,2048]{2,1,0:T(8,128)(2,1)} %get-tuple-element.19), channel_id=1, source_target_pairs={{0,1},{1,0},{2,3},{3,2},{4,5},{5,4},{6,7},{7,6},{8,9},{9,8},{10,11... | collective-permute-start | bytes 1572872 | tf_op jit(solution)/shard_map/ring/ppermute | solution.py:202
  87.1 2.2 %collective-permute-start.7 = (bf16[2,64,2048]{2,1,0:T(8,128)(2,1)}, bf16[2,64,2048]{2,1,0:T(8,128)(2,1)}, u32[]{:S(2)}, u32[]{:S(2)}) collective-permute-start(bf16[2,64,2048]{2,1,0:T(8,128)(2,1)} %collective-permute-done.5.refs_0_), channel_id=1, source_target_pairs={{0,128},{128,256},{256,384},{384,512},{512,640},{640,768},{768,896... | collective-permute-start | bytes 1572872 | tf_op jit(solution)/shard_map/ring/ppermute | solution.py:197
  89.3 0.0 collective-permute-done.1.p2.rest_10_
  89.3 1.9 %collective-permute-start = (bf16[128,4096]{1,0:T(8,128)(2,1)S(1)}, bf16[128,4096]{1,0:T(8,128)(2,1)S(1)}, u32[]{:S(2)}, u32[]{:S(2)}) collective-permute-start(bf16[128,4096]{1,0:T(8,128)(2,1)S(1)} %copy-done.1), channel_id=1, source_target_pairs={{0,1},{1,0},{2,3},{3,2},{4,5},{5,4},{6,7},{7,6},{8,9},{9,8},{10,11... | collective-permute-start | bytes 3145736 | tf_op jit(solution)/shard_map/pools/ppermute | solution.py:209
  91.2 0.0 collective-permute-done.9.rest_4_
  91.3 0.0 copy-start.4
  91.3 0.9 copy-done.4
  92.1 2.4 %collective-permute-start.2 = (bf16[128,4096]{1,0:T(8,128)(2,1)S(1)}, bf16[128,4096]{1,0:T(8,128)(2,1)}, u32[]{:S(2)}, u32[]{:S(2)}) collective-permute-start(bf16[128,4096]{1,0:T(8,128)(2,1)S(1)} %collective-permute-done.1.p2.rest_10_), channel_id=1, source_target_pairs={{0,1},{1,0},{2,3},{3,2},{4,5},{5,4},{6,7},{7,6},{8,9},{9,8},{10,11... | collective-permute-start | bytes 3145736 | tf_op jit(solution)/shard_map/pools/ppermute | solution.py:210
  94.6 0.1 pad_add_fusion.place_ref
  94.6 0.0 collective-permute-done.8.refs_1_
  94.6 0.0 collective-permute-done.10.rest_5_
  94.6 4.2 %collective-permute-done.7.refs_0_ = bf16[2,64,2048]{2,1,0:T(8,128)(2,1)} collective-permute-done((bf16[2,64,2048]{2,1,0:T(8,128)(2,1)}, bf16[2,64,2048]{2,1,0:T(8,128)(2,1)}, u32[]{:S(2)}, u32[]{:S(2)}) %collective-permute-start.7) | collective-permute-done | bytes 524320 | tf_op jit(solution)/shard_map/ring/ppermute | solution.py:197
  98.8 1.0 slice.6
  99.8 1.0 slice.7
  100.8 0.0 copy-start
  100.8 0.0 copy-start.9
  100.8 2.1 %collective-permute-start.13 = (bf16[1,64,2048]{2,1,0:T(8,128)(2,1)S(1)}, bf16[1,64,2048]{2,1,0:T(8,128)(2,1)S(1)}, u32[]{:S(2)}, u32[]{:S(2)}) collective-permute-start(bf16[1,64,2048]{2,1,0:T(8,128)(2,1)S(1)} %slice.7), channel_id=1, source_target_pairs={{0,897},{128,1},{256,129},{384,257},{512,385},{640,513},{768,641},... | collective-permute-start | bytes 786440 | tf_op jit(solution)/shard_map/ring/ppermute | solution.py:205
  102.8 4.1 %collective-permute-start.11 = (bf16[1,64,2048]{2,1,0:T(8,128)(2,1)S(1)}, bf16[1,64,2048]{2,1,0:T(8,128)(2,1)S(1)}, u32[]{:S(2)}, u32[]{:S(2)}) collective-permute-start(bf16[1,64,2048]{2,1,0:T(8,128)(2,1)S(1)} %slice.6), channel_id=1, source_target_pairs={{0,128},{128,256},{256,384},{384,512},{512,640},{640,768},{768,896... | collective-permute-start | bytes 786440 | tf_op jit(solution)/shard_map/ring/ppermute | solution.py:204
  107.0 1.3 %hand.5 = (bf16[2,64,2048]{2,1,0:T(8,128)(2,1)S(1)}, bf16[2,64,2048]{2,1,0:T(8,128)(2,1)S(1)}) custom-call(bf16[2,64,2048]{2,1,0:T(8,128)(2,1)} %collective-permute-done.7.refs_0_, bf16[2,64,2048]{2,1,0:T(8,128)(2,1)} %collective-permute-done.8.refs_1_), custom_call_target="tpu_custom_call" | custom-call | flops 8589934592 | bytes 4194304 | tf_op jit(solution)/shard_map/ring/hand/pallas_call | solution.py:149
  108.2 1.9 %collective-permute-start.12 = (bf16[2,64,2048]{2,1,0:T(8,128)(2,1)S(1)}, bf16[2,64,2048]{2,1,0:T(8,128)(2,1)S(1)}, u32[]{:S(2)}, u32[]{:S(2)}) collective-permute-start(bf16[2,64,2048]{2,1,0:T(8,128)(2,1)S(1)} %get-tuple-element.25), channel_id=1, source_target_pairs={{0,1},{1,0},{2,3},{3,2},{4,5},{5,4},{6,7},{7,6},{8,9},{9,8},{10,11... | collective-permute-start | bytes 1572872 | tf_op jit(solution)/shard_map/ring/ppermute | solution.py:202
  110.2 0.0 collective-permute-done.p1.rest_9_
  110.2 0.0 collective-permute-done.2.p3.rest_11_
  110.2 0.0 copy-start.10
  110.2 0.0 copy-start.11
  110.2 0.0 copy-done
  110.2 0.0 copy-done.9
  110.2 0.6 copy-done.10
  110.9 0.0 copy-done.11
  110.9 2.9 %hard.1.hard_ref = f32[128,512]{1,0:T(8,128)S(1)} custom-call(s32[4]{0:T(128)S(1)} %pad_add_fusion.place_ref, s32[30,128]{1,0:T(8,128)S(1)} %bitcast.27, s32[1,128]{1,0:T(1,128)S(1)} %bitcast.29, s32[4,32]{1,0:T(4,128)S(1)} %bitcast.28, bf16[128,4096]{1,0:T(8,128)(2,1)S(1)} %copy-done, bf16[128,4096]{1,0:T(8,128)(2,1)S(1)} %copy-done.1, ...), custom_call_target="tpu_custom_call" | custom-call | flops 8589934592 | bytes 6291456 | tf_op jit(solution)/shard_map/hard/pallas_call | solution.py:136
  113.8 0.0 collective-permute-done.13.rest_7_
  113.8 0.0 collective-permute-done.11.rest_3_
  113.8 0.0 collective-permute-done.12.rest_6_
  113.8 0.0 copy-start.8
  113.9 0.0 copy-done.3
  113.9 0.0 copy-done.5
  113.9 0.0 copy-done.7
  113.9 0.6 copy-done.8
  114.5 6.0 %tail.1 = (bf16[128,4096]{1,0:T(8,128)(2,1)}, f32[1,128]{1,0:T(1,128)}) custom-call(s32[4]{0:T(128)S(1)} %pad_add_fusion.place_ref, s32[1,128]{1,0:T(1,128)S(1)} %bitcast.26, f32[128,512]{1,0:T(8,128)S(1)} %hard.1.hard_ref, bf16[128,4096]{1,0:T(8,128)(2,1)S(1)} %copy-done, bf16[3,64,2048]{2,1,0:T(8,128)(2,1)S(1)} %copy-done.3, ...), custom_call_target="tpu_custom_call" | custom-call | flops 2147483648 | bytes 12582912 | tf_op jit(solution)/shard_map/tail/pallas_call | solution.py:163
  (8 shorter events, 0.1 us)
Async XLA Ops:
  2.1 24.9 %all-to-all-start = ((bf16[8,2,2048]{2,1,0:T(2,128)(2,1)}), bf16[8,2,2048]{2,1,0:T(2,128)(2,1)S(1)}, u32[]{:S(2)}, u32[]{:S(2)}) async-start(bf16[8,2,2048]{2,1,0:T(2,128)(2,1)} %bitcast.9), calls=%async_computation | async-start | bytes 131072 | tf_op jit(solution)/shard_map/cross/all_to_all | solution.py:187
  27.9 27.3 %copy-start.1 = (bf16[128,4096]{1,0:T(8,128)(2,1)S(1)}, bf16[128,4096]{1,0:T(8,128)(2,1)}, u32[]{:S(2)}) copy-start(bf16[128,4096]{1,0:T(8,128)(2,1)} %rest_8_) | copy-start | bytes 3145732
  47.2 12.1 %collective-permute-start.4 = (bf16[2,64,2048]{2,1,0:T(8,128)(2,1)S(1)}, bf16[2,64,2048]{2,1,0:T(8,128)(2,1)S(1)}, u32[]{:S(2)}, u32[]{:S(2)}) collective-permute-start(bf16[2,64,2048]{2,1,0:T(8,128)(2,1)S(1)} %copy_bitcast_fusion.refs_0_), channel_id=1, source_target_pairs={{0,896},{128,0},{256,128},{384,256},{512,384},{640,512},{768,640},... | collective-permute-start | bytes 1572872 | tf_op jit(solution)/shard_map/ring/ppermute | solution.py:197
  53.3 11.4 %collective-permute-start.3 = (bf16[2,64,2048]{2,1,0:T(8,128)(2,1)S(1)}, bf16[2,64,2048]{2,1,0:T(8,128)(2,1)S(1)}, u32[]{:S(2)}, u32[]{:S(2)}) collective-permute-start(bf16[2,64,2048]{2,1,0:T(8,128)(2,1)S(1)} %copy_bitcast_fusion.refs_0_), channel_id=1, source_target_pairs={{0,128},{128,256},{256,384},{384,512},{512,640},{640,768},{768,896... | collective-permute-start | bytes 1572872 | tf_op jit(solution)/shard_map/ring/ppermute | solution.py:197
  55.2 34.1 %collective-permute-start.1 = (bf16[128,4096]{1,0:T(8,128)(2,1)S(1)}, bf16[128,4096]{1,0:T(8,128)(2,1)S(1)}, u32[]{:S(2)}, u32[]{:S(2)}) collective-permute-start(bf16[128,4096]{1,0:T(8,128)(2,1)S(1)} %copy-done.1), channel_id=1, source_target_pairs={{0,2},{1,3},{2,0},{3,1},{4,6},{5,7},{6,4},{7,5},{8,10},{9,11},{10,... | collective-permute-start | bytes 3145736 | tf_op jit(solution)/shard_map/pools/ppermute | solution.py:208
  59.4 15.4 %collective-permute-start.6 = (bf16[2,64,2048]{2,1,0:T(8,128)(2,1)S(1)}, bf16[2,64,2048]{2,1,0:T(8,128)(2,1)}, u32[]{:S(2)}, u32[]{:S(2)}) collective-permute-start(bf16[2,64,2048]{2,1,0:T(8,128)(2,1)S(1)} %collective-permute-done.4.refs_2_), channel_id=1, source_target_pairs={{0,896},{128,0},{256,128},{384,256},{512,384},{640,512},{768,640},... | collective-permute-start | bytes 1572872 | tf_op jit(solution)/shard_map/ring/ppermute | solution.py:197
  64.7 12.0 %collective-permute-start.5 = (bf16[2,64,2048]{2,1,0:T(8,128)(2,1)S(1)}, bf16[2,64,2048]{2,1,0:T(8,128)(2,1)}, u32[]{:S(2)}, u32[]{:S(2)}) collective-permute-start(bf16[2,64,2048]{2,1,0:T(8,128)(2,1)S(1)} %collective-permute-done.3.refs_1_), channel_id=1, source_target_pairs={{0,128},{128,256},{256,384},{384,512},{512,640},{640,768},{768,896... | collective-permute-start | bytes 1572872 | tf_op jit(solution)/shard_map/ring/ppermute | solution.py:197
  66.7 0.9 copy-start.2
  67.6 23.6 %collective-permute-start.9 = (bf16[3,64,2048]{2,1,0:T(8,128)(2,1)S(1)}, bf16[3,64,2048]{2,1,0:T(8,128)(2,1)S(1)}, u32[]{:S(2)}, u32[]{:S(2)}) collective-permute-start(bf16[3,64,2048]{2,1,0:T(8,128)(2,1)S(1)} %get-tuple-element.18), channel_id=1, source_target_pairs={{0,1},{1,0},{2,3},{3,2},{4,5},{5,4},{6,7},{7,6},{8,9},{9,8},{10,11... | collective-permute-start | bytes 2359304 | tf_op jit(solution)/shard_map/ring/ppermute | solution.py:202
  74.8 19.9 %collective-permute-start.8 = (bf16[2,64,2048]{2,1,0:T(8,128)(2,1)}, bf16[2,64,2048]{2,1,0:T(8,128)(2,1)}, u32[]{:S(2)}, u32[]{:S(2)}) collective-permute-start(bf16[2,64,2048]{2,1,0:T(8,128)(2,1)} %collective-permute-done.6.refs_1_), channel_id=1, source_target_pairs={{0,896},{128,0},{256,128},{384,256},{512,384},{640,512},{768,640},... | collective-permute-start | bytes 1572872 | tf_op jit(solution)/shard_map/ring/ppermute | solution.py:197
  78.7 0.8 copy-start.6
  79.5 15.1 %collective-permute-start.10 = (bf16[2,64,2048]{2,1,0:T(8,128)(2,1)}, bf16[2,64,2048]{2,1,0:T(8,128)(2,1)}, u32[]{:S(2)}, u32[]{:S(2)}) collective-permute-start(bf16[2,64,2048]{2,1,0:T(8,128)(2,1)} %get-tuple-element.19), channel_id=1, source_target_pairs={{0,1},{1,0},{2,3},{3,2},{4,5},{5,4},{6,7},{7,6},{8,9},{9,8},{10,11... | collective-permute-start | bytes 1572872 | tf_op jit(solution)/shard_map/ring/ppermute | solution.py:202
  87.1 11.7 %collective-permute-start.7 = (bf16[2,64,2048]{2,1,0:T(8,128)(2,1)}, bf16[2,64,2048]{2,1,0:T(8,128)(2,1)}, u32[]{:S(2)}, u32[]{:S(2)}) collective-permute-start(bf16[2,64,2048]{2,1,0:T(8,128)(2,1)} %collective-permute-done.5.refs_0_), channel_id=1, source_target_pairs={{0,128},{128,256},{256,384},{384,512},{512,640},{640,768},{768,896... | collective-permute-start | bytes 1572872 | tf_op jit(solution)/shard_map/ring/ppermute | solution.py:197
  89.3 20.8 %collective-permute-start = (bf16[128,4096]{1,0:T(8,128)(2,1)S(1)}, bf16[128,4096]{1,0:T(8,128)(2,1)S(1)}, u32[]{:S(2)}, u32[]{:S(2)}) collective-permute-start(bf16[128,4096]{1,0:T(8,128)(2,1)S(1)} %copy-done.1), channel_id=1, source_target_pairs={{0,1},{1,0},{2,3},{3,2},{4,5},{5,4},{6,7},{7,6},{8,9},{9,8},{10,11... | collective-permute-start | bytes 3145736 | tf_op jit(solution)/shard_map/pools/ppermute | solution.py:209
  91.3 0.9 copy-start.4
  92.1 18.0 %collective-permute-start.2 = (bf16[128,4096]{1,0:T(8,128)(2,1)S(1)}, bf16[128,4096]{1,0:T(8,128)(2,1)}, u32[]{:S(2)}, u32[]{:S(2)}) collective-permute-start(bf16[128,4096]{1,0:T(8,128)(2,1)S(1)} %collective-permute-done.1.p2.rest_10_), channel_id=1, source_target_pairs={{0,1},{1,0},{2,3},{3,2},{4,5},{5,4},{6,7},{7,6},{8,9},{9,8},{10,11... | collective-permute-start | bytes 3145736 | tf_op jit(solution)/shard_map/pools/ppermute | solution.py:210
  100.8 9.5 %copy-start = (bf16[128,4096]{1,0:T(8,128)(2,1)S(1)}, bf16[128,4096]{1,0:T(8,128)(2,1)}, u32[]{:S(2)}) copy-start(bf16[128,4096]{1,0:T(8,128)(2,1)} %q_ref.3) | copy-start | bytes 3145732
  100.8 9.5 %copy-start.9 = (s32[128,30]{0,1:T(8,128)S(1)}, s32[128,30]{0,1:T(8,128)}, u32[]{:S(2)}) copy-start(s32[128,30]{0,1:T(8,128)} %param.12) | copy-start | bytes 46084
  100.8 13.0 %collective-permute-start.13 = (bf16[1,64,2048]{2,1,0:T(8,128)(2,1)S(1)}, bf16[1,64,2048]{2,1,0:T(8,128)(2,1)S(1)}, u32[]{:S(2)}, u32[]{:S(2)}) collective-permute-start(bf16[1,64,2048]{2,1,0:T(8,128)(2,1)S(1)} %slice.7), channel_id=1, source_target_pairs={{0,897},{128,1},{256,129},{384,257},{512,385},{640,513},{768,641},... | collective-permute-start | bytes 786440 | tf_op jit(solution)/shard_map/ring/ppermute | solution.py:205
  102.8 11.0 %collective-permute-start.11 = (bf16[1,64,2048]{2,1,0:T(8,128)(2,1)S(1)}, bf16[1,64,2048]{2,1,0:T(8,128)(2,1)S(1)}, u32[]{:S(2)}, u32[]{:S(2)}) collective-permute-start(bf16[1,64,2048]{2,1,0:T(8,128)(2,1)S(1)} %slice.6), channel_id=1, source_target_pairs={{0,128},{128,256},{256,384},{384,512},{512,640},{640,768},{768,896... | collective-permute-start | bytes 786440 | tf_op jit(solution)/shard_map/ring/ppermute | solution.py:204
  108.2 5.6 %collective-permute-start.12 = (bf16[2,64,2048]{2,1,0:T(8,128)(2,1)S(1)}, bf16[2,64,2048]{2,1,0:T(8,128)(2,1)S(1)}, u32[]{:S(2)}, u32[]{:S(2)}) collective-permute-start(bf16[2,64,2048]{2,1,0:T(8,128)(2,1)S(1)} %get-tuple-element.25), channel_id=1, source_target_pairs={{0,1},{1,0},{2,3},{3,2},{4,5},{5,4},{6,7},{7,6},{8,9},{9,8},{10,11... | collective-permute-start | bytes 1572872 | tf_op jit(solution)/shard_map/ring/ppermute | solution.py:202
  110.2 0.7 copy-start.10
  110.2 0.7 copy-start.11
  110.9 3.0 %copy-start.3 = (bf16[3,64,2048]{2,1,0:T(8,128)(2,1)S(1)}, bf16[3,64,2048]{2,1,0:T(8,128)(2,1)}, u32[]{:S(2)}) copy-start(bf16[3,64,2048]{2,1,0:T(8,128)(2,1)} %copy-done.2) | copy-start | bytes 2359300
  110.9 3.0 %copy-start.5 = (bf16[3,64,2048]{2,1,0:T(8,128)(2,1)S(1)}, bf16[3,64,2048]{2,1,0:T(8,128)(2,1)}, u32[]{:S(2)}) copy-start(bf16[3,64,2048]{2,1,0:T(8,128)(2,1)} %copy-done.4) | copy-start | bytes 2359300
  110.9 3.0 %copy-start.7 = (bf16[2,64,2048]{2,1,0:T(8,128)(2,1)S(1)}, bf16[2,64,2048]{2,1,0:T(8,128)(2,1)}, u32[]{:S(2)}) copy-start(bf16[2,64,2048]{2,1,0:T(8,128)(2,1)} %copy-done.6) | copy-start | bytes 1572868
  113.8 0.7 copy-start.8

commit v5 on v4

v5 whole, which is shorter than its diff:
```python
import functools

import jax
import jax.numpy as jnp
import numpy as np
from jax import lax
from jax.experimental import pallas as pl
from jax.experimental.pallas import tpu as pltpu
from jax.sharding import Mesh, PartitionSpec as P

DEVICES = np.arange(1024).reshape(8, 4, 8, 2, 2)


def lines(order):
    return DEVICES.transpose(order)


ALONG_Y = lines((0, 1, 3, 4, 2))
ALONG_Z = lines((1, 2, 3, 4, 0))
CROSS = lines((0, 2, 3, 1, 4)).reshape(-1, 8).tolist()
NEAR = np.concatenate([ALONG_Y[:, :, :, 0].reshape(-1, 8), ALONG_Z[:, :, :, 1].reshape(-1, 8)]).tolist()


def ring(groups):
    return [(g[i], g[(i + 1 - 2 * (g[i] & 1)) % 8]) for g in groups.reshape(-1, 8) for i in range(8)]


RING_Z = ring(ALONG_Z)
RING_Y = ring(ALONG_Y)
OTHER_CORE = [(i, i ^ 1) for i in range(1024)]
OTHER_CHIP = [(i, i ^ 2) for i in range(1024)]
BLOCK = 64


def dots(a, b):
    return lax.dot_general(a, b, (((1,), (1,)), ((), ())), preferred_element_type=jnp.float32)


def hard_kernel(place_ref, refs_ref, count_ref, list_ref, q_ref, pool, out_ref):
    most, rows = refs_ref.shape
    owners, slots = list_ref.shape
    span = owners * slots
    own = place_ref[3]
    at = lax.broadcasted_iota(jnp.int32, (span, rows), 0)
    live = lax.broadcasted_iota(jnp.int32, (most, rows), 0) < count_ref[...]
    refs = jnp.where(live, refs_ref[...], -1)
    present = jnp.zeros((span, rows), jnp.float32)
    for i in range(most):
        present = present + jnp.where(refs[i : i + 1, :] == at, 1.0, 0.0)
    present = present.astype(jnp.bfloat16)
    row = lax.broadcasted_iota(jnp.int32, (span, span), 0)
    owner = lax.broadcasted_iota(jnp.int32, (span, span), 1) // slots
    lists = jnp.concatenate([list_ref[i : i + 1, :] for i in range(owners)], axis=1)
    same = lists == row
    for i in range(4):
        match = jnp.where(same & (owner == (own ^ i)), 1.0, 0.0).astype(jnp.bfloat16)
        used = lax.dot_general(present, match, (((0,), (1,)), ((), ())), preferred_element_type=jnp.float32)
        value = 0.0 if i else dots(q_ref[...], pool[...])
        out_ref[:, i * span : (i + 1) * span] = jnp.where(used > 0, value, -jnp.inf)


def hard_rest_kernel(hard_ref, q_ref, p1, p2, p3, out_ref):
    span = p1.shape[0]
    out_ref[:, :span] = hard_ref[:, :span]
    for i, pool in ((1, p1), (2, p2), (3, p3)):
        at = slice(i * span, (i + 1) * span)
        out_ref[:, at] = hard_ref[:, at] + dots(q_ref[...], pool[...])


def passage(shape, dim, place, ring_is_z):
    at = lax.broadcasted_iota(jnp.int32, shape, dim)
    block, inner, hi, row = at >> 6, (at >> 3) & 7, (at >> 1) & 3, at & 1
    step = (block + 1) >> 1
    below = (block & 1) != place[2]
    shift = jnp.where(below, 8 - step, step)
    if ring_is_z:
        z, y = (place[0] + shift) & 7, inner
    else:
        z, y = inner, (place[1] + shift) & 7
    return ((z * 4 + hi) * 8 + y) * 2 + row


def sort_kernel(place_ref, mine_ref, theirs_ref, left_ref, right_ref, keep_ref):
    core = place_ref[2]
    own = 8 * core

    def order(source, target):
        for i in range(8):
            piece = source[i]
            first, second = piece[:8], piece[8:]
            at = slice(8 * i, 8 * i + 8)
            target[0, at] = jnp.where(own == 0, first, second)
            target[1, at] = jnp.where(own == 0, second, first)

    @pl.when(core == 0)
    def _():
        order(mine_ref, left_ref)
        order(theirs_ref, right_ref)

    @pl.when(core == 1)
    def _():
        order(theirs_ref, left_ref)
        order(mine_ref, right_ref)

    keep_ref[0] = left_ref[0]
    keep_ref[1] = right_ref[0]


def hand_kernel(left_ref, right_ref, keep_left_ref, keep_right_ref, give_ref):
    keep_left_ref[0] = left_ref[0]
    keep_right_ref[0] = right_ref[0]
    give_ref[0] = left_ref[1]
    give_ref[1] = right_ref[1]


def tail_kernel(place_ref, pos_ref, hard_ref, q_ref, *rest):
    blocks, (p0, p1, p2, p3), (grad_ref, loss_ref, left_ref, right_ref) = rest[:12], rest[12:16], rest[16:]
    keep, l1, r1, e1, l2, r2, e2, l3, r3, e3, l4, r4 = blocks
    half = left_ref.shape[1]
    total = left_ref.shape[0]
    lefts = (keep.at[0], l1.at[0], e1.at[0], l2.at[0], e2.at[0], l3.at[0], e3.at[0], l4.at[0])
    rights = (keep.at[1], r1.at[0], e1.at[1], r2.at[0], e2.at[1], r3.at[0], e3.at[1], r4.at[0])
    for parts, rows_ref in ((lefts, left_ref), (rights, right_ref)):
        for i, part in enumerate(parts):
            rows_ref[i * BLOCK : (i + 1) * BLOCK, :] = part[...]

    place = (place_ref[0], place_ref[1], place_ref[2])
    left_index = passage((1, total), 1, place, True)
    right_index = passage((total, 1), 0, place, False)
    order = jnp.where(right_index == left_index, 1.0, 0.0).astype(jnp.bfloat16)
    right_logits = dots(q_ref[:, half:], right_ref[...])
    high = right_logits.astype(jnp.bfloat16)
    left_over = right_logits - high.astype(jnp.float32)
    middle = left_over.astype(jnp.bfloat16)
    low = (left_over - middle.astype(jnp.float32)).astype(jnp.bfloat16)
    moved = jnp.dot(low, order, preferred_element_type=jnp.float32)
    moved = moved + jnp.dot(middle, order, preferred_element_type=jnp.float32)
    moved = moved + jnp.dot(high, order, preferred_element_type=jnp.float32)
    logits = dots(q_ref[:, :half], left_ref[...]) + moved

    hard = hard_ref[...]
    peak = jnp.maximum(jnp.max(logits, axis=1, keepdims=True), jnp.max(hard, axis=1, keepdims=True))
    cycle_exp = jnp.exp(logits - peak)
    hard_exp = jnp.exp(hard - peak)
    denominator = jnp.sum(cycle_exp, axis=1, keepdims=True) + jnp.sum(hard_exp, axis=1, keepdims=True)
    rows = q_ref.shape[0]
    eye = lax.broadcasted_iota(jnp.int32, (rows, rows), 0) == lax.broadcasted_iota(jnp.int32, (rows, rows), 1)
    positives = jnp.sum(jnp.where(eye, pos_ref[...].astype(jnp.float32), 0.0), axis=1, keepdims=True)
    positive = left_index == positives.astype(jnp.int32)
    chosen = jnp.sum(jnp.where(positive, logits, 0.0), axis=1, keepdims=True)
    loss = jnp.log(denominator) + peak - chosen
    loss_ref[...] = jnp.sum(jnp.where(eye, loss, 0.0), axis=0, keepdims=True)
    weights = (cycle_exp / denominator - jnp.where(positive, 1.0, 0.0)).astype(jnp.bfloat16)
    hard_weights = (hard_exp / denominator).astype(jnp.bfloat16)
    right_weights = dots(weights, order).astype(jnp.bfloat16)

    for start, w, rows_ref in ((0, weights, left_ref), (half, right_weights, right_ref)):
        all_weights = jnp.concatenate([w, hard_weights], axis=1)
        for chunk in range(0, half, 512):
            at = slice(start + chunk, start + chunk + 512)
            all_rows = [rows_ref[:, chunk : chunk + 512]] + [pool[:, at] for pool in (p0, p1, p2, p3)]
            grad = jnp.dot(all_weights, jnp.concatenate(all_rows, axis=0), preferred_element_type=jnp.float32)
            grad_ref[:, at] = grad.astype(jnp.bfloat16)


VMEM = functools.partial(pl.BlockSpec, memory_space=pltpu.VMEM)
SMEM = functools.partial(pl.BlockSpec, memory_space=pltpu.SMEM)


def small_call(kernel, outs, args, name, scalars=0, flops=2**33):
    return pl.pallas_call(
        kernel,
        out_shape=outs,
        in_specs=[SMEM()] * scalars + [VMEM()] * (len(args) - scalars),
        out_specs=jax.tree.map(lambda _: VMEM(), outs),
        compiler_params=pltpu.CompilerParams(vmem_limit_bytes=8 * 2**20),
        cost_estimate=pl.CostEstimate(flops=flops, bytes_accessed=4 * 2**20, transcendentals=0),
        name=name,
    )(*args)


def hard_call(place, refs, count, lists, queries, pool):
    rows = queries.shape[0]
    out = jax.ShapeDtypeStruct((rows, 4 * lists.size), jnp.float32)
    args = (place, refs.T, count.reshape(1, rows), lists[0], queries, pool)
    return small_call(hard_kernel, out, args, "hard", scalars=1)


def hard_rest_call(hard, queries, pools):
    out = jax.ShapeDtypeStruct(hard.shape, hard.dtype)
    return small_call(hard_rest_kernel, out, (hard, queries, *pools), "hard_rest")


def sort_call(place, mine, theirs):
    out = jax.ShapeDtypeStruct((2, BLOCK, mine.shape[2]), mine.dtype)
    return small_call(sort_kernel, (out, out, out), (place, mine, theirs), "sort", scalars=1)


def hand_call(left, right):
    out = jax.ShapeDtypeStruct(left.shape, left.dtype)
    one = jax.ShapeDtypeStruct((1,) + left.shape[1:], left.dtype)
    return small_call(hand_kernel, (one, one, out), (left, right), "hand")


def tail_call(place, positive, hard, queries, blocks, pools):
    rows, width = queries.shape
    half = width // 2
    return pl.pallas_call(
        tail_kernel,
        out_shape=(
            jax.ShapeDtypeStruct((rows, width), jnp.bfloat16),
            jax.ShapeDtypeStruct((1, rows), jnp.float32),
        ),
        in_specs=[SMEM()] + [VMEM()] * (3 + len(blocks) + len(pools)),
        out_specs=(VMEM(), VMEM()),
        scratch_shapes=[pltpu.VMEM((8 * BLOCK, half), jnp.bfloat16), pltpu.VMEM((8 * BLOCK, half), jnp.bfloat16)],
        compiler_params=pltpu.CompilerParams(vmem_limit_bytes=16 * 2**20),
        cost_estimate=pl.CostEstimate(flops=2**31, bytes_accessed=12 * 2**20, transcendentals=2**17),
        name="tail",
    )(place, positive.reshape(1, rows), hard, queries, *blocks, *pools)


def body(queries, passages, pool, positive_ids, request_lists, hard_refs, hard_count):
    half = passages.shape[1] // 2
    device = lax.axis_index("d")
    core = device & 1
    place = jnp.stack([device >> 7, (device >> 2) & 7, core, device & 3]).astype(jnp.int32)

    with jax.named_scope("cross"):
        halves = passages.reshape(2, 2, half).transpose(1, 0, 2)
        sent = jnp.broadcast_to(halves[None], (4, 2, 2, half)).reshape(8, 2, half)
        got = lax.all_to_all(sent, "d", 0, 0, axis_index_groups=CROSS, tiled=True)
    with jax.named_scope("own_pool"):
        hard = hard_call(place, hard_refs, hard_count, request_lists, queries, pool)
    got, hard = lax.optimization_barrier((got, hard))
    with jax.named_scope("near"):
        got = got.reshape(4, 2, 2, half).transpose(1, 0, 2, 3).reshape(1, 16, half)
        sent = jnp.broadcast_to(got, (8, 16, half))
        near = lax.all_to_all(sent, "d", 0, 0, axis_index_groups=NEAR, tiled=True)
        theirs = lax.ppermute(near, "d", OTHER_CORE)
        left, right, keep = sort_call(place, near, theirs)
    with jax.named_scope("pool_x"):
        near, pool = lax.optimization_barrier((near, pool))
        pool_x = lax.ppermute(pool, "d", OTHER_CHIP)
    with jax.named_scope("ring"):
        blocks = [keep]
        for step in range(3):
            left, right = lax.ppermute(left, "d", RING_Z), lax.ppermute(right, "d", RING_Y)
            if step == 0:
                left, pool = lax.optimization_barrier((left, pool))
                pool_c = lax.ppermute(pool, "d", OTHER_CORE)
            if step == 2:
                left, right, *blocks = lax.optimization_barrier((left, right, *blocks))
            keep_left, keep_right, give = hand_call(left, right)
            blocks += [keep_left, keep_right, lax.ppermute(give, "d", OTHER_CORE)]
        blocks += [lax.ppermute(keep_left, "d", RING_Z), lax.ppermute(keep_right, "d", RING_Y)]
    with jax.named_scope("other_pools"):
        pool_xc = lax.ppermute(pool_x, "d", OTHER_CORE)
        pools = (pool, pool_c, pool_x, pool_xc)
        hard = hard_rest_call(hard, queries, pools[1:])
    grad, loss = tail_call(place, positive_ids, hard, queries, blocks, pools)
    return grad, loss.reshape(-1)


def solution(mesh):
    flat = Mesh(mesh.devices.reshape(1024), ("d",))
    return jax.shard_map(
        body,
        mesh=flat,
        in_specs=(P("d", None), P("d", None), P("d", None), P("d"), P("d", None, None), P("d", None), P("d")),
        out_specs=(P("d", None), P("d")),
        check_vma=False,
    )
```

time: 121 us -> 114 us (0.942)
  Pallas kernels: 12.3 us -> 8.21 us
  local copies, waits for them, and re-layouts: 8.08 us -> 4.69 us
    ppermute x11 -> x12, waiting for transfers between devices: 5.9 us -> 11.1 us  [the longest x3 3.91 us: body(): lax.ppermute(right, 'd', RING_Y)]
    all_to_all x1, waiting for transfers between devices: 7.47 us -> 2.98 us  [body(): got = lax.all_to_all(sent, 'd', 0, 0, axis_index_groups=CROSS, tiled=True)]
    pallas_call x4 -> x6, Pallas kernels: 6.34 us -> 3.19 us  [small_call(): pl.pallas_call(kernel, out_shape=outs, in_specs=[SMEM()] * scalars + [VME...]
    slice x2 -> x0, local copies, waits for them, and re-layouts: 1.94 us -> none  [the longest x1 0.97 us: body(): handed.append(lax.ppermute(down[1:], 'd', DOWN_OTHER_CORE))]
    ppermute x11 -> x12, starting transfers between devices: 42 us -> 40.9 us  [the longest x3 20.4 us: body(): lax.ppermute(left, 'd', RING_Z)]
    unnamed x24 -> x16, local copies, waits for them, and re-layouts: 3.86 us -> 3.15 us
  transfers between devices with their start and end apart: 15 -> 16, of which waited for: 3 -> 6; matrix products, arithmetic and copies ran while one was open for 2% -> 0% of each run, Pallas kernels for 5% -> 2%
where the time goes in v5:
time: 114 us; the launch traced here: 112 us
  starting transfers between devices  65.2 us (57%)
  blocking collectives  19.2 us (17%)
  waiting for transfers between devices  14.1 us (12%)
  Pallas kernels  8.21 us (7%)
  local copies, waits for them, and re-layouts  4.69 us (4%)
    ppermute x3, starting transfers between devices, body(): lax.ppermute(left, 'd', RING_Z)  20.4 us
    all_to_all x1, blocking collectives, body(): near = lax.all_to_all(sent, 'd', 0, 0, axis_index_groups=NEAR, tiled=True)  19.2 us
    all_to_all x1, starting transfers between devices, body(): got = lax.all_to_all(sent, 'd', 0, 0, axis_index_groups=CROSS, tiled=True)  17.4 us
    ppermute x3, starting transfers between devices, body(): lax.ppermute(right, 'd', RING_Y)  5.76 us
    ppermute x3, starting transfers between devices, body(): blocks += [keep_left, keep_right, lax.ppermute(give, 'd', OTHER_CORE)]  5.76 us
    pallas_call x1, Pallas kernels, tail_call(): pl.pallas_call(tail_kernel, out_shape=(jax.ShapeDtypeStruct((rows, width)...  5.02 us
    ppermute x1, starting transfers between devices, body(): lax.ppermute(keep_left, 'd', RING_Z)  4.13 us
    ppermute x3, waiting for transfers between devices, body(): lax.ppermute(right, 'd', RING_Y)  3.91 us
  transfers between devices with their start and end apart: 16, of which 6 were waited for; matrix products, arithmetic and copies ran while one was open for 0% of the time, Pallas kernels for 2%

profile of v5, /device:TPU:1, one launch (start us, length us, event | category | flops | bytes accessed | tf_op | source)
XLA Modules:
  0.0 112.3 jit_solution(12343329890875796892)
XLA Ops:
  0.6 0.7 reshape.26
  1.4 0.7 broadcast_in_dim.6
  2.1 17.4 %all-to-all-start = ((bf16[8,2,2048]{2,1,0:T(2,128)(2,1)}), bf16[8,2,2048]{2,1,0:T(2,128)(2,1)S(1)}, u32[]{:S(2)}, u32[]{:S(2)}) async-start(bf16[8,2,2048]{2,1,0:T(2,128)(2,1)} %bitcast.6), calls=%async_computation | async-start | bytes 131072 | tf_op jit(solution)/shard_map/cross/all_to_all | solution.py:232
  19.5 0.0 copy-start.5
  19.5 0.1 pad_add_fusion.place_ref
  19.5 0.0 copy-start.6
  19.5 0.0 copy-start.7
  19.5 0.6 copy-done.5
  20.2 0.0 copy-done.6
  20.2 0.0 copy-done.7
  20.2 0.0 copy-start
  20.2 1.2 %copy-done = bf16[128,4096]{1,0:T(8,128)(2,1)S(1)} copy-done((bf16[128,4096]{1,0:T(8,128)(2,1)S(1)}, bf16[128,4096]{1,0:T(8,128)(2,1)}, u32[]{:S(2)}) %copy-start) | copy-done | bytes 1048600
  21.5 0.0 copy-start.2
  21.5 1.2 %copy-done.2 = bf16[128,4096]{1,0:T(8,128)(2,1)S(1)} copy-done((bf16[128,4096]{1,0:T(8,128)(2,1)S(1)}, bf16[128,4096]{1,0:T(8,128)(2,1)}, u32[]{:S(2)}) %copy-start.2) | copy-done | bytes 1048600
  22.7 1.3 %hard.1.hard_ref = f32[128,512]{1,0:T(8,128)S(1)} custom-call(s32[4]{0:T(128)S(1)} %pad_add_fusion.place_ref, s32[30,128]{1,0:T(8,128)S(1)} %bitcast.15, s32[1,128]{1,0:T(1,128)S(1)} %bitcast.17, s32[4,32]{1,0:T(4,128)S(1)} %bitcast.16, bf16[128,4096]{1,0:T(8,128)(2,1)S(1)} %copy-done, bf16[128,4096]{1,0:T(8,128)(2,1)S(1)} %copy-done.2), custom_call_target="tpu_custom_call" | custom-call | flops 8589934592 | bytes 4194304 | tf_op jit(solution)/shard_map/own_pool/hard/pallas_call | solution.py:171
  24.0 3.0 %all-to-all-done = bf16[8,2,2048]{2,1,0:T(2,128)(2,1)S(1)} async-done(((bf16[8,2,2048]{2,1,0:T(2,128)(2,1)}), bf16[8,2,2048]{2,1,0:T(2,128)(2,1)S(1)}, u32[]{:S(2)}, u32[]{:S(2)}) %all-to-all-start) | async-done | bytes 65568 | tf_op jit(solution)/shard_map/cross/all_to_all | solution.py:232
  27.1 19.2 %all_to_all.10.mine_ref = bf16[8,16,2048]{2,1,0:T(8,128)(2,1)S(1)} all-to-all(bf16[8,16,2048]{2,1,0:T(8,128)(2,1)S(1)} %broadcast_in_dim.15), channel_id=1, replica_groups={{0,4,8,12,16,20,24,28},{2,6,10,14,18,22,26,30},{32,36,40,44,48,52,56,60..., dimensions={0} | all-to-all | bytes 1048576 | tf_op jit(solution)/shard_map/near/all_to_all | solution.py:239
  46.2 0.0 copy-start.3
  46.2 2.0 %collective-permute-start = (bf16[8,16,2048]{2,1,0:T(8,128)(2,1)S(1)}, bf16[8,16,2048]{2,1,0:T(8,128)(2,1)S(1)}, u32[]{:S(2)}, u32[]{:S(2)}) collective-permute-start(bf16[8,16,2048]{2,1,0:T(8,128)(2,1)S(1)} %all_to_all.10.mine_ref), channel_id=1, source_target_pairs={{0,1},{1,0},{2,3},{3,2},{4,5},{5,4},{6,7},{7,6},{8,9},{9,8},{10,11... | collective-permute-start | bytes 1572872 | tf_op jit(solution)/shard_map/near/ppermute | solution.py:240
  48.3 1.9 %collective-permute-done.theirs_ref = bf16[8,16,2048]{2,1,0:T(8,128)(2,1)S(1)} collective-permute-done((bf16[8,16,2048]{2,1,0:T(8,128)(2,1)S(1)}, bf16[8,16,2048]{2,1,0:T(8,128)(2,1)S(1)}, u32[]{:S(2)}, u32[]{:S(2)}) %collective-permute-start) | collective-permute-done | bytes 524320 | tf_op jit(solution)/shard_map/near/ppermute | solution.py:240
  50.2 0.7 sort.1
  50.8 9.7 %collective-permute-start.1 = (bf16[2,64,2048]{2,1,0:T(8,128)(2,1)S(1)}, bf16[2,64,2048]{2,1,0:T(8,128)(2,1)S(1)}, u32[]{:S(2)}, u32[]{:S(2)}) collective-permute-start(bf16[2,64,2048]{2,1,0:T(8,128)(2,1)S(1)} %get-tuple-element.32), channel_id=1, source_target_pairs={{0,128},{128,256},{256,384},{384,512},{512,640},{640,768},{768,896... | collective-permute-start | bytes 1572872 | tf_op jit(solution)/shard_map/ring/ppermute | solution.py:248
  60.6 1.9 %collective-permute-start.7 = (bf16[2,64,2048]{2,1,0:T(8,128)(2,1)S(1)}, bf16[2,64,2048]{2,1,0:T(8,128)(2,1)S(1)}, u32[]{:S(2)}, u32[]{:S(2)}) collective-permute-start(bf16[2,64,2048]{2,1,0:T(8,128)(2,1)S(1)} %get-tuple-element.36), channel_id=1, source_target_pairs={{0,4},{4,8},{8,12},{12,16},{16,20},{20,24},{24,28},{28,0},{1,29},{... | collective-permute-start | bytes 1572872 | tf_op jit(solution)/shard_map/ring/ppermute | solution.py:248
  62.5 0.0 copy-done.3
  62.5 2.5 %collective-permute-start.3 = (bf16[128,4096]{1,0:T(8,128)(2,1)S(1)}, bf16[128,4096]{1,0:T(8,128)(2,1)S(1)}, u32[]{:S(2)}, u32[]{:S(2)}) collective-permute-start(bf16[128,4096]{1,0:T(8,128)(2,1)S(1)} %copy-done.3), channel_id=1, source_target_pairs={{0,2},{1,3},{2,0},{3,1},{4,6},{5,7},{6,4},{7,5},{8,10},{9,11},{10,... | collective-permute-start | bytes 3145736 | tf_op jit(solution)/shard_map/pool_x/ppermute | solution.py:244
  65.1 1.6 %collective-permute-done.1.left_ref = bf16[2,64,2048]{2,1,0:T(8,128)(2,1)S(1)} collective-permute-done((bf16[2,64,2048]{2,1,0:T(8,128)(2,1)S(1)}, bf16[2,64,2048]{2,1,0:T(8,128)(2,1)S(1)}, u32[]{:S(2)}, u32[]{:S(2)}) %collective-permute-start.1) | collective-permute-done | bytes 524320 | tf_op jit(solution)/shard_map/ring/ppermute | solution.py:248
  66.7 5.3 %collective-permute-start.5 = (bf16[2,64,2048]{2,1,0:T(8,128)(2,1)S(1)}, bf16[2,64,2048]{2,1,0:T(8,128)(2,1)S(1)}, u32[]{:S(2)}, u32[]{:S(2)}) collective-permute-start(bf16[2,64,2048]{2,1,0:T(8,128)(2,1)S(1)} %collective-permute-done.1.left_ref), channel_id=1, source_target_pairs={{0,128},{128,256},{256,384},{384,512},{512,640},{640,768},{768,896... | collective-permute-start | bytes 1572872 | tf_op jit(solution)/shard_map/ring/ppermute | solution.py:248
  72.0 0.0 collective-permute-done.7.right_ref
  72.0 1.9 %collective-permute-start.8 = (bf16[2,64,2048]{2,1,0:T(8,128)(2,1)S(1)}, bf16[2,64,2048]{2,1,0:T(8,128)(2,1)S(1)}, u32[]{:S(2)}, u32[]{:S(2)}) collective-permute-start(bf16[2,64,2048]{2,1,0:T(8,128)(2,1)S(1)} %collective-permute-done.7.right_ref), channel_id=1, source_target_pairs={{0,4},{4,8},{8,12},{12,16},{16,20},{20,24},{24,28},{28,0},{1,29},{... | collective-permute-start | bytes 1572872 | tf_op jit(solution)/shard_map/ring/ppermute | solution.py:248
  73.9 0.1 hand.3
  74.0 1.9 %collective-permute-start.10 = (bf16[2,64,2048]{2,1,0:T(8,128)(2,1)S(1)}, bf16[2,64,2048]{2,1,0:T(8,128)(2,1)S(1)}, u32[]{:S(2)}, u32[]{:S(2)}) collective-permute-start(bf16[2,64,2048]{2,1,0:T(8,128)(2,1)S(1)} %get-tuple-element.40), channel_id=1, source_target_pairs={{0,1},{1,0},{2,3},{3,2},{4,5},{5,4},{6,7},{7,6},{8,9},{9,8},{10,11... | collective-permute-start | bytes 1572872 | tf_op jit(solution)/shard_map/ring/ppermute | solution.py:255
  75.9 2.2 %collective-permute-done.5.left_ref = bf16[2,64,2048]{2,1,0:T(8,128)(2,1)S(1)} collective-permute-done((bf16[2,64,2048]{2,1,0:T(8,128)(2,1)S(1)}, bf16[2,64,2048]{2,1,0:T(8,128)(2,1)S(1)}, u32[]{:S(2)}, u32[]{:S(2)}) %collective-permute-start.5) | collective-permute-done | bytes 524320 | tf_op jit(solution)/shard_map/ring/ppermute | solution.py:248
  78.1 5.3 %collective-permute-start.6 = (bf16[2,64,2048]{2,1,0:T(8,128)(2,1)S(1)}, bf16[2,64,2048]{2,1,0:T(8,128)(2,1)S(1)}, u32[]{:S(2)}, u32[]{:S(2)}) collective-permute-start(bf16[2,64,2048]{2,1,0:T(8,128)(2,1)S(1)} %collective-permute-done.5.left_ref), channel_id=1, source_target_pairs={{0,128},{128,256},{256,384},{384,512},{512,640},{640,768},{768,896... | collective-permute-start | bytes 1572872 | tf_op jit(solution)/shard_map/ring/ppermute | solution.py:248
  83.4 0.0 collective-permute-done.8.right_ref
  83.4 0.1 hand.4
  83.5 1.9 %collective-permute-start.11 = (bf16[2,64,2048]{2,1,0:T(8,128)(2,1)S(1)}, bf16[2,64,2048]{2,1,0:T(8,128)(2,1)S(1)}, u32[]{:S(2)}, u32[]{:S(2)}) collective-permute-start(bf16[2,64,2048]{2,1,0:T(8,128)(2,1)S(1)} %get-tuple-element.43), channel_id=1, source_target_pairs={{0,1},{1,0},{2,3},{3,2},{4,5},{5,4},{6,7},{7,6},{8,9},{9,8},{10,11... | collective-permute-start | bytes 1572872 | tf_op jit(solution)/shard_map/ring/ppermute | solution.py:255
  85.4 1.9 %collective-permute-start.9 = (bf16[2,64,2048]{2,1,0:T(8,128)(2,1)S(1)}, bf16[2,64,2048]{2,1,0:T(8,128)(2,1)S(1)}, u32[]{:S(2)}, u32[]{:S(2)}) collective-permute-start(bf16[2,64,2048]{2,1,0:T(8,128)(2,1)S(1)} %collective-permute-done.8.right_ref), channel_id=1, source_target_pairs={{0,4},{4,8},{8,12},{12,16},{16,20},{20,24},{24,28},{28,0},{1,29},{... | collective-permute-start | bytes 1572872 | tf_op jit(solution)/shard_map/ring/ppermute | solution.py:248
  87.4 0.0 collective-permute-done.3.p2.rest_14_
  87.4 2.4 %collective-permute-start.2 = (bf16[128,4096]{1,0:T(8,128)(2,1)S(1)}, bf16[128,4096]{1,0:T(8,128)(2,1)S(1)}, u32[]{:S(2)}, u32[]{:S(2)}) collective-permute-start(bf16[128,4096]{1,0:T(8,128)(2,1)S(1)} %copy-done.3), channel_id=1, source_target_pairs={{0,1},{1,0},{2,3},{3,2},{4,5},{5,4},{6,7},{7,6},{8,9},{9,8},{10,11... | collective-permute-start | bytes 3145736 | tf_op jit(solution)/shard_map/ring/ppermute | solution.py:251
  89.8 0.0 collective-permute-done.10.rest_3_
  89.8 1.9 %collective-permute-start.4 = (bf16[128,4096]{1,0:T(8,128)(2,1)S(1)}, bf16[128,4096]{1,0:T(8,128)(2,1)S(1)}, u32[]{:S(2)}, u32[]{:S(2)}) collective-permute-start(bf16[128,4096]{1,0:T(8,128)(2,1)S(1)} %collective-permute-done.3.p2.rest_14_), channel_id=1, source_target_pairs={{0,1},{1,0},{2,3},{3,2},{4,5},{5,4},{6,7},{7,6},{8,9},{9,8},{10,11... | collective-permute-start | bytes 3145736 | tf_op jit(solution)/shard_map/other_pools/ppermute | solution.py:258
  91.7 0.0 collective-permute-done.6.left_ref
  91.7 0.0 collective-permute-done.11.rest_6_
  91.8 3.9 %collective-permute-done.9.right_ref = bf16[2,64,2048]{2,1,0:T(8,128)(2,1)S(1)} collective-permute-done((bf16[2,64,2048]{2,1,0:T(8,128)(2,1)S(1)}, bf16[2,64,2048]{2,1,0:T(8,128)(2,1)S(1)}, u32[]{:S(2)}, u32[]{:S(2)}) %collective-permute-start.9) | collective-permute-done | bytes 524320 | tf_op jit(solution)/shard_map/ring/ppermute | solution.py:248
  95.7 0.0 copy-start.1
  95.7 0.1 hand.5
  95.7 4.1 %collective-permute-start.13 = (bf16[1,64,2048]{2,1,0:T(8,128)(2,1)S(1)}, bf16[1,64,2048]{2,1,0:T(8,128)(2,1)S(1)}, u32[]{:S(2)}, u32[]{:S(2)}) collective-permute-start(bf16[1,64,2048]{2,1,0:T(8,128)(2,1)S(1)} %get-tuple-element.53.rest_7_), channel_id=1, source_target_pairs={{0,128},{128,256},{256,384},{384,512},{512,640},{640,768},{768,896... | collective-permute-start | bytes 786440 | tf_op jit(solution)/shard_map/ring/ppermute | solution.py:256
  99.9 2.8 %collective-permute-start.14 = (bf16[1,64,2048]{2,1,0:T(8,128)(2,1)S(1)}, bf16[1,64,2048]{2,1,0:T(8,128)(2,1)S(1)}, u32[]{:S(2)}, u32[]{:S(2)}) collective-permute-start(bf16[1,64,2048]{2,1,0:T(8,128)(2,1)S(1)} %get-tuple-element.54.rest_8_), channel_id=1, source_target_pairs={{0,4},{4,8},{8,12},{12,16},{16,20},{20,24},{24,28},{28,0},{1,29},{... | collective-permute-start | bytes 786440 | tf_op jit(solution)/shard_map/ring/ppermute | solution.py:256
  102.7 1.9 %collective-permute-start.12 = (bf16[2,64,2048]{2,1,0:T(8,128)(2,1)S(1)}, bf16[2,64,2048]{2,1,0:T(8,128)(2,1)S(1)}, u32[]{:S(2)}, u32[]{:S(2)}) collective-permute-start(bf16[2,64,2048]{2,1,0:T(8,128)(2,1)S(1)} %get-tuple-element.55), channel_id=1, source_target_pairs={{0,1},{1,0},{2,3},{3,2},{4,5},{5,4},{6,7},{7,6},{8,9},{9,8},{10,11... | collective-permute-start | bytes 1572872 | tf_op jit(solution)/shard_map/ring/ppermute | solution.py:255
  104.6 0.0 collective-permute-done.2.p1.rest_13_
  104.7 0.0 collective-permute-done.4.p3.rest_15_
  104.7 0.0 copy-done.1
  104.7 1.0 hard_rest.1.hard_ref
  105.7 0.0 copy-start.4
  105.7 0.0 collective-permute-done.13.rest_10_
  105.8 1.5 %collective-permute-done.14.rest_11_ = bf16[1,64,2048]{2,1,0:T(8,128)(2,1)S(1)} collective-permute-done((bf16[1,64,2048]{2,1,0:T(8,128)(2,1)S(1)}, bf16[1,64,2048]{2,1,0:T(8,128)(2,1)S(1)}, u32[]{:S(2)}, u32[]{:S(2)}) %collective-permute-start.14) | collective-permute-done | bytes 262176 | tf_op jit(solution)/shard_map/ring/ppermute | solution.py:256
  107.3 0.0 collective-permute-done.12.rest_9_
  107.3 0.0 copy-done.4
  107.3 5.0 %tail.1 = (bf16[128,4096]{1,0:T(8,128)(2,1)}, f32[1,128]{1,0:T(1,128)}) custom-call(s32[4]{0:T(128)S(1)} %pad_add_fusion.place_ref, s32[1,128]{1,0:T(1,128)S(1)} %bitcast.14, f32[128,512]{1,0:T(8,128)S(1)} %hard_rest.1.hard_ref, bf16[128,4096]{1,0:T(8,128)(2,1)S(1)} %copy-done.1, bf16[2,64,2048]{2,1,0:T(8,128)(2,1)S(1)} %get-tuple-element.44.rest_0_, ...), custom_call_target="tpu_custom_call" | custom-call | flops 2147483648 | bytes 12582912 | tf_op jit(solution)/shard_map/tail/pallas_call | solution.py:208
  (4 shorter events, 0.1 us)
Async XLA Ops:
  2.1 24.9 %all-to-all-start = ((bf16[8,2,2048]{2,1,0:T(2,128)(2,1)}), bf16[8,2,2048]{2,1,0:T(2,128)(2,1)S(1)}, u32[]{:S(2)}, u32[]{:S(2)}) async-start(bf16[8,2,2048]{2,1,0:T(2,128)(2,1)} %bitcast.6), calls=%async_computation | async-start | bytes 131072 | tf_op jit(solution)/shard_map/cross/all_to_all | solution.py:232
  19.5 0.7 copy-start.5
  19.5 0.7 copy-start.6
  19.5 0.7 copy-start.7
  20.2 1.2 %copy-start = (bf16[128,4096]{1,0:T(8,128)(2,1)S(1)}, bf16[128,4096]{1,0:T(8,128)(2,1)}, u32[]{:S(2)}) copy-start(bf16[128,4096]{1,0:T(8,128)(2,1)} %q_ref.5) | copy-start | bytes 3145732
  21.5 1.2 %copy-start.2 = (bf16[128,4096]{1,0:T(8,128)(2,1)S(1)}, bf16[128,4096]{1,0:T(8,128)(2,1)}, u32[]{:S(2)}) copy-start(bf16[128,4096]{1,0:T(8,128)(2,1)} %rest_12_) | copy-start | bytes 3145732
  46.2 16.3 %copy-start.3 = (bf16[128,4096]{1,0:T(8,128)(2,1)S(1)}, bf16[128,4096]{1,0:T(8,128)(2,1)}, u32[]{:S(2)}) copy-start(bf16[128,4096]{1,0:T(8,128)(2,1)} %rest_12_) | copy-start | bytes 3145732
  46.2 3.9 %collective-permute-start = (bf16[8,16,2048]{2,1,0:T(8,128)(2,1)S(1)}, bf16[8,16,2048]{2,1,0:T(8,128)(2,1)S(1)}, u32[]{:S(2)}, u32[]{:S(2)}) collective-permute-start(bf16[8,16,2048]{2,1,0:T(8,128)(2,1)S(1)} %all_to_all.10.mine_ref), channel_id=1, source_target_pairs={{0,1},{1,0},{2,3},{3,2},{4,5},{5,4},{6,7},{7,6},{8,9},{9,8},{10,11... | collective-permute-start | bytes 1572872 | tf_op jit(solution)/shard_map/near/ppermute | solution.py:240
  50.8 15.9 %collective-permute-start.1 = (bf16[2,64,2048]{2,1,0:T(8,128)(2,1)S(1)}, bf16[2,64,2048]{2,1,0:T(8,128)(2,1)S(1)}, u32[]{:S(2)}, u32[]{:S(2)}) collective-permute-start(bf16[2,64,2048]{2,1,0:T(8,128)(2,1)S(1)} %get-tuple-element.32), channel_id=1, source_target_pairs={{0,128},{128,256},{256,384},{384,512},{512,640},{640,768},{768,896... | collective-permute-start | bytes 1572872 | tf_op jit(solution)/shard_map/ring/ppermute | solution.py:248
  60.6 11.4 %collective-permute-start.7 = (bf16[2,64,2048]{2,1,0:T(8,128)(2,1)S(1)}, bf16[2,64,2048]{2,1,0:T(8,128)(2,1)S(1)}, u32[]{:S(2)}, u32[]{:S(2)}) collective-permute-start(bf16[2,64,2048]{2,1,0:T(8,128)(2,1)S(1)} %get-tuple-element.36), channel_id=1, source_target_pairs={{0,4},{4,8},{8,12},{12,16},{16,20},{20,24},{24,28},{28,0},{1,29},{... | collective-permute-start | bytes 1572872 | tf_op jit(solution)/shard_map/ring/ppermute | solution.py:248
  62.5 24.8 %collective-permute-start.3 = (bf16[128,4096]{1,0:T(8,128)(2,1)S(1)}, bf16[128,4096]{1,0:T(8,128)(2,1)S(1)}, u32[]{:S(2)}, u32[]{:S(2)}) collective-permute-start(bf16[128,4096]{1,0:T(8,128)(2,1)S(1)} %copy-done.3), channel_id=1, source_target_pairs={{0,2},{1,3},{2,0},{3,1},{4,6},{5,7},{6,4},{7,5},{8,10},{9,11},{10,... | collective-permute-start | bytes 3145736 | tf_op jit(solution)/shard_map/pool_x/ppermute | solution.py:244
  66.7 11.4 %collective-permute-start.5 = (bf16[2,64,2048]{2,1,0:T(8,128)(2,1)S(1)}, bf16[2,64,2048]{2,1,0:T(8,128)(2,1)S(1)}, u32[]{:S(2)}, u32[]{:S(2)}) collective-permute-start(bf16[2,64,2048]{2,1,0:T(8,128)(2,1)S(1)} %collective-permute-done.1.left_ref), channel_id=1, source_target_pairs={{0,128},{128,256},{256,384},{384,512},{512,640},{640,768},{768,896... | collective-permute-start | bytes 1572872 | tf_op jit(solution)/shard_map/ring/ppermute | solution.py:248
  72.0 11.4 %collective-permute-start.8 = (bf16[2,64,2048]{2,1,0:T(8,128)(2,1)S(1)}, bf16[2,64,2048]{2,1,0:T(8,128)(2,1)S(1)}, u32[]{:S(2)}, u32[]{:S(2)}) collective-permute-start(bf16[2,64,2048]{2,1,0:T(8,128)(2,1)S(1)} %collective-permute-done.7.right_ref), channel_id=1, source_target_pairs={{0,4},{4,8},{8,12},{12,16},{16,20},{20,24},{24,28},{28,0},{1,29},{... | collective-permute-start | bytes 1572872 | tf_op jit(solution)/shard_map/ring/ppermute | solution.py:248
  74.0 15.8 %collective-permute-start.10 = (bf16[2,64,2048]{2,1,0:T(8,128)(2,1)S(1)}, bf16[2,64,2048]{2,1,0:T(8,128)(2,1)S(1)}, u32[]{:S(2)}, u32[]{:S(2)}) collective-permute-start(bf16[2,64,2048]{2,1,0:T(8,128)(2,1)S(1)} %get-tuple-element.40), channel_id=1, source_target_pairs={{0,1},{1,0},{2,3},{3,2},{4,5},{5,4},{6,7},{7,6},{8,9},{9,8},{10,11... | collective-permute-start | bytes 1572872 | tf_op jit(solution)/shard_map/ring/ppermute | solution.py:255
  78.1 13.6 %collective-permute-start.6 = (bf16[2,64,2048]{2,1,0:T(8,128)(2,1)S(1)}, bf16[2,64,2048]{2,1,0:T(8,128)(2,1)S(1)}, u32[]{:S(2)}, u32[]{:S(2)}) collective-permute-start(bf16[2,64,2048]{2,1,0:T(8,128)(2,1)S(1)} %collective-permute-done.5.left_ref), channel_id=1, source_target_pairs={{0,128},{128,256},{256,384},{384,512},{512,640},{640,768},{768,896... | collective-permute-start | bytes 1572872 | tf_op jit(solution)/shard_map/ring/ppermute | solution.py:248
  83.5 8.2 %collective-permute-start.11 = (bf16[2,64,2048]{2,1,0:T(8,128)(2,1)S(1)}, bf16[2,64,2048]{2,1,0:T(8,128)(2,1)S(1)}, u32[]{:S(2)}, u32[]{:S(2)}) collective-permute-start(bf16[2,64,2048]{2,1,0:T(8,128)(2,1)S(1)} %get-tuple-element.43), channel_id=1, source_target_pairs={{0,1},{1,0},{2,3},{3,2},{4,5},{5,4},{6,7},{7,6},{8,9},{9,8},{10,11... | collective-permute-start | bytes 1572872 | tf_op jit(solution)/shard_map/ring/ppermute | solution.py:255
  85.4 10.2 %collective-permute-start.9 = (bf16[2,64,2048]{2,1,0:T(8,128)(2,1)S(1)}, bf16[2,64,2048]{2,1,0:T(8,128)(2,1)S(1)}, u32[]{:S(2)}, u32[]{:S(2)}) collective-permute-start(bf16[2,64,2048]{2,1,0:T(8,128)(2,1)S(1)} %collective-permute-done.8.right_ref), channel_id=1, source_target_pairs={{0,4},{4,8},{8,12},{12,16},{16,20},{20,24},{24,28},{28,0},{1,29},{... | collective-permute-start | bytes 1572872 | tf_op jit(solution)/shard_map/ring/ppermute | solution.py:248
  87.4 17.3 %collective-permute-start.2 = (bf16[128,4096]{1,0:T(8,128)(2,1)S(1)}, bf16[128,4096]{1,0:T(8,128)(2,1)S(1)}, u32[]{:S(2)}, u32[]{:S(2)}) collective-permute-start(bf16[128,4096]{1,0:T(8,128)(2,1)S(1)} %copy-done.3), channel_id=1, source_target_pairs={{0,1},{1,0},{2,3},{3,2},{4,5},{5,4},{6,7},{7,6},{8,9},{9,8},{10,11... | collective-permute-start | bytes 3145736 | tf_op jit(solution)/shard_map/ring/ppermute | solution.py:251
  89.8 14.9 %collective-permute-start.4 = (bf16[128,4096]{1,0:T(8,128)(2,1)S(1)}, bf16[128,4096]{1,0:T(8,128)(2,1)S(1)}, u32[]{:S(2)}, u32[]{:S(2)}) collective-permute-start(bf16[128,4096]{1,0:T(8,128)(2,1)S(1)} %collective-permute-done.3.p2.rest_14_), channel_id=1, source_target_pairs={{0,1},{1,0},{2,3},{3,2},{4,5},{5,4},{6,7},{7,6},{8,9},{9,8},{10,11... | collective-permute-start | bytes 3145736 | tf_op jit(solution)/shard_map/other_pools/ppermute | solution.py:258
  95.7 9.0 %copy-start.1 = (bf16[128,4096]{1,0:T(8,128)(2,1)S(1)}, bf16[128,4096]{1,0:T(8,128)(2,1)}, u32[]{:S(2)}) copy-start(bf16[128,4096]{1,0:T(8,128)(2,1)} %q_ref.5) | copy-start | bytes 3145732
  95.7 10.0 %collective-permute-start.13 = (bf16[1,64,2048]{2,1,0:T(8,128)(2,1)S(1)}, bf16[1,64,2048]{2,1,0:T(8,128)(2,1)S(1)}, u32[]{:S(2)}, u32[]{:S(2)}) collective-permute-start(bf16[1,64,2048]{2,1,0:T(8,128)(2,1)S(1)} %get-tuple-element.53.rest_7_), channel_id=1, source_target_pairs={{0,128},{128,256},{256,384},{384,512},{512,640},{640,768},{768,896... | collective-permute-start | bytes 786440 | tf_op jit(solution)/shard_map/ring/ppermute | solution.py:256
  99.9 7.4 %collective-permute-start.14 = (bf16[1,64,2048]{2,1,0:T(8,128)(2,1)S(1)}, bf16[1,64,2048]{2,1,0:T(8,128)(2,1)S(1)}, u32[]{:S(2)}, u32[]{:S(2)}) collective-permute-start(bf16[1,64,2048]{2,1,0:T(8,128)(2,1)S(1)} %get-tuple-element.54.rest_8_), channel_id=1, source_target_pairs={{0,4},{4,8},{8,12},{12,16},{16,20},{20,24},{24,28},{28,0},{1,29},{... | collective-permute-start | bytes 786440 | tf_op jit(solution)/shard_map/ring/ppermute | solution.py:256
  102.7 4.6 %collective-permute-start.12 = (bf16[2,64,2048]{2,1,0:T(8,128)(2,1)S(1)}, bf16[2,64,2048]{2,1,0:T(8,128)(2,1)S(1)}, u32[]{:S(2)}, u32[]{:S(2)}) collective-permute-start(bf16[2,64,2048]{2,1,0:T(8,128)(2,1)S(1)} %get-tuple-element.55), channel_id=1, source_target_pairs={{0,1},{1,0},{2,3},{3,2},{4,5},{5,4},{6,7},{7,6},{8,9},{9,8},{10,11... | collective-permute-start | bytes 1572872 | tf_op jit(solution)/shard_map/ring/ppermute | solution.py:255
  105.7 1.6 %copy-start.4 = (s32[128]{0:T(128)S(1)}, s32[128]{0:T(128)}, u32[]{:S(2)}) copy-start(s32[128]{0:T(128)} %param.10) | copy-start | bytes 1540

commit v6 on v5

--- a/solution.py
+++ b/solution.py
@@ -36,7 +36,7 @@
     return lax.dot_general(a, b, (((1,), (1,)), ((), ())), preferred_element_type=jnp.float32)
 
 
-def hard_kernel(place_ref, refs_ref, count_ref, list_ref, q_ref, pool, out_ref):
+def mask_kernel(place_ref, refs_ref, count_ref, list_ref, out_ref):
     most, rows = refs_ref.shape
     owners, slots = list_ref.shape
     span = owners * slots
@@ -55,16 +55,20 @@
     for i in range(4):
         match = jnp.where(same & (owner == (own ^ i)), 1.0, 0.0).astype(jnp.bfloat16)
         used = lax.dot_general(present, match, (((0,), (1,)), ((), ())), preferred_element_type=jnp.float32)
-        value = 0.0 if i else dots(q_ref[...], pool[...])
-        out_ref[:, i * span : (i + 1) * span] = jnp.where(used > 0, value, -jnp.inf)
-
-
-def hard_rest_kernel(hard_ref, q_ref, p1, p2, p3, out_ref):
-    span = p1.shape[0]
-    out_ref[:, :span] = hard_ref[:, :span]
-    for i, pool in ((1, p1), (2, p2), (3, p3)):
+        out_ref[:, i * span : (i + 1) * span] = jnp.where(used > 0, 0.0, -jnp.inf)
+
+
+def hard_kernel(mask_ref, q_ref, p0, p1, p2, p3, out_ref):
+    span = p0.shape[0]
+    for i, pool in enumerate((p0, p1, p2, p3)):
         at = slice(i * span, (i + 1) * span)
-        out_ref[:, at] = hard_ref[:, at] + dots(q_ref[...], pool[...])
+        out_ref[:, at] = mask_ref[:, at] + dots(q_ref[...], pool[...])
+
+
+def copies_kernel(x_ref, out_ref):
+    half = out_ref.shape[2]
+    for i in range(out_ref.shape[0]):
+        out_ref[i] = x_ref[:, (i % 2) * half : (i % 2 + 1) * half]
 
 
 def passage(shape, dim, place, ring_is_z):
@@ -114,7 +118,8 @@
 
 
 def tail_kernel(place_ref, pos_ref, hard_ref, q_ref, *rest):
-    blocks, (p0, p1, p2, p3), (grad_ref, loss_ref, left_ref, right_ref) = rest[:12], rest[12:16], rest[16:]
+    blocks, (p0, p1, p2, p3), (grad_ref, loss_ref, left_ref, right_ref) = rest[:12], rest[12:16], rest[16:20]
+    out_ref, sems = rest[20:]
     keep, l1, r1, e1, l2, r2, e2, l3, r3, e3, l4, r4 = blocks
     half = left_ref.shape[1]
     total = left_ref.shape[0]
@@ -154,13 +159,19 @@
     hard_weights = (hard_exp / denominator).astype(jnp.bfloat16)
     right_weights = dots(weights, order).astype(jnp.bfloat16)
 
+    copies = []
     for start, w, rows_ref in ((0, weights, left_ref), (half, right_weights, right_ref)):
         all_weights = jnp.concatenate([w, hard_weights], axis=1)
         for chunk in range(0, half, 512):
             at = slice(start + chunk, start + chunk + 512)
             all_rows = [rows_ref[:, chunk : chunk + 512]] + [pool[:, at] for pool in (p0, p1, p2, p3)]
             grad = jnp.dot(all_weights, jnp.concatenate(all_rows, axis=0), preferred_element_type=jnp.float32)
-            grad_ref[:, at] = grad.astype(jnp.bfloat16)
+            out_ref[:, at] = grad.astype(jnp.bfloat16)
+            copy = pltpu.make_async_copy(out_ref.at[:, at], grad_ref.at[:, at], sems.at[len(copies)])
+            copy.start()
+            copies.append(copy)
+    for copy in copies:
+        copy.wait()
 
 
 VMEM = functools.partial(pl.BlockSpec, memory_space=pltpu.VMEM)
@@ -179,16 +190,21 @@
     )(*args)
 
 
-def hard_call(place, refs, count, lists, queries, pool):
-    rows = queries.shape[0]
+def mask_call(place, refs, count, lists):
+    rows = refs.shape[0]
     out = jax.ShapeDtypeStruct((rows, 4 * lists.size), jnp.float32)
-    args = (place, refs.T, count.reshape(1, rows), lists[0], queries, pool)
-    return small_call(hard_kernel, out, args, "hard", scalars=1)
-
-
-def hard_rest_call(hard, queries, pools):
-    out = jax.ShapeDtypeStruct(hard.shape, hard.dtype)
-    return small_call(hard_rest_kernel, out, (hard, queries, *pools), "hard_rest")
+    return small_call(mask_kernel, out, (place, refs.T, count.reshape(1, rows), lists[0]), "mask", scalars=1)
+
+
+def hard_call(mask, queries, pools):
+    out = jax.ShapeDtypeStruct(mask.shape, mask.dtype)
+    return small_call(hard_kernel, out, (mask, queries, *pools), "hard")
+
+
+def copies_call(passages):
+    rows, width = passages.shape
+    out = jax.ShapeDtypeStruct((8, rows, width // 2), passages.dtype)
+    return small_call(copies_kernel, out, (passages,), "copies", flops=2**20)
 
 
 def sort_call(place, mine, theirs):
@@ -212,8 +228,13 @@
             jax.ShapeDtypeStruct((1, rows), jnp.float32),
         ),
         in_specs=[SMEM()] + [VMEM()] * (3 + len(blocks) + len(pools)),
-        out_specs=(VMEM(), VMEM()),
-        scratch_shapes=[pltpu.VMEM((8 * BLOCK, half), jnp.bfloat16), pltpu.VMEM((8 * BLOCK, half), jnp.bfloat16)],
+        out_specs=(pl.BlockSpec(memory_space=pl.ANY), VMEM()),
+        scratch_shapes=[
+            pltpu.VMEM((8 * BLOCK, half), jnp.bfloat16),
+            pltpu.VMEM((8 * BLOCK, half), jnp.bfloat16),
+            pltpu.VMEM((rows, width), jnp.bfloat16),
+            pltpu.SemaphoreType.DMA((8,)),
+        ],
         compiler_params=pltpu.CompilerParams(vmem_limit_bytes=16 * 2**20),
         cost_estimate=pl.CostEstimate(flops=2**31, bytes_accessed=12 * 2**20, transcendentals=2**17),
         name="tail",
@@ -227,12 +248,10 @@
     place = jnp.stack([device >> 7, (device >> 2) & 7, core, device & 3]).astype(jnp.int32)
 
     with jax.named_scope("cross"):
-        halves = passages.reshape(2, 2, half).transpose(1, 0, 2)
-        sent = jnp.broadcast_to(halves[None], (4, 2, 2, half)).reshape(8, 2, half)
-        got = lax.all_to_all(sent, "d", 0, 0, axis_index_groups=CROSS, tiled=True)
-    with jax.named_scope("own_pool"):
-        hard = hard_call(place, hard_refs, hard_count, request_lists, queries, pool)
-    got, hard = lax.optimization_barrier((got, hard))
+        got = lax.all_to_all(copies_call(passages), "d", 0, 0, axis_index_groups=CROSS, tiled=True)
+    with jax.named_scope("used"):
+        mask = mask_call(place, hard_refs, hard_count, request_lists)
+    got, mask = lax.optimization_barrier((got, mask))
     with jax.named_scope("near"):
         got = got.reshape(4, 2, 2, half).transpose(1, 0, 2, 3).reshape(1, 16, half)
         sent = jnp.broadcast_to(got, (8, 16, half))
@@ -244,20 +263,26 @@
         pool_x = lax.ppermute(pool, "d", OTHER_CHIP)
     with jax.named_scope("ring"):
         blocks = [keep]
+        left, right = lax.ppermute(left, "d", RING_Z), lax.ppermute(right, "d", RING_Y)
         for step in range(3):
-            left, right = lax.ppermute(left, "d", RING_Z), lax.ppermute(right, "d", RING_Y)
             if step == 0:
                 left, pool = lax.optimization_barrier((left, pool))
-                pool_c = lax.ppermute(pool, "d", OTHER_CORE)
+            if step == 1:
+                _, pool_x = lax.optimization_barrier((left, pool_x))
             if step == 2:
                 left, right, *blocks = lax.optimization_barrier((left, right, *blocks))
+            else:
+                next_left, next_right = lax.ppermute(left, "d", RING_Z), lax.ppermute(right, "d", RING_Y)
             keep_left, keep_right, give = hand_call(left, right)
+            if step == 2:
+                next_left, next_right = lax.ppermute(keep_left, "d", RING_Z), lax.ppermute(keep_right, "d", RING_Y)
             blocks += [keep_left, keep_right, lax.ppermute(give, "d", OTHER_CORE)]
-        blocks += [lax.ppermute(keep_left, "d", RING_Z), lax.ppermute(keep_right, "d", RING_Y)]
+            left, right = next_left, next_right
+        blocks += [left, right]
     with jax.named_scope("other_pools"):
-        pool_xc = lax.ppermute(pool_x, "d", OTHER_CORE)
+        pool_c, pool_xc = lax.ppermute(pool, "d", OTHER_CORE), lax.ppermute(pool_x, "d", OTHER_CORE)
         pools = (pool, pool_c, pool_x, pool_xc)
-        hard = hard_rest_call(hard, queries, pools[1:])
+        hard = hard_call(mask, queries, pools)
     grad, loss = tail_call(place, positive_ids, hard, queries, blocks, pools)
     return grad, loss.reshape(-1)
 

time: 114 us -> 111 us (0.974)
  local copies, waits for them, and re-layouts: 4.69 us -> 1.7 us
    all_to_all x1, waiting for transfers between devices: 2.98 us -> 5.74 us  [body(): lax.all_to_all(copies_call(passages), 'd', 0, 0, axis_index_groups=CROSS,...]
    ppermute x3, waiting for transfers between devices: 3.91 us -> 1.92 us  [body(): lax.ppermute(right, 'd', RING_Y)]
    unnamed x16 -> x14, local copies, waits for them, and re-layouts: 3.15 us -> 1.58 us
    ppermute x1, waiting for transfers between devices: 1.53 us -> 0.01 us  [body(): lax.ppermute(keep_right, 'd', RING_Y)]
    ppermute x1, starting transfers between devices: 2.84 us -> 4.3 us  [body(): lax.ppermute(keep_right, 'd', RING_Y)]
    ppermute x1, starting transfers between devices: 4.13 us -> 2.8 us  [body(): lax.ppermute(keep_left, 'd', RING_Z)]
    pallas_call x6 -> x7, Pallas kernels: 3.19 us -> 3.82 us  [small_call(): pl.pallas_call(kernel, out_shape=outs, in_specs=[SMEM()] * scalars + [VME...]
where the time goes in v6:
time: 111 us; the launch traced here: 110 us
  starting transfers between devices  65.3 us (59%)
  blocking collectives  19.2 us (17%)
  waiting for transfers between devices  13.8 us (12%)
  Pallas kernels  9.1 us (8%)
  local copies, waits for them, and re-layouts  1.7 us (2%)
    ppermute x3, starting transfers between devices, body(): lax.ppermute(left, 'd', RING_Z)  20.4 us
    all_to_all x1, blocking collectives, body(): near = lax.all_to_all(sent, 'd', 0, 0, axis_index_groups=NEAR, tiled=True)  19.2 us
    all_to_all x1, starting transfers between devices, body(): lax.all_to_all(copies_call(passages), 'd', 0, 0, axis_index_groups=CROSS,...  17.4 us
    ppermute x3, starting transfers between devices, body(): blocks += [keep_left, keep_right, lax.ppermute(give, 'd', OTHER_CORE)]  5.76 us
    ppermute x3, starting transfers between devices, body(): lax.ppermute(right, 'd', RING_Y)  5.76 us
    all_to_all x1, waiting for transfers between devices, body(): lax.all_to_all(copies_call(passages), 'd', 0, 0, axis_index_groups=CROSS,...  5.74 us
    pallas_call x1, Pallas kernels, tail_call(): pl.pallas_call(tail_kernel, out_shape=(jax.ShapeDtypeStruct((rows, width)...  5.28 us
    ppermute x1, starting transfers between devices, body(): lax.ppermute(keep_right, 'd', RING_Y)  4.3 us
  transfers between devices with their start and end apart: 16, of which 6 were waited for; matrix products, arithmetic and copies ran while one was open for 0% of the time, Pallas kernels for 2%

profile of v6, /device:TPU:1, one launch (start us, length us, event | category | flops | bytes accessed | tf_op | source)
XLA Modules:
  0.0 110.0 jit_solution(16491262319295188616)
XLA Ops:
  0.6 0.0 copy-start.2
  0.6 0.7 copy-done.2
  1.3 0.6 copies.1
  2.0 17.4 %all-to-all-start = ((bf16[8,2,2048]{2,1,0:T(2,128)(2,1)}), bf16[8,2,2048]{2,1,0:T(2,128)(2,1)S(1)}, u32[]{:S(2)}, u32[]{:S(2)}) async-start(bf16[8,2,2048]{2,1,0:T(2,128)(2,1)} %copies.1), calls=%async_computation | async-start | bytes 131072 | tf_op jit(solution)/shard_map/cross/all_to_all | solution.py:251
  19.4 0.0 copy-start.4
  19.4 0.1 pad_add_fusion.place_ref
  19.5 0.0 copy-start.5
  19.5 0.0 copy-start.6
  19.5 0.6 copy-done.4
  20.1 0.0 copy-done.5
  20.2 0.0 copy-done.6
  20.2 1.0 mask.1.mask_ref
  21.1 5.7 %all-to-all-done = bf16[8,2,2048]{2,1,0:T(2,128)(2,1)S(1)} async-done(((bf16[8,2,2048]{2,1,0:T(2,128)(2,1)}), bf16[8,2,2048]{2,1,0:T(2,128)(2,1)S(1)}, u32[]{:S(2)}, u32[]{:S(2)}) %all-to-all-start) | async-done | bytes 65568 | tf_op jit(solution)/shard_map/cross/all_to_all | solution.py:251
  27.0 19.2 %all_to_all.10.mine_ref = bf16[8,16,2048]{2,1,0:T(8,128)(2,1)S(1)} all-to-all(bf16[8,16,2048]{2,1,0:T(8,128)(2,1)S(1)} %broadcast_in_dim.8), channel_id=1, replica_groups={{0,4,8,12,16,20,24,28},{2,6,10,14,18,22,26,30},{32,36,40,44,48,52,56,60..., dimensions={0} | all-to-all | bytes 1048576 | tf_op jit(solution)/shard_map/near/all_to_all | solution.py:258
  46.2 0.0 copy-start.1
  46.2 2.0 %collective-permute-start = (bf16[8,16,2048]{2,1,0:T(8,128)(2,1)S(1)}, bf16[8,16,2048]{2,1,0:T(8,128)(2,1)S(1)}, u32[]{:S(2)}, u32[]{:S(2)}) collective-permute-start(bf16[8,16,2048]{2,1,0:T(8,128)(2,1)S(1)} %all_to_all.10.mine_ref), channel_id=1, source_target_pairs={{0,1},{1,0},{2,3},{3,2},{4,5},{5,4},{6,7},{7,6},{8,9},{9,8},{10,11... | collective-permute-start | bytes 1572872 | tf_op jit(solution)/shard_map/near/ppermute | solution.py:259
  48.2 1.9 %collective-permute-done.theirs_ref = bf16[8,16,2048]{2,1,0:T(8,128)(2,1)S(1)} collective-permute-done((bf16[8,16,2048]{2,1,0:T(8,128)(2,1)S(1)}, bf16[8,16,2048]{2,1,0:T(8,128)(2,1)S(1)}, u32[]{:S(2)}, u32[]{:S(2)}) %collective-permute-start) | collective-permute-done | bytes 524320 | tf_op jit(solution)/shard_map/near/ppermute | solution.py:259
  50.1 0.7 sort.1
  50.8 9.7 %collective-permute-start.1 = (bf16[2,64,2048]{2,1,0:T(8,128)(2,1)S(1)}, bf16[2,64,2048]{2,1,0:T(8,128)(2,1)S(1)}, u32[]{:S(2)}, u32[]{:S(2)}) collective-permute-start(bf16[2,64,2048]{2,1,0:T(8,128)(2,1)S(1)} %get-tuple-element.33), channel_id=1, source_target_pairs={{0,128},{128,256},{256,384},{384,512},{512,640},{640,768},{768,896... | collective-permute-start | bytes 1572872 | tf_op jit(solution)/shard_map/ring/ppermute | solution.py:266
  60.5 1.9 %collective-permute-start.7 = (bf16[2,64,2048]{2,1,0:T(8,128)(2,1)S(1)}, bf16[2,64,2048]{2,1,0:T(8,128)(2,1)S(1)}, u32[]{:S(2)}, u32[]{:S(2)}) collective-permute-start(bf16[2,64,2048]{2,1,0:T(8,128)(2,1)S(1)} %get-tuple-element.38), channel_id=1, source_target_pairs={{0,4},{4,8},{8,12},{12,16},{16,20},{20,24},{24,28},{28,0},{1,29},{... | collective-permute-start | bytes 1572872 | tf_op jit(solution)/shard_map/ring/ppermute | solution.py:266
  62.4 0.0 copy-done.1
  62.4 2.5 %collective-permute-start.4 = (bf16[128,4096]{1,0:T(8,128)(2,1)S(1)}, bf16[128,4096]{1,0:T(8,128)(2,1)S(1)}, u32[]{:S(2)}, u32[]{:S(2)}) collective-permute-start(bf16[128,4096]{1,0:T(8,128)(2,1)S(1)} %copy-done.1), channel_id=1, source_target_pairs={{0,2},{1,3},{2,0},{3,1},{4,6},{5,7},{6,4},{7,5},{8,10},{9,11},{10,... | collective-permute-start | bytes 3145736 | tf_op jit(solution)/shard_map/pool_x/ppermute | solution.py:263
  65.0 1.6 %collective-permute-done.1.left_ref = bf16[2,64,2048]{2,1,0:T(8,128)(2,1)S(1)} collective-permute-done((bf16[2,64,2048]{2,1,0:T(8,128)(2,1)S(1)}, bf16[2,64,2048]{2,1,0:T(8,128)(2,1)S(1)}, u32[]{:S(2)}, u32[]{:S(2)}) %collective-permute-start.1) | collective-permute-done | bytes 524320 | tf_op jit(solution)/shard_map/ring/ppermute | solution.py:266
  66.6 5.3 %collective-permute-start.3 = (bf16[2,64,2048]{2,1,0:T(8,128)(2,1)S(1)}, bf16[2,64,2048]{2,1,0:T(8,128)(2,1)S(1)}, u32[]{:S(2)}, u32[]{:S(2)}) collective-permute-start(bf16[2,64,2048]{2,1,0:T(8,128)(2,1)S(1)} %collective-permute-done.1.left_ref), channel_id=1, source_target_pairs={{0,128},{128,256},{256,384},{384,512},{512,640},{640,768},{768,896... | collective-permute-start | bytes 1572872 | tf_op jit(solution)/shard_map/ring/ppermute | solution.py:275
  71.9 0.0 collective-permute-done.7.right_ref
  71.9 1.9 %collective-permute-start.8 = (bf16[2,64,2048]{2,1,0:T(8,128)(2,1)S(1)}, bf16[2,64,2048]{2,1,0:T(8,128)(2,1)S(1)}, u32[]{:S(2)}, u32[]{:S(2)}) collective-permute-start(bf16[2,64,2048]{2,1,0:T(8,128)(2,1)S(1)} %collective-permute-done.7.right_ref), channel_id=1, source_target_pairs={{0,4},{4,8},{8,12},{12,16},{16,20},{20,24},{24,28},{28,0},{1,29},{... | collective-permute-start | bytes 1572872 | tf_op jit(solution)/shard_map/ring/ppermute | solution.py:275
  73.9 0.1 hand.3
  73.9 1.9 %collective-permute-start.10 = (bf16[2,64,2048]{2,1,0:T(8,128)(2,1)S(1)}, bf16[2,64,2048]{2,1,0:T(8,128)(2,1)S(1)}, u32[]{:S(2)}, u32[]{:S(2)}) collective-permute-start(bf16[2,64,2048]{2,1,0:T(8,128)(2,1)S(1)} %get-tuple-element.42), channel_id=1, source_target_pairs={{0,1},{1,0},{2,3},{3,2},{4,5},{5,4},{6,7},{7,6},{8,9},{9,8},{10,11... | collective-permute-start | bytes 1572872 | tf_op jit(solution)/shard_map/ring/ppermute | solution.py:279
  75.9 2.2 %collective-permute-done.3.left_ref = bf16[2,64,2048]{2,1,0:T(8,128)(2,1)S(1)} collective-permute-done((bf16[2,64,2048]{2,1,0:T(8,128)(2,1)S(1)}, bf16[2,64,2048]{2,1,0:T(8,128)(2,1)S(1)}, u32[]{:S(2)}, u32[]{:S(2)}) %collective-permute-start.3) | collective-permute-done | bytes 524320 | tf_op jit(solution)/shard_map/ring/ppermute | solution.py:275
  78.0 5.3 %collective-permute-start.6 = (bf16[2,64,2048]{2,1,0:T(8,128)(2,1)S(1)}, bf16[2,64,2048]{2,1,0:T(8,128)(2,1)S(1)}, u32[]{:S(2)}, u32[]{:S(2)}) collective-permute-start(bf16[2,64,2048]{2,1,0:T(8,128)(2,1)S(1)} %collective-permute-done.3.left_ref), channel_id=1, source_target_pairs={{0,128},{128,256},{256,384},{384,512},{512,640},{640,768},{768,896... | collective-permute-start | bytes 1572872 | tf_op jit(solution)/shard_map/ring/ppermute | solution.py:275
  83.3 0.0 collective-permute-done.8.right_ref
  83.4 1.9 %collective-permute-start.9 = (bf16[2,64,2048]{2,1,0:T(8,128)(2,1)S(1)}, bf16[2,64,2048]{2,1,0:T(8,128)(2,1)S(1)}, u32[]{:S(2)}, u32[]{:S(2)}) collective-permute-start(bf16[2,64,2048]{2,1,0:T(8,128)(2,1)S(1)} %collective-permute-done.8.right_ref), channel_id=1, source_target_pairs={{0,4},{4,8},{8,12},{12,16},{16,20},{20,24},{24,28},{28,0},{1,29},{... | collective-permute-start | bytes 1572872 | tf_op jit(solution)/shard_map/ring/ppermute | solution.py:275
  85.3 0.1 hand.4
  85.4 1.9 %collective-permute-start.11 = (bf16[2,64,2048]{2,1,0:T(8,128)(2,1)S(1)}, bf16[2,64,2048]{2,1,0:T(8,128)(2,1)S(1)}, u32[]{:S(2)}, u32[]{:S(2)}) collective-permute-start(bf16[2,64,2048]{2,1,0:T(8,128)(2,1)S(1)} %get-tuple-element.45), channel_id=1, source_target_pairs={{0,1},{1,0},{2,3},{3,2},{4,5},{5,4},{6,7},{7,6},{8,9},{9,8},{10,11... | collective-permute-start | bytes 1572872 | tf_op jit(solution)/shard_map/ring/ppermute | solution.py:279
  87.3 0.0 collective-permute-done.4.p2.rest_14_
  87.3 2.4 %collective-permute-start.2 = (bf16[128,4096]{1,0:T(8,128)(2,1)S(1)}, bf16[128,4096]{1,0:T(8,128)(2,1)S(1)}, u32[]{:S(2)}, u32[]{:S(2)}) collective-permute-start(bf16[128,4096]{1,0:T(8,128)(2,1)S(1)} %copy-done.1), channel_id=1, source_target_pairs={{0,1},{1,0},{2,3},{3,2},{4,5},{5,4},{6,7},{7,6},{8,9},{9,8},{10,11... | collective-permute-start | bytes 3145736 | tf_op jit(solution)/shard_map/other_pools/ppermute | solution.py:283
  89.7 0.0 collective-permute-done.10.rest_3_
  89.7 1.9 %collective-permute-start.5 = (bf16[128,4096]{1,0:T(8,128)(2,1)S(1)}, bf16[128,4096]{1,0:T(8,128)(2,1)S(1)}, u32[]{:S(2)}, u32[]{:S(2)}) collective-permute-start(bf16[128,4096]{1,0:T(8,128)(2,1)S(1)} %collective-permute-done.4.p2.rest_14_), channel_id=1, source_target_pairs={{0,1},{1,0},{2,3},{3,2},{4,5},{5,4},{6,7},{7,6},{8,9},{9,8},{10,11... | collective-permute-start | bytes 3145736 | tf_op jit(solution)/shard_map/other_pools/ppermute | solution.py:283
  91.7 0.0 collective-permute-done.6.left_ref
  91.7 1.9 %collective-permute-done.9.right_ref = bf16[2,64,2048]{2,1,0:T(8,128)(2,1)S(1)} collective-permute-done((bf16[2,64,2048]{2,1,0:T(8,128)(2,1)S(1)}, bf16[2,64,2048]{2,1,0:T(8,128)(2,1)S(1)}, u32[]{:S(2)}, u32[]{:S(2)}) %collective-permute-start.9) | collective-permute-done | bytes 524320 | tf_op jit(solution)/shard_map/ring/ppermute | solution.py:275
  93.6 0.0 collective-permute-done.11.rest_6_
  93.6 0.0 copy-start
  93.6 0.1 hand.5
  93.7 2.8 %collective-permute-start.13 = (bf16[1,64,2048]{2,1,0:T(8,128)(2,1)S(1)}, bf16[1,64,2048]{2,1,0:T(8,128)(2,1)S(1)}, u32[]{:S(2)}, u32[]{:S(2)}) collective-permute-start(bf16[1,64,2048]{2,1,0:T(8,128)(2,1)S(1)} %get-tuple-element.55.rest_7_), channel_id=1, source_target_pairs={{0,128},{128,256},{256,384},{384,512},{512,640},{640,768},{768,896... | collective-permute-start | bytes 786440 | tf_op jit(solution)/shard_map/ring/ppermute | solution.py:278
  96.5 4.3 %collective-permute-start.14 = (bf16[1,64,2048]{2,1,0:T(8,128)(2,1)S(1)}, bf16[1,64,2048]{2,1,0:T(8,128)(2,1)S(1)}, u32[]{:S(2)}, u32[]{:S(2)}) collective-permute-start(bf16[1,64,2048]{2,1,0:T(8,128)(2,1)S(1)} %get-tuple-element.56.rest_8_), channel_id=1, source_target_pairs={{0,4},{4,8},{8,12},{12,16},{16,20},{20,24},{24,28},{28,0},{1,29},{... | collective-permute-start | bytes 786440 | tf_op jit(solution)/shard_map/ring/ppermute | solution.py:278
  100.8 1.9 %collective-permute-start.12 = (bf16[2,64,2048]{2,1,0:T(8,128)(2,1)S(1)}, bf16[2,64,2048]{2,1,0:T(8,128)(2,1)S(1)}, u32[]{:S(2)}, u32[]{:S(2)}) collective-permute-start(bf16[2,64,2048]{2,1,0:T(8,128)(2,1)S(1)} %get-tuple-element.57), channel_id=1, source_target_pairs={{0,1},{1,0},{2,3},{3,2},{4,5},{5,4},{6,7},{7,6},{8,9},{9,8},{10,11... | collective-permute-start | bytes 1572872 | tf_op jit(solution)/shard_map/ring/ppermute | solution.py:279
  102.7 0.0 collective-permute-done.2.p1.rest_13_
  102.7 0.0 collective-permute-done.5.p3.rest_15_
  102.7 0.0 copy-done
  102.7 1.4 %hard.1.hard_ref = f32[128,512]{1,0:T(8,128)S(1)} custom-call(f32[128,512]{1,0:T(8,128)S(1)} %mask.1.mask_ref, bf16[128,4096]{1,0:T(8,128)(2,1)S(1)} %copy-done, bf16[128,4096]{1,0:T(8,128)(2,1)S(1)} %copy-done.1, bf16[128,4096]{1,0:T(8,128)(2,1)S(1)} %collective-permute-done.2.p1.rest_13_, bf16[128,4096]{1,0:T(8,128)(2,1)S(1)} %collective-permute-done.4.p2.rest_14_, ...), custom_call_target="tpu_custom_call" | custom-call | flops 8589934592 | bytes 4194304 | tf_op jit(solution)/shard_map/other_pools/hard/pallas_call | solution.py:182
  104.1 0.0 copy-start.3
  104.1 0.0 collective-permute-done.13.rest_10_
  104.1 0.0 collective-permute-done.14.rest_11_
  104.1 0.5 collective-permute-done.12.rest_9_
  104.6 0.2 copy-done.3
  104.7 5.3 %tail.1 = (bf16[128,4096]{1,0:T(8,128)(2,1)}, f32[1,128]{1,0:T(1,128)}) custom-call(s32[4]{0:T(128)S(1)} %pad_add_fusion.place_ref, s32[1,128]{1,0:T(1,128)S(1)} %bitcast.12, f32[128,512]{1,0:T(8,128)S(1)} %hard.1.hard_ref, bf16[128,4096]{1,0:T(8,128)(2,1)S(1)} %copy-done, bf16[2,64,2048]{2,1,0:T(8,128)(2,1)S(1)} %get-tuple-element.46.rest_0_, ...), custom_call_target="tpu_custom_call" | custom-call | flops 2147483648 | bytes 12582912 | tf_op jit(solution)/shard_map/tail/pallas_call | solution.py:224
  (3 shorter events, 0.1 us)
Async XLA Ops:
  0.6 0.7 copy-start.2
  2.0 24.9 %all-to-all-start = ((bf16[8,2,2048]{2,1,0:T(2,128)(2,1)}), bf16[8,2,2048]{2,1,0:T(2,128)(2,1)S(1)}, u32[]{:S(2)}, u32[]{:S(2)}) async-start(bf16[8,2,2048]{2,1,0:T(2,128)(2,1)} %copies.1), calls=%async_computation | async-start | bytes 131072 | tf_op jit(solution)/shard_map/cross/all_to_all | solution.py:251
  19.4 0.7 copy-start.4
  19.5 0.7 copy-start.5
  19.5 0.7 copy-start.6
  46.2 16.3 %copy-start.1 = (bf16[128,4096]{1,0:T(8,128)(2,1)S(1)}, bf16[128,4096]{1,0:T(8,128)(2,1)}, u32[]{:S(2)}) copy-start(bf16[128,4096]{1,0:T(8,128)(2,1)} %rest_12_) | copy-start | bytes 3145732
  46.2 3.9 %collective-permute-start = (bf16[8,16,2048]{2,1,0:T(8,128)(2,1)S(1)}, bf16[8,16,2048]{2,1,0:T(8,128)(2,1)S(1)}, u32[]{:S(2)}, u32[]{:S(2)}) collective-permute-start(bf16[8,16,2048]{2,1,0:T(8,128)(2,1)S(1)} %all_to_all.10.mine_ref), channel_id=1, source_target_pairs={{0,1},{1,0},{2,3},{3,2},{4,5},{5,4},{6,7},{7,6},{8,9},{9,8},{10,11... | collective-permute-start | bytes 1572872 | tf_op jit(solution)/shard_map/near/ppermute | solution.py:259
  50.8 15.9 %collective-permute-start.1 = (bf16[2,64,2048]{2,1,0:T(8,128)(2,1)S(1)}, bf16[2,64,2048]{2,1,0:T(8,128)(2,1)S(1)}, u32[]{:S(2)}, u32[]{:S(2)}) collective-permute-start(bf16[2,64,2048]{2,1,0:T(8,128)(2,1)S(1)} %get-tuple-element.33), channel_id=1, source_target_pairs={{0,128},{128,256},{256,384},{384,512},{512,640},{640,768},{768,896... | collective-permute-start | bytes 1572872 | tf_op jit(solution)/shard_map/ring/ppermute | solution.py:266
  60.5 11.4 %collective-permute-start.7 = (bf16[2,64,2048]{2,1,0:T(8,128)(2,1)S(1)}, bf16[2,64,2048]{2,1,0:T(8,128)(2,1)S(1)}, u32[]{:S(2)}, u32[]{:S(2)}) collective-permute-start(bf16[2,64,2048]{2,1,0:T(8,128)(2,1)S(1)} %get-tuple-element.38), channel_id=1, source_target_pairs={{0,4},{4,8},{8,12},{12,16},{16,20},{20,24},{24,28},{28,0},{1,29},{... | collective-permute-start | bytes 1572872 | tf_op jit(solution)/shard_map/ring/ppermute | solution.py:266
  62.4 24.8 %collective-permute-start.4 = (bf16[128,4096]{1,0:T(8,128)(2,1)S(1)}, bf16[128,4096]{1,0:T(8,128)(2,1)S(1)}, u32[]{:S(2)}, u32[]{:S(2)}) collective-permute-start(bf16[128,4096]{1,0:T(8,128)(2,1)S(1)} %copy-done.1), channel_id=1, source_target_pairs={{0,2},{1,3},{2,0},{3,1},{4,6},{5,7},{6,4},{7,5},{8,10},{9,11},{10,... | collective-permute-start | bytes 3145736 | tf_op jit(solution)/shard_map/pool_x/ppermute | solution.py:263
  66.6 11.4 %collective-permute-start.3 = (bf16[2,64,2048]{2,1,0:T(8,128)(2,1)S(1)}, bf16[2,64,2048]{2,1,0:T(8,128)(2,1)S(1)}, u32[]{:S(2)}, u32[]{:S(2)}) collective-permute-start(bf16[2,64,2048]{2,1,0:T(8,128)(2,1)S(1)} %collective-permute-done.1.left_ref), channel_id=1, source_target_pairs={{0,128},{128,256},{256,384},{384,512},{512,640},{640,768},{768,896... | collective-permute-start | bytes 1572872 | tf_op jit(solution)/shard_map/ring/ppermute | solution.py:275
  71.9 11.4 %collective-permute-start.8 = (bf16[2,64,2048]{2,1,0:T(8,128)(2,1)S(1)}, bf16[2,64,2048]{2,1,0:T(8,128)(2,1)S(1)}, u32[]{:S(2)}, u32[]{:S(2)}) collective-permute-start(bf16[2,64,2048]{2,1,0:T(8,128)(2,1)S(1)} %collective-permute-done.7.right_ref), channel_id=1, source_target_pairs={{0,4},{4,8},{8,12},{12,16},{16,20},{20,24},{24,28},{28,0},{1,29},{... | collective-permute-start | bytes 1572872 | tf_op jit(solution)/shard_map/ring/ppermute | solution.py:275
  73.9 15.8 %collective-permute-start.10 = (bf16[2,64,2048]{2,1,0:T(8,128)(2,1)S(1)}, bf16[2,64,2048]{2,1,0:T(8,128)(2,1)S(1)}, u32[]{:S(2)}, u32[]{:S(2)}) collective-permute-start(bf16[2,64,2048]{2,1,0:T(8,128)(2,1)S(1)} %get-tuple-element.42), channel_id=1, source_target_pairs={{0,1},{1,0},{2,3},{3,2},{4,5},{5,4},{6,7},{7,6},{8,9},{9,8},{10,11... | collective-permute-start | bytes 1572872 | tf_op jit(solution)/shard_map/ring/ppermute | solution.py:279
  78.0 13.6 %collective-permute-start.6 = (bf16[2,64,2048]{2,1,0:T(8,128)(2,1)S(1)}, bf16[2,64,2048]{2,1,0:T(8,128)(2,1)S(1)}, u32[]{:S(2)}, u32[]{:S(2)}) collective-permute-start(bf16[2,64,2048]{2,1,0:T(8,128)(2,1)S(1)} %collective-permute-done.3.left_ref), channel_id=1, source_target_pairs={{0,128},{128,256},{256,384},{384,512},{512,640},{640,768},{768,896... | collective-permute-start | bytes 1572872 | tf_op jit(solution)/shard_map/ring/ppermute | solution.py:275
  83.4 10.2 %collective-permute-start.9 = (bf16[2,64,2048]{2,1,0:T(8,128)(2,1)S(1)}, bf16[2,64,2048]{2,1,0:T(8,128)(2,1)S(1)}, u32[]{:S(2)}, u32[]{:S(2)}) collective-permute-start(bf16[2,64,2048]{2,1,0:T(8,128)(2,1)S(1)} %collective-permute-done.8.right_ref), channel_id=1, source_target_pairs={{0,4},{4,8},{8,12},{12,16},{16,20},{20,24},{24,28},{28,0},{1,29},{... | collective-permute-start | bytes 1572872 | tf_op jit(solution)/shard_map/ring/ppermute | solution.py:275
  85.4 8.2 %collective-permute-start.11 = (bf16[2,64,2048]{2,1,0:T(8,128)(2,1)S(1)}, bf16[2,64,2048]{2,1,0:T(8,128)(2,1)S(1)}, u32[]{:S(2)}, u32[]{:S(2)}) collective-permute-start(bf16[2,64,2048]{2,1,0:T(8,128)(2,1)S(1)} %get-tuple-element.45), channel_id=1, source_target_pairs={{0,1},{1,0},{2,3},{3,2},{4,5},{5,4},{6,7},{7,6},{8,9},{9,8},{10,11... | collective-permute-start | bytes 1572872 | tf_op jit(solution)/shard_map/ring/ppermute | solution.py:279
  87.3 15.4 %collective-permute-start.2 = (bf16[128,4096]{1,0:T(8,128)(2,1)S(1)}, bf16[128,4096]{1,0:T(8,128)(2,1)S(1)}, u32[]{:S(2)}, u32[]{:S(2)}) collective-permute-start(bf16[128,4096]{1,0:T(8,128)(2,1)S(1)} %copy-done.1), channel_id=1, source_target_pairs={{0,1},{1,0},{2,3},{3,2},{4,5},{5,4},{6,7},{7,6},{8,9},{9,8},{10,11... | collective-permute-start | bytes 3145736 | tf_op jit(solution)/shard_map/other_pools/ppermute | solution.py:283
  89.7 13.0 %collective-permute-start.5 = (bf16[128,4096]{1,0:T(8,128)(2,1)S(1)}, bf16[128,4096]{1,0:T(8,128)(2,1)S(1)}, u32[]{:S(2)}, u32[]{:S(2)}) collective-permute-start(bf16[128,4096]{1,0:T(8,128)(2,1)S(1)} %collective-permute-done.4.p2.rest_14_), channel_id=1, source_target_pairs={{0,1},{1,0},{2,3},{3,2},{4,5},{5,4},{6,7},{7,6},{8,9},{9,8},{10,11... | collective-permute-start | bytes 3145736 | tf_op jit(solution)/shard_map/other_pools/ppermute | solution.py:283
  93.6 9.1 %copy-start = (bf16[128,4096]{1,0:T(8,128)(2,1)S(1)}, bf16[128,4096]{1,0:T(8,128)(2,1)}, u32[]{:S(2)}) copy-start(bf16[128,4096]{1,0:T(8,128)(2,1)} %q_ref.3) | copy-start | bytes 3145732
  93.7 10.4 %collective-permute-start.13 = (bf16[1,64,2048]{2,1,0:T(8,128)(2,1)S(1)}, bf16[1,64,2048]{2,1,0:T(8,128)(2,1)S(1)}, u32[]{:S(2)}, u32[]{:S(2)}) collective-permute-start(bf16[1,64,2048]{2,1,0:T(8,128)(2,1)S(1)} %get-tuple-element.55.rest_7_), channel_id=1, source_target_pairs={{0,128},{128,256},{256,384},{384,512},{512,640},{640,768},{768,896... | collective-permute-start | bytes 786440 | tf_op jit(solution)/shard_map/ring/ppermute | solution.py:278
  96.5 7.7 %collective-permute-start.14 = (bf16[1,64,2048]{2,1,0:T(8,128)(2,1)S(1)}, bf16[1,64,2048]{2,1,0:T(8,128)(2,1)S(1)}, u32[]{:S(2)}, u32[]{:S(2)}) collective-permute-start(bf16[1,64,2048]{2,1,0:T(8,128)(2,1)S(1)} %get-tuple-element.56.rest_8_), channel_id=1, source_target_pairs={{0,4},{4,8},{8,12},{12,16},{16,20},{20,24},{24,28},{28,0},{1,29},{... | collective-permute-start | bytes 786440 | tf_op jit(solution)/shard_map/ring/ppermute | solution.py:278
  100.8 3.8 %collective-permute-start.12 = (bf16[2,64,2048]{2,1,0:T(8,128)(2,1)S(1)}, bf16[2,64,2048]{2,1,0:T(8,128)(2,1)S(1)}, u32[]{:S(2)}, u32[]{:S(2)}) collective-permute-start(bf16[2,64,2048]{2,1,0:T(8,128)(2,1)S(1)} %get-tuple-element.57), channel_id=1, source_target_pairs={{0,1},{1,0},{2,3},{3,2},{4,5},{5,4},{6,7},{7,6},{8,9},{9,8},{10,11... | collective-permute-start | bytes 1572872 | tf_op jit(solution)/shard_map/ring/ppermute | solution.py:279
  104.1 0.7 copy-start.3

commit v7 on v6

--- a/solution.py
+++ b/solution.py
@@ -21,12 +21,14 @@
 NEAR = np.concatenate([ALONG_Y[:, :, :, 0].reshape(-1, 8), ALONG_Z[:, :, :, 1].reshape(-1, 8)]).tolist()
 
 
-def ring(groups):
-    return [(g[i], g[(i + 1 - 2 * (g[i] & 1)) % 8]) for g in groups.reshape(-1, 8) for i in range(8)]
+def ring(groups, far=1):
+    return [(g[i], g[(i + far * (1 - 2 * (g[i] & 1))) % 8]) for g in groups.reshape(-1, 8) for i in range(8)]
 
 
 RING_Z = ring(ALONG_Z)
 RING_Y = ring(ALONG_Y)
+RING_Z2 = ring(ALONG_Z, 2)
+RING_Y2 = ring(ALONG_Y, 2)
 OTHER_CORE = [(i, i ^ 1) for i in range(1024)]
 OTHER_CHIP = [(i, i ^ 2) for i in range(1024)]
 BLOCK = 64
@@ -110,21 +112,26 @@
     keep_ref[1] = right_ref[0]
 
 
-def hand_kernel(left_ref, right_ref, keep_left_ref, keep_right_ref, give_ref):
+def hand_kernel(left_ref, right_ref, *rest):
+    waiting, (keep_left_ref, keep_right_ref, give_ref) = rest[:-3], rest[-3:]
     keep_left_ref[0] = left_ref[0]
     keep_right_ref[0] = right_ref[0]
-    give_ref[0] = left_ref[1]
-    give_ref[1] = right_ref[1]
+    at = 0
+    for part in waiting:
+        give_ref[: part.shape[0]] = part[...]
+        at = part.shape[0]
+    give_ref[at] = left_ref[1]
+    give_ref[at + 1] = right_ref[1]
 
 
 def tail_kernel(place_ref, pos_ref, hard_ref, q_ref, *rest):
-    blocks, (p0, p1, p2, p3), (grad_ref, loss_ref, left_ref, right_ref) = rest[:12], rest[12:16], rest[16:20]
-    out_ref, sems = rest[20:]
-    keep, l1, r1, e1, l2, r2, e2, l3, r3, e3, l4, r4 = blocks
+    blocks, (p0, p1, p2, p3), (grad_ref, loss_ref, left_ref, right_ref) = rest[:11], rest[11:15], rest[15:19]
+    out_ref, sems = rest[19:]
+    keep, l1, r1, e1, l2, r2, l3, r3, e23, l4, r4 = blocks
     half = left_ref.shape[1]
     total = left_ref.shape[0]
-    lefts = (keep.at[0], l1.at[0], e1.at[0], l2.at[0], e2.at[0], l3.at[0], e3.at[0], l4.at[0])
-    rights = (keep.at[1], r1.at[0], e1.at[1], r2.at[0], e2.at[1], r3.at[0], e3.at[1], r4.at[0])
+    lefts = (keep.at[0], l1.at[0], e1.at[0], l2.at[0], e23.at[0], l3.at[0], e23.at[2], l4.at[0])
+    rights = (keep.at[1], r1.at[0], e1.at[1], r2.at[0], e23.at[1], r3.at[0], e23.at[3], r4.at[0])
     for parts, rows_ref in ((lefts, left_ref), (rights, right_ref)):
         for i, part in enumerate(parts):
             rows_ref[i * BLOCK : (i + 1) * BLOCK, :] = part[...]
@@ -198,7 +205,7 @@
 
 def hard_call(mask, queries, pools):
     out = jax.ShapeDtypeStruct(mask.shape, mask.dtype)
-    return small_call(hard_kernel, out, (mask, queries, *pools), "hard")
+    return small_call(hard_kernel, out, (mask, queries, *pools), "hard", flops=2**34)
 
 
 def copies_call(passages):
@@ -212,10 +219,10 @@
     return small_call(sort_kernel, (out, out, out), (place, mine, theirs), "sort", scalars=1)
 
 
-def hand_call(left, right):
-    out = jax.ShapeDtypeStruct(left.shape, left.dtype)
+def hand_call(left, right, *waiting, flops=2**33):
     one = jax.ShapeDtypeStruct((1,) + left.shape[1:], left.dtype)
-    return small_call(hand_kernel, (one, one, out), (left, right), "hand")
+    out = jax.ShapeDtypeStruct((2 + sum(part.shape[0] for part in waiting),) + left.shape[1:], left.dtype)
+    return small_call(hand_kernel, (one, one, out), (left, right, *waiting), "hand", flops=flops)
 
 
 def tail_call(place, positive, hard, queries, blocks, pools):
@@ -264,26 +271,29 @@
     with jax.named_scope("ring"):
         blocks = [keep]
         left, right = lax.ppermute(left, "d", RING_Z), lax.ppermute(right, "d", RING_Y)
+        pool_c = lax.ppermute(pool, "d", OTHER_CORE)
         for step in range(3):
+            waiting = ()
+            if step < 2:
+                next_left, next_right = lax.ppermute(left, "d", RING_Z), lax.ppermute(right, "d", RING_Y)
+            else:
+                left, right, *blocks = lax.optimization_barrier((left, right, *blocks))
+                waiting = (give,)
             if step == 0:
-                left, pool = lax.optimization_barrier((left, pool))
+                left, pool_c = lax.optimization_barrier((left, pool_c))
+            keep_left, keep_right, give = hand_call(left, right, *waiting, flops=2**33 if step < 2 else 2**35)
+            blocks += [keep_left, keep_right]
             if step == 1:
-                _, pool_x = lax.optimization_barrier((left, pool_x))
-            if step == 2:
-                left, right, *blocks = lax.optimization_barrier((left, right, *blocks))
+                _, pool_x = lax.optimization_barrier((give, pool_x))
+                last = [lax.ppermute(keep_left, "d", RING_Z2), lax.ppermute(keep_right, "d", RING_Y2)]
             else:
-                next_left, next_right = lax.ppermute(left, "d", RING_Z), lax.ppermute(right, "d", RING_Y)
-            keep_left, keep_right, give = hand_call(left, right)
-            if step == 2:
-                next_left, next_right = lax.ppermute(keep_left, "d", RING_Z), lax.ppermute(keep_right, "d", RING_Y)
-            blocks += [keep_left, keep_right, lax.ppermute(give, "d", OTHER_CORE)]
+                blocks.append(lax.ppermute(give, "d", OTHER_CORE))
             left, right = next_left, next_right
-        blocks += [left, right]
     with jax.named_scope("other_pools"):
-        pool_c, pool_xc = lax.ppermute(pool, "d", OTHER_CORE), lax.ppermute(pool_x, "d", OTHER_CORE)
+        pool_xc = lax.ppermute(pool_x, "d", OTHER_CORE)
         pools = (pool, pool_c, pool_x, pool_xc)
         hard = hard_call(mask, queries, pools)
-    grad, loss = tail_call(place, positive_ids, hard, queries, blocks, pools)
+    grad, loss = tail_call(place, positive_ids, hard, queries, blocks + last, pools)
     return grad, loss.reshape(-1)
 
 

time: 111 us -> 110 us (level)
    ppermute x7 -> x6, waiting for transfers between devices: 0.47 us -> 3.21 us  [the longest x1 3.2 us: body(): lax.ppermute(keep_right, 'd', RING_Y2)]
    ppermute x3, waiting for transfers between devices: 1.92 us -> 0.01 us  [body(): lax.ppermute(right, 'd', RING_Y)]
    ppermute x1, waiting for transfers between devices: 1.88 us -> 0.01 us  [body(): theirs = lax.ppermute(near, 'd', OTHER_CORE)]
    ppermute x7 -> x6, starting transfers between devices: 17.2 us -> 16.5 us  [the longest x1 5.56 us: body(): lax.ppermute(keep_left, 'd', RING_Z2)]
  transfers between devices with their start and end apart: 16 -> 15, of which waited for: 6 -> 4; matrix products, arithmetic and copies ran while one was open for 0% -> 0% of each run, Pallas kernels for 2% -> 3%
where the time goes in v7:
time: 110 us; the launch traced here: 109 us
  starting transfers between devices  64.3 us (58%)
  blocking collectives  19.2 us (17%)
  waiting for transfers between devices  12.7 us (12%)
  Pallas kernels  9.15 us (8%)
  local copies, waits for them, and re-layouts  2.19 us (2%)
    ppermute x3, starting transfers between devices, body(): lax.ppermute(left, 'd', RING_Z)  20.2 us
    all_to_all x1, blocking collectives, body(): near = lax.all_to_all(sent, 'd', 0, 0, axis_index_groups=NEAR, tiled=True)  19.2 us
    all_to_all x1, starting transfers between devices, body(): lax.all_to_all(copies_call(passages), 'd', 0, 0, axis_index_groups=CROSS,...  17.4 us
    ppermute x3, starting transfers between devices, body(): lax.ppermute(right, 'd', RING_Y)  5.76 us
    all_to_all x1, waiting for transfers between devices, body(): lax.all_to_all(copies_call(passages), 'd', 0, 0, axis_index_groups=CROSS,...  5.72 us
    ppermute x1, starting transfers between devices, body(): lax.ppermute(keep_left, 'd', RING_Z2)  5.56 us
    pallas_call x1, Pallas kernels, tail_call(): pl.pallas_call(tail_kernel, out_shape=(jax.ShapeDtypeStruct((rows, width)...  5.3 us
    ppermute x2, starting transfers between devices, body(): blocks.append(lax.ppermute(give, 'd', OTHER_CORE))  3.97 us
  transfers between devices with their start and end apart: 15, of which 4 were waited for; matrix products, arithmetic and copies ran while one was open for 0% of the time, Pallas kernels for 3%

profile of v7, /device:TPU:1, one launch (start us, length us, event | category | flops | bytes accessed | tf_op | source)
XLA Modules:
  0.0 108.6 jit_solution(13214518420630621067)
XLA Ops:
  0.6 0.0 copy-start.2
  0.6 0.7 copy-done.2
  1.3 0.6 copies.1
  2.0 17.4 %all-to-all-start = ((bf16[8,2,2048]{2,1,0:T(2,128)(2,1)}), bf16[8,2,2048]{2,1,0:T(2,128)(2,1)S(1)}, u32[]{:S(2)}, u32[]{:S(2)}) async-start(bf16[8,2,2048]{2,1,0:T(2,128)(2,1)} %copies.1), calls=%async_computation | async-start | bytes 131072 | tf_op jit(solution)/shard_map/cross/all_to_all | solution.py:258
  19.4 0.0 copy-start.4
  19.4 0.1 pad_add_fusion.place_ref
  19.5 0.0 copy-start.5
  19.5 0.0 copy-start.6
  19.5 0.6 copy-done.4
  20.1 0.0 copy-done.5
  20.2 0.0 copy-done.6
  20.2 1.0 mask.1.mask_ref
  21.1 0.0 copy-start.1
  21.1 5.7 %all-to-all-done = bf16[8,2,2048]{2,1,0:T(2,128)(2,1)S(1)} async-done(((bf16[8,2,2048]{2,1,0:T(2,128)(2,1)}), bf16[8,2,2048]{2,1,0:T(2,128)(2,1)S(1)}, u32[]{:S(2)}, u32[]{:S(2)}) %all-to-all-start) | async-done | bytes 65568 | tf_op jit(solution)/shard_map/cross/all_to_all | solution.py:258
  27.0 19.2 %all_to_all.10.mine_ref = bf16[8,16,2048]{2,1,0:T(8,128)(2,1)S(1)} all-to-all(bf16[8,16,2048]{2,1,0:T(8,128)(2,1)S(1)} %broadcast_in_dim.8), channel_id=1, replica_groups={{0,4,8,12,16,20,24,28},{2,6,10,14,18,22,26,30},{32,36,40,44,48,52,56,60..., dimensions={0} | all-to-all | bytes 1048576 | tf_op jit(solution)/shard_map/near/all_to_all | solution.py:265
  46.2 1.9 %collective-permute-start = (bf16[8,16,2048]{2,1,0:T(8,128)(2,1)S(1)}, bf16[8,16,2048]{2,1,0:T(8,128)(2,1)S(1)}, u32[]{:S(2)}, u32[]{:S(2)}) collective-permute-start(bf16[8,16,2048]{2,1,0:T(8,128)(2,1)S(1)} %all_to_all.10.mine_ref), channel_id=1, source_target_pairs={{0,1},{1,0},{2,3},{3,2},{4,5},{5,4},{6,7},{7,6},{8,9},{9,8},{10,11... | collective-permute-start | bytes 1572872 | tf_op jit(solution)/shard_map/near/ppermute | solution.py:266
  48.1 0.0 copy-done.1
  48.1 2.4 %collective-permute-start.2 = (bf16[128,4096]{1,0:T(8,128)(2,1)S(1)}, bf16[128,4096]{1,0:T(8,128)(2,1)S(1)}, u32[]{:S(2)}, u32[]{:S(2)}) collective-permute-start(bf16[128,4096]{1,0:T(8,128)(2,1)S(1)} %copy-done.1), channel_id=1, source_target_pairs={{0,1},{1,0},{2,3},{3,2},{4,5},{5,4},{6,7},{7,6},{8,9},{9,8},{10,11... | collective-permute-start | bytes 3145736 | tf_op jit(solution)/shard_map/ring/ppermute | solution.py:274
  50.5 0.0 collective-permute-done.theirs_ref
  50.5 0.7 sort.1
  51.2 9.6 %collective-permute-start.1 = (bf16[2,64,2048]{2,1,0:T(8,128)(2,1)S(1)}, bf16[2,64,2048]{2,1,0:T(8,128)(2,1)S(1)}, u32[]{:S(2)}, u32[]{:S(2)}) collective-permute-start(bf16[2,64,2048]{2,1,0:T(8,128)(2,1)S(1)} %get-tuple-element.33), channel_id=1, source_target_pairs={{0,128},{128,256},{256,384},{384,512},{512,640},{640,768},{768,896... | collective-permute-start | bytes 1572872 | tf_op jit(solution)/shard_map/ring/ppermute | solution.py:273
  60.8 1.9 %collective-permute-start.4 = (bf16[2,64,2048]{2,1,0:T(8,128)(2,1)S(1)}, bf16[2,64,2048]{2,1,0:T(8,128)(2,1)S(1)}, u32[]{:S(2)}, u32[]{:S(2)}) collective-permute-start(bf16[2,64,2048]{2,1,0:T(8,128)(2,1)S(1)} %get-tuple-element.35), channel_id=1, source_target_pairs={{0,4},{4,8},{8,12},{12,16},{16,20},{20,24},{24,28},{28,0},{1,29},{... | collective-permute-start | bytes 1572872 | tf_op jit(solution)/shard_map/ring/ppermute | solution.py:273
  62.7 2.5 %collective-permute-start.6 = (bf16[128,4096]{1,0:T(8,128)(2,1)S(1)}, bf16[128,4096]{1,0:T(8,128)(2,1)S(1)}, u32[]{:S(2)}, u32[]{:S(2)}) collective-permute-start(bf16[128,4096]{1,0:T(8,128)(2,1)S(1)} %copy-done.1), channel_id=1, source_target_pairs={{0,2},{1,3},{2,0},{3,1},{4,6},{5,7},{6,4},{7,5},{8,10},{9,11},{10,... | collective-permute-start | bytes 3145736 | tf_op jit(solution)/shard_map/pool_x/ppermute | solution.py:270
  65.3 0.0 collective-permute-done.2.p1.rest_12_
  65.3 1.6 %collective-permute-done.1.left_ref = bf16[2,64,2048]{2,1,0:T(8,128)(2,1)S(1)} collective-permute-done((bf16[2,64,2048]{2,1,0:T(8,128)(2,1)S(1)}, bf16[2,64,2048]{2,1,0:T(8,128)(2,1)S(1)}, u32[]{:S(2)}, u32[]{:S(2)}) %collective-permute-start.1) | collective-permute-done | bytes 524320 | tf_op jit(solution)/shard_map/ring/ppermute | solution.py:273
  66.9 5.3 %collective-permute-start.3 = (bf16[2,64,2048]{2,1,0:T(8,128)(2,1)S(1)}, bf16[2,64,2048]{2,1,0:T(8,128)(2,1)S(1)}, u32[]{:S(2)}, u32[]{:S(2)}) collective-permute-start(bf16[2,64,2048]{2,1,0:T(8,128)(2,1)S(1)} %collective-permute-done.1.left_ref), channel_id=1, source_target_pairs={{0,128},{128,256},{256,384},{384,512},{512,640},{640,768},{768,896... | collective-permute-start | bytes 1572872 | tf_op jit(solution)/shard_map/ring/ppermute | solution.py:278
  72.2 0.0 collective-permute-done.4.right_ref
  72.2 1.9 %collective-permute-start.5 = (bf16[2,64,2048]{2,1,0:T(8,128)(2,1)S(1)}, bf16[2,64,2048]{2,1,0:T(8,128)(2,1)S(1)}, u32[]{:S(2)}, u32[]{:S(2)}) collective-permute-start(bf16[2,64,2048]{2,1,0:T(8,128)(2,1)S(1)} %collective-permute-done.4.right_ref), channel_id=1, source_target_pairs={{0,4},{4,8},{8,12},{12,16},{16,20},{20,24},{24,28},{28,0},{1,29},{... | collective-permute-start | bytes 1572872 | tf_op jit(solution)/shard_map/ring/ppermute | solution.py:278
  74.2 0.1 hand.4
  74.2 1.9 %collective-permute-start.10 = (bf16[2,64,2048]{2,1,0:T(8,128)(2,1)S(1)}, bf16[2,64,2048]{2,1,0:T(8,128)(2,1)S(1)}, u32[]{:S(2)}, u32[]{:S(2)}) collective-permute-start(bf16[2,64,2048]{2,1,0:T(8,128)(2,1)S(1)} %get-tuple-element.42), channel_id=1, source_target_pairs={{0,1},{1,0},{2,3},{3,2},{4,5},{5,4},{6,7},{7,6},{8,9},{9,8},{10,11... | collective-permute-start | bytes 1572872 | tf_op jit(solution)/shard_map/ring/ppermute | solution.py:290
  76.2 2.2 %collective-permute-done.3.left_ref = bf16[2,64,2048]{2,1,0:T(8,128)(2,1)S(1)} collective-permute-done((bf16[2,64,2048]{2,1,0:T(8,128)(2,1)S(1)}, bf16[2,64,2048]{2,1,0:T(8,128)(2,1)S(1)}, u32[]{:S(2)}, u32[]{:S(2)}) %collective-permute-start.3) | collective-permute-done | bytes 524320 | tf_op jit(solution)/shard_map/ring/ppermute | solution.py:278
  78.3 5.3 %collective-permute-start.8 = (bf16[2,64,2048]{2,1,0:T(8,128)(2,1)S(1)}, bf16[2,64,2048]{2,1,0:T(8,128)(2,1)S(1)}, u32[]{:S(2)}, u32[]{:S(2)}) collective-permute-start(bf16[2,64,2048]{2,1,0:T(8,128)(2,1)S(1)} %collective-permute-done.3.left_ref), channel_id=1, source_target_pairs={{0,128},{128,256},{256,384},{384,512},{512,640},{640,768},{768,896... | collective-permute-start | bytes 1572872 | tf_op jit(solution)/shard_map/ring/ppermute | solution.py:278
  83.6 0.0 collective-permute-done.5.right_ref
  83.7 1.9 %collective-permute-start.9 = (bf16[2,64,2048]{2,1,0:T(8,128)(2,1)S(1)}, bf16[2,64,2048]{2,1,0:T(8,128)(2,1)S(1)}, u32[]{:S(2)}, u32[]{:S(2)}) collective-permute-start(bf16[2,64,2048]{2,1,0:T(8,128)(2,1)S(1)} %collective-permute-done.5.right_ref), channel_id=1, source_target_pairs={{0,4},{4,8},{8,12},{12,16},{16,20},{20,24},{24,28},{28,0},{1,29},{... | collective-permute-start | bytes 1572872 | tf_op jit(solution)/shard_map/ring/ppermute | solution.py:278
  85.6 0.1 hand.3
  85.7 0.0 collective-permute-done.6.p2.rest_13_
  85.7 1.9 %collective-permute-start.7 = (bf16[128,4096]{1,0:T(8,128)(2,1)S(1)}, bf16[128,4096]{1,0:T(8,128)(2,1)S(1)}, u32[]{:S(2)}, u32[]{:S(2)}) collective-permute-start(bf16[128,4096]{1,0:T(8,128)(2,1)S(1)} %collective-permute-done.6.p2.rest_13_), channel_id=1, source_target_pairs={{0,1},{1,0},{2,3},{3,2},{4,5},{5,4},{6,7},{7,6},{8,9},{9,8},{10,11... | collective-permute-start | bytes 3145736 | tf_op jit(solution)/shard_map/other_pools/ppermute | solution.py:293
  87.6 5.6 %collective-permute-start.12 = (bf16[1,64,2048]{2,1,0:T(8,128)(2,1)S(1)}, bf16[1,64,2048]{2,1,0:T(8,128)(2,1)S(1)}, u32[]{:S(2)}, u32[]{:S(2)}) collective-permute-start(bf16[1,64,2048]{2,1,0:T(8,128)(2,1)S(1)} %get-tuple-element.49.rest_4_), channel_id=1, source_target_pairs={{0,256},{128,384},{256,512},{384,640},{512,768},{640,896},{768,0},... | collective-permute-start | bytes 786440 | tf_op jit(solution)/shard_map/ring/ppermute | solution.py:288
  93.2 0.0 collective-permute-done.10.rest_3_
  93.2 2.6 %collective-permute-start.13 = (bf16[1,64,2048]{2,1,0:T(8,128)(2,1)S(1)}, bf16[1,64,2048]{2,1,0:T(8,128)(2,1)S(1)}, u32[]{:S(2)}, u32[]{:S(2)}) collective-permute-start(bf16[1,64,2048]{2,1,0:T(8,128)(2,1)S(1)} %get-tuple-element.50.rest_5_), channel_id=1, source_target_pairs={{0,8},{4,12},{8,16},{12,20},{16,24},{20,28},{24,0},{28,4},{1,25},{... | collective-permute-start | bytes 786440 | tf_op jit(solution)/shard_map/ring/ppermute | solution.py:288
  95.8 0.0 collective-permute-done.8.left_ref
  95.8 0.0 collective-permute-done.9.right_ref
  95.8 0.0 copy-start
  95.8 0.1 hand.5
  96.0 2.1 %collective-permute-start.11 = (bf16[4,64,2048]{2,1,0:T(8,128)(2,1)S(1)}, bf16[4,64,2048]{2,1,0:T(8,128)(2,1)S(1)}, u32[]{:S(2)}, u32[]{:S(2)}) collective-permute-start(bf16[4,64,2048]{2,1,0:T(8,128)(2,1)S(1)} %get-tuple-element.55), channel_id=1, source_target_pairs={{0,1},{1,0},{2,3},{3,2},{4,5},{5,4},{6,7},{7,6},{8,9},{9,8},{10,11... | collective-permute-start | bytes 3145736 | tf_op jit(solution)/shard_map/ring/ppermute | solution.py:290
  98.0 0.0 collective-permute-done.7.p3.rest_14_
  98.0 0.0 copy-done
  98.0 1.4 %hard.1.hard_ref = f32[128,512]{1,0:T(8,128)S(1)} custom-call(f32[128,512]{1,0:T(8,128)S(1)} %mask.1.mask_ref, bf16[128,4096]{1,0:T(8,128)(2,1)S(1)} %copy-done, bf16[128,4096]{1,0:T(8,128)(2,1)S(1)} %copy-done.1, bf16[128,4096]{1,0:T(8,128)(2,1)S(1)} %collective-permute-done.2.p1.rest_12_, bf16[128,4096]{1,0:T(8,128)(2,1)S(1)} %collective-permute-done.6.p2.rest_13_, ...), custom_call_target="tpu_custom_call" | custom-call | flops 17179869184 | bytes 4194304 | tf_op jit(solution)/shard_map/other_pools/hard/pallas_call | solution.py:189
  99.4 0.0 collective-permute-done.12.rest_9_
  99.4 3.2 %collective-permute-done.13.rest_10_ = bf16[1,64,2048]{2,1,0:T(8,128)(2,1)S(1)} collective-permute-done((bf16[1,64,2048]{2,1,0:T(8,128)(2,1)S(1)}, bf16[1,64,2048]{2,1,0:T(8,128)(2,1)S(1)}, u32[]{:S(2)}, u32[]{:S(2)}) %collective-permute-start.13) | collective-permute-done | bytes 262176 | tf_op jit(solution)/shard_map/ring/ppermute | solution.py:288
  102.6 0.0 collective-permute-done.11.rest_8_
  102.6 0.0 copy-start.3
  102.6 0.7 copy-done.3
  103.3 5.3 %tail.1 = (bf16[128,4096]{1,0:T(8,128)(2,1)}, f32[1,128]{1,0:T(1,128)}) custom-call(s32[4]{0:T(128)S(1)} %pad_add_fusion.place_ref, s32[1,128]{1,0:T(1,128)S(1)} %bitcast.12, f32[128,512]{1,0:T(8,128)S(1)} %hard.1.hard_ref, bf16[128,4096]{1,0:T(8,128)(2,1)S(1)} %copy-done, bf16[2,64,2048]{2,1,0:T(8,128)(2,1)S(1)} %get-tuple-element.45.rest_0_, ...), custom_call_target="tpu_custom_call" | custom-call | flops 2147483648 | bytes 12582912 | tf_op jit(solution)/shard_map/tail/pallas_call | solution.py:231
  (3 shorter events, 0.1 us)
Async XLA Ops:
  0.6 0.7 copy-start.2
  2.0 24.9 %all-to-all-start = ((bf16[8,2,2048]{2,1,0:T(2,128)(2,1)}), bf16[8,2,2048]{2,1,0:T(2,128)(2,1)S(1)}, u32[]{:S(2)}, u32[]{:S(2)}) async-start(bf16[8,2,2048]{2,1,0:T(2,128)(2,1)} %copies.1), calls=%async_computation | async-start | bytes 131072 | tf_op jit(solution)/shard_map/cross/all_to_all | solution.py:258
  19.4 0.7 copy-start.4
  19.5 0.7 copy-start.5
  19.5 0.7 copy-start.6
  21.1 27.0 %copy-start.1 = (bf16[128,4096]{1,0:T(8,128)(2,1)S(1)}, bf16[128,4096]{1,0:T(8,128)(2,1)}, u32[]{:S(2)}) copy-start(bf16[128,4096]{1,0:T(8,128)(2,1)} %rest_11_) | copy-start | bytes 3145732
  46.2 4.3 %collective-permute-start = (bf16[8,16,2048]{2,1,0:T(8,128)(2,1)S(1)}, bf16[8,16,2048]{2,1,0:T(8,128)(2,1)S(1)}, u32[]{:S(2)}, u32[]{:S(2)}) collective-permute-start(bf16[8,16,2048]{2,1,0:T(8,128)(2,1)S(1)} %all_to_all.10.mine_ref), channel_id=1, source_target_pairs={{0,1},{1,0},{2,3},{3,2},{4,5},{5,4},{6,7},{7,6},{8,9},{9,8},{10,11... | collective-permute-start | bytes 1572872 | tf_op jit(solution)/shard_map/near/ppermute | solution.py:266
  48.1 17.2 %collective-permute-start.2 = (bf16[128,4096]{1,0:T(8,128)(2,1)S(1)}, bf16[128,4096]{1,0:T(8,128)(2,1)S(1)}, u32[]{:S(2)}, u32[]{:S(2)}) collective-permute-start(bf16[128,4096]{1,0:T(8,128)(2,1)S(1)} %copy-done.1), channel_id=1, source_target_pairs={{0,1},{1,0},{2,3},{3,2},{4,5},{5,4},{6,7},{7,6},{8,9},{9,8},{10,11... | collective-permute-start | bytes 3145736 | tf_op jit(solution)/shard_map/ring/ppermute | solution.py:274
  51.2 15.7 %collective-permute-start.1 = (bf16[2,64,2048]{2,1,0:T(8,128)(2,1)S(1)}, bf16[2,64,2048]{2,1,0:T(8,128)(2,1)S(1)}, u32[]{:S(2)}, u32[]{:S(2)}) collective-permute-start(bf16[2,64,2048]{2,1,0:T(8,128)(2,1)S(1)} %get-tuple-element.33), channel_id=1, source_target_pairs={{0,128},{128,256},{256,384},{384,512},{512,640},{640,768},{768,896... | collective-permute-start | bytes 1572872 | tf_op jit(solution)/shard_map/ring/ppermute | solution.py:273
  60.8 11.4 %collective-permute-start.4 = (bf16[2,64,2048]{2,1,0:T(8,128)(2,1)S(1)}, bf16[2,64,2048]{2,1,0:T(8,128)(2,1)S(1)}, u32[]{:S(2)}, u32[]{:S(2)}) collective-permute-start(bf16[2,64,2048]{2,1,0:T(8,128)(2,1)S(1)} %get-tuple-element.35), channel_id=1, source_target_pairs={{0,4},{4,8},{8,12},{12,16},{16,20},{20,24},{24,28},{28,0},{1,29},{... | collective-permute-start | bytes 1572872 | tf_op jit(solution)/shard_map/ring/ppermute | solution.py:273
  62.7 22.9 %collective-permute-start.6 = (bf16[128,4096]{1,0:T(8,128)(2,1)S(1)}, bf16[128,4096]{1,0:T(8,128)(2,1)S(1)}, u32[]{:S(2)}, u32[]{:S(2)}) collective-permute-start(bf16[128,4096]{1,0:T(8,128)(2,1)S(1)} %copy-done.1), channel_id=1, source_target_pairs={{0,2},{1,3},{2,0},{3,1},{4,6},{5,7},{6,4},{7,5},{8,10},{9,11},{10,... | collective-permute-start | bytes 3145736 | tf_op jit(solution)/shard_map/pool_x/ppermute | solution.py:270
  66.9 11.4 %collective-permute-start.3 = (bf16[2,64,2048]{2,1,0:T(8,128)(2,1)S(1)}, bf16[2,64,2048]{2,1,0:T(8,128)(2,1)S(1)}, u32[]{:S(2)}, u32[]{:S(2)}) collective-permute-start(bf16[2,64,2048]{2,1,0:T(8,128)(2,1)S(1)} %collective-permute-done.1.left_ref), channel_id=1, source_target_pairs={{0,128},{128,256},{256,384},{384,512},{512,640},{640,768},{768,896... | collective-permute-start | bytes 1572872 | tf_op jit(solution)/shard_map/ring/ppermute | solution.py:278
  72.2 11.4 %collective-permute-start.5 = (bf16[2,64,2048]{2,1,0:T(8,128)(2,1)S(1)}, bf16[2,64,2048]{2,1,0:T(8,128)(2,1)S(1)}, u32[]{:S(2)}, u32[]{:S(2)}) collective-permute-start(bf16[2,64,2048]{2,1,0:T(8,128)(2,1)S(1)} %collective-permute-done.4.right_ref), channel_id=1, source_target_pairs={{0,4},{4,8},{8,12},{12,16},{16,20},{20,24},{24,28},{28,0},{1,29},{... | collective-permute-start | bytes 1572872 | tf_op jit(solution)/shard_map/ring/ppermute | solution.py:278
  74.2 18.9 %collective-permute-start.10 = (bf16[2,64,2048]{2,1,0:T(8,128)(2,1)S(1)}, bf16[2,64,2048]{2,1,0:T(8,128)(2,1)S(1)}, u32[]{:S(2)}, u32[]{:S(2)}) collective-permute-start(bf16[2,64,2048]{2,1,0:T(8,128)(2,1)S(1)} %get-tuple-element.42), channel_id=1, source_target_pairs={{0,1},{1,0},{2,3},{3,2},{4,5},{5,4},{6,7},{7,6},{8,9},{9,8},{10,11... | collective-permute-start | bytes 1572872 | tf_op jit(solution)/shard_map/ring/ppermute | solution.py:290
  78.3 17.5 %collective-permute-start.8 = (bf16[2,64,2048]{2,1,0:T(8,128)(2,1)S(1)}, bf16[2,64,2048]{2,1,0:T(8,128)(2,1)S(1)}, u32[]{:S(2)}, u32[]{:S(2)}) collective-permute-start(bf16[2,64,2048]{2,1,0:T(8,128)(2,1)S(1)} %collective-permute-done.3.left_ref), channel_id=1, source_target_pairs={{0,128},{128,256},{256,384},{384,512},{512,640},{640,768},{768,896... | collective-permute-start | bytes 1572872 | tf_op jit(solution)/shard_map/ring/ppermute | solution.py:278
  83.7 12.2 %collective-permute-start.9 = (bf16[2,64,2048]{2,1,0:T(8,128)(2,1)S(1)}, bf16[2,64,2048]{2,1,0:T(8,128)(2,1)S(1)}, u32[]{:S(2)}, u32[]{:S(2)}) collective-permute-start(bf16[2,64,2048]{2,1,0:T(8,128)(2,1)S(1)} %collective-permute-done.5.right_ref), channel_id=1, source_target_pairs={{0,4},{4,8},{8,12},{12,16},{16,20},{20,24},{24,28},{28,0},{1,29},{... | collective-permute-start | bytes 1572872 | tf_op jit(solution)/shard_map/ring/ppermute | solution.py:278
  85.7 12.3 %collective-permute-start.7 = (bf16[128,4096]{1,0:T(8,128)(2,1)S(1)}, bf16[128,4096]{1,0:T(8,128)(2,1)S(1)}, u32[]{:S(2)}, u32[]{:S(2)}) collective-permute-start(bf16[128,4096]{1,0:T(8,128)(2,1)S(1)} %collective-permute-done.6.p2.rest_13_), channel_id=1, source_target_pairs={{0,1},{1,0},{2,3},{3,2},{4,5},{5,4},{6,7},{7,6},{8,9},{9,8},{10,11... | collective-permute-start | bytes 3145736 | tf_op jit(solution)/shard_map/other_pools/ppermute | solution.py:293
  87.6 11.8 %collective-permute-start.12 = (bf16[1,64,2048]{2,1,0:T(8,128)(2,1)S(1)}, bf16[1,64,2048]{2,1,0:T(8,128)(2,1)S(1)}, u32[]{:S(2)}, u32[]{:S(2)}) collective-permute-start(bf16[1,64,2048]{2,1,0:T(8,128)(2,1)S(1)} %get-tuple-element.49.rest_4_), channel_id=1, source_target_pairs={{0,256},{128,384},{256,512},{384,640},{512,768},{640,896},{768,0},... | collective-permute-start | bytes 786440 | tf_op jit(solution)/shard_map/ring/ppermute | solution.py:288
  93.2 9.4 %collective-permute-start.13 = (bf16[1,64,2048]{2,1,0:T(8,128)(2,1)S(1)}, bf16[1,64,2048]{2,1,0:T(8,128)(2,1)S(1)}, u32[]{:S(2)}, u32[]{:S(2)}) collective-permute-start(bf16[1,64,2048]{2,1,0:T(8,128)(2,1)S(1)} %get-tuple-element.50.rest_5_), channel_id=1, source_target_pairs={{0,8},{4,12},{8,16},{12,20},{16,24},{20,28},{24,0},{28,4},{1,25},{... | collective-permute-start | bytes 786440 | tf_op jit(solution)/shard_map/ring/ppermute | solution.py:288
  95.8 2.2 %copy-start = (bf16[128,4096]{1,0:T(8,128)(2,1)S(1)}, bf16[128,4096]{1,0:T(8,128)(2,1)}, u32[]{:S(2)}) copy-start(bf16[128,4096]{1,0:T(8,128)(2,1)} %q_ref.3) | copy-start | bytes 3145732
  96.0 6.7 %collective-permute-start.11 = (bf16[4,64,2048]{2,1,0:T(8,128)(2,1)S(1)}, bf16[4,64,2048]{2,1,0:T(8,128)(2,1)S(1)}, u32[]{:S(2)}, u32[]{:S(2)}) collective-permute-start(bf16[4,64,2048]{2,1,0:T(8,128)(2,1)S(1)} %get-tuple-element.55), channel_id=1, source_target_pairs={{0,1},{1,0},{2,3},{3,2},{4,5},{5,4},{6,7},{7,6},{8,9},{9,8},{10,11... | collective-permute-start | bytes 3145736 | tf_op jit(solution)/shard_map/ring/ppermute | solution.py:290
  102.6 0.7 copy-start.3

commit v8 on v7

--- a/solution.py
+++ b/solution.py
@@ -277,6 +277,7 @@
             if step < 2:
                 next_left, next_right = lax.ppermute(left, "d", RING_Z), lax.ppermute(right, "d", RING_Y)
             else:
+                _, pool_x = lax.optimization_barrier((left, pool_x))
                 left, right, *blocks = lax.optimization_barrier((left, right, *blocks))
                 waiting = (give,)
             if step == 0:
@@ -284,7 +285,6 @@
             keep_left, keep_right, give = hand_call(left, right, *waiting, flops=2**33 if step < 2 else 2**35)
             blocks += [keep_left, keep_right]
             if step == 1:
-                _, pool_x = lax.optimization_barrier((give, pool_x))
                 last = [lax.ppermute(keep_left, "d", RING_Z2), lax.ppermute(keep_right, "d", RING_Y2)]
             else:
                 blocks.append(lax.ppermute(give, "d", OTHER_CORE))

time: 110 us -> 110 us (level); the launches traced: 109 us -> 110 us
  waiting for transfers between devices: 12.7 us -> 16 us
  starting transfers between devices: 64.3 us -> 62.2 us
    ppermute x3, waiting for transfers between devices: 0.01 us -> 4.37 us  [body(): lax.ppermute(right, 'd', RING_Y)]
    ppermute x1, starting transfers between devices: 5.56 us -> 2.1 us  [body(): lax.ppermute(keep_left, 'd', RING_Z2)]
    ppermute x1, waiting for transfers between devices: 3.2 us -> 0.01 us  [body(): lax.ppermute(keep_right, 'd', RING_Y2)]
    ppermute x1, starting transfers between devices: 1.92 us -> 3.96 us  [body(): pool_xc = lax.ppermute(pool_x, 'd', OTHER_CORE)]
    ppermute x2, waiting for transfers between devices: 0.01 us -> 1.17 us  [body(): blocks.append(lax.ppermute(give, 'd', OTHER_CORE))]
  transfers between devices with their start and end apart: 15 -> 15, of which waited for: 4 -> 7; matrix products, arithmetic and copies ran while one was open for 0% -> 0% of each run, Pallas kernels for 3% -> 3%
where the time goes in v8:
time: 110 us
  starting transfers between devices  62.2 us (57%)
  blocking collectives  19.2 us (17%)
  waiting for transfers between devices  16 us (15%)
  Pallas kernels  9.15 us (8%)
  local copies, waits for them, and re-layouts  2.19 us (2%)
    ppermute x3, starting transfers between devices, body(): lax.ppermute(left, 'd', RING_Z)  20.2 us
    all_to_all x1, blocking collectives, body(): near = lax.all_to_all(sent, 'd', 0, 0, axis_index_groups=NEAR, tiled=True)  19.2 us
    all_to_all x1, starting transfers between devices, body(): lax.all_to_all(copies_call(passages), 'd', 0, 0, axis_index_groups=CROSS,...  17.4 us
    ppermute x3, starting transfers between devices, body(): lax.ppermute(right, 'd', RING_Y)  5.76 us
    all_to_all x1, waiting for transfers between devices, body(): lax.all_to_all(copies_call(passages), 'd', 0, 0, axis_index_groups=CROSS,...  5.72 us
    pallas_call x1, Pallas kernels, tail_call(): pl.pallas_call(tail_kernel, out_shape=(jax.ShapeDtypeStruct((rows, width)...  5.3 us
    ppermute x3, waiting for transfers between devices, body(): lax.ppermute(left, 'd', RING_Z)  4.64 us
    ppermute x3, waiting for transfers between devices, body(): lax.ppermute(right, 'd', RING_Y)  4.37 us
  transfers between devices with their start and end apart: 15, of which 7 were waited for; matrix products, arithmetic and copies ran while one was open for 0% of the time, Pallas kernels for 3%

profile of v8, /device:TPU:1, one launch (start us, length us, event | category | flops | bytes accessed | tf_op | source)
XLA Modules:
  0.0 109.7 jit_solution(3544813729234003046)
XLA Ops:
  0.6 0.0 copy-start.2
  0.6 0.7 copy-done.2
  1.3 0.6 copies.1
  2.0 17.4 %all-to-all-start = ((bf16[8,2,2048]{2,1,0:T(2,128)(2,1)}), bf16[8,2,2048]{2,1,0:T(2,128)(2,1)S(1)}, u32[]{:S(2)}, u32[]{:S(2)}) async-start(bf16[8,2,2048]{2,1,0:T(2,128)(2,1)} %copies.1), calls=%async_computation | async-start | bytes 131072 | tf_op jit(solution)/shard_map/cross/all_to_all | solution.py:258
  19.4 0.0 copy-start.4
  19.4 0.1 pad_add_fusion.place_ref
  19.5 0.0 copy-start.5
  19.5 0.0 copy-start.6
  19.5 0.6 copy-done.4
  20.1 0.0 copy-done.5
  20.2 0.0 copy-done.6
  20.2 1.0 mask.1.mask_ref
  21.1 0.0 copy-start.1
  21.1 5.7 %all-to-all-done = bf16[8,2,2048]{2,1,0:T(2,128)(2,1)S(1)} async-done(((bf16[8,2,2048]{2,1,0:T(2,128)(2,1)}), bf16[8,2,2048]{2,1,0:T(2,128)(2,1)S(1)}, u32[]{:S(2)}, u32[]{:S(2)}) %all-to-all-start) | async-done | bytes 65568 | tf_op jit(solution)/shard_map/cross/all_to_all | solution.py:258
  27.0 19.2 %all_to_all.10.mine_ref = bf16[8,16,2048]{2,1,0:T(8,128)(2,1)S(1)} all-to-all(bf16[8,16,2048]{2,1,0:T(8,128)(2,1)S(1)} %broadcast_in_dim.8), channel_id=1, replica_groups={{0,4,8,12,16,20,24,28},{2,6,10,14,18,22,26,30},{32,36,40,44,48,52,56,60..., dimensions={0} | all-to-all | bytes 1048576 | tf_op jit(solution)/shard_map/near/all_to_all | solution.py:265
  46.2 1.9 %collective-permute-start = (bf16[8,16,2048]{2,1,0:T(8,128)(2,1)S(1)}, bf16[8,16,2048]{2,1,0:T(8,128)(2,1)S(1)}, u32[]{:S(2)}, u32[]{:S(2)}) collective-permute-start(bf16[8,16,2048]{2,1,0:T(8,128)(2,1)S(1)} %all_to_all.10.mine_ref), channel_id=1, source_target_pairs={{0,1},{1,0},{2,3},{3,2},{4,5},{5,4},{6,7},{7,6},{8,9},{9,8},{10,11... | collective-permute-start | bytes 1572872 | tf_op jit(solution)/shard_map/near/ppermute | solution.py:266
  48.1 0.0 copy-done.1
  48.1 2.4 %collective-permute-start.2 = (bf16[128,4096]{1,0:T(8,128)(2,1)S(1)}, bf16[128,4096]{1,0:T(8,128)(2,1)S(1)}, u32[]{:S(2)}, u32[]{:S(2)}) collective-permute-start(bf16[128,4096]{1,0:T(8,128)(2,1)S(1)} %copy-done.1), channel_id=1, source_target_pairs={{0,1},{1,0},{2,3},{3,2},{4,5},{5,4},{6,7},{7,6},{8,9},{9,8},{10,11... | collective-permute-start | bytes 3145736 | tf_op jit(solution)/shard_map/ring/ppermute | solution.py:274
  50.5 0.0 collective-permute-done.theirs_ref
  50.5 0.7 sort.1
  51.2 9.6 %collective-permute-start.1 = (bf16[2,64,2048]{2,1,0:T(8,128)(2,1)S(1)}, bf16[2,64,2048]{2,1,0:T(8,128)(2,1)S(1)}, u32[]{:S(2)}, u32[]{:S(2)}) collective-permute-start(bf16[2,64,2048]{2,1,0:T(8,128)(2,1)S(1)} %get-tuple-element.33), channel_id=1, source_target_pairs={{0,128},{128,256},{256,384},{384,512},{512,640},{640,768},{768,896... | collective-permute-start | bytes 1572872 | tf_op jit(solution)/shard_map/ring/ppermute | solution.py:273
  60.8 1.9 %collective-permute-start.7 = (bf16[2,64,2048]{2,1,0:T(8,128)(2,1)S(1)}, bf16[2,64,2048]{2,1,0:T(8,128)(2,1)S(1)}, u32[]{:S(2)}, u32[]{:S(2)}) collective-permute-start(bf16[2,64,2048]{2,1,0:T(8,128)(2,1)S(1)} %get-tuple-element.36), channel_id=1, source_target_pairs={{0,4},{4,8},{8,12},{12,16},{16,20},{20,24},{24,28},{28,0},{1,29},{... | collective-permute-start | bytes 1572872 | tf_op jit(solution)/shard_map/ring/ppermute | solution.py:273
  62.7 2.5 %collective-permute-start.5 = (bf16[128,4096]{1,0:T(8,128)(2,1)S(1)}, bf16[128,4096]{1,0:T(8,128)(2,1)S(1)}, u32[]{:S(2)}, u32[]{:S(2)}) collective-permute-start(bf16[128,4096]{1,0:T(8,128)(2,1)S(1)} %copy-done.1), channel_id=1, source_target_pairs={{0,2},{1,3},{2,0},{3,1},{4,6},{5,7},{6,4},{7,5},{8,10},{9,11},{10,... | collective-permute-start | bytes 3145736 | tf_op jit(solution)/shard_map/pool_x/ppermute | solution.py:270
  65.3 0.0 collective-permute-done.2.p1.rest_12_
  65.3 1.6 %collective-permute-done.1.left_ref = bf16[2,64,2048]{2,1,0:T(8,128)(2,1)S(1)} collective-permute-done((bf16[2,64,2048]{2,1,0:T(8,128)(2,1)S(1)}, bf16[2,64,2048]{2,1,0:T(8,128)(2,1)S(1)}, u32[]{:S(2)}, u32[]{:S(2)}) %collective-permute-start.1) | collective-permute-done | bytes 524320 | tf_op jit(solution)/shard_map/ring/ppermute | solution.py:273
  66.9 5.3 %collective-permute-start.3 = (bf16[2,64,2048]{2,1,0:T(8,128)(2,1)S(1)}, bf16[2,64,2048]{2,1,0:T(8,128)(2,1)S(1)}, u32[]{:S(2)}, u32[]{:S(2)}) collective-permute-start(bf16[2,64,2048]{2,1,0:T(8,128)(2,1)S(1)} %collective-permute-done.1.left_ref), channel_id=1, source_target_pairs={{0,128},{128,256},{256,384},{384,512},{512,640},{640,768},{768,896... | collective-permute-start | bytes 1572872 | tf_op jit(solution)/shard_map/ring/ppermute | solution.py:278
  72.2 0.0 collective-permute-done.7.right_ref
  72.2 1.9 %collective-permute-start.8 = (bf16[2,64,2048]{2,1,0:T(8,128)(2,1)S(1)}, bf16[2,64,2048]{2,1,0:T(8,128)(2,1)S(1)}, u32[]{:S(2)}, u32[]{:S(2)}) collective-permute-start(bf16[2,64,2048]{2,1,0:T(8,128)(2,1)S(1)} %collective-permute-done.7.right_ref), channel_id=1, source_target_pairs={{0,4},{4,8},{8,12},{12,16},{16,20},{20,24},{24,28},{28,0},{1,29},{... | collective-permute-start | bytes 1572872 | tf_op jit(solution)/shard_map/ring/ppermute | solution.py:278
  74.2 0.1 hand.3
  74.2 1.9 %collective-permute-start.10 = (bf16[2,64,2048]{2,1,0:T(8,128)(2,1)S(1)}, bf16[2,64,2048]{2,1,0:T(8,128)(2,1)S(1)}, u32[]{:S(2)}, u32[]{:S(2)}) collective-permute-start(bf16[2,64,2048]{2,1,0:T(8,128)(2,1)S(1)} %get-tuple-element.41), channel_id=1, source_target_pairs={{0,1},{1,0},{2,3},{3,2},{4,5},{5,4},{6,7},{7,6},{8,9},{9,8},{10,11... | collective-permute-start | bytes 1572872 | tf_op jit(solution)/shard_map/ring/ppermute | solution.py:290
  76.2 2.2 %collective-permute-done.3.left_ref = bf16[2,64,2048]{2,1,0:T(8,128)(2,1)S(1)} collective-permute-done((bf16[2,64,2048]{2,1,0:T(8,128)(2,1)S(1)}, bf16[2,64,2048]{2,1,0:T(8,128)(2,1)S(1)}, u32[]{:S(2)}, u32[]{:S(2)}) %collective-permute-start.3) | collective-permute-done | bytes 524320 | tf_op jit(solution)/shard_map/ring/ppermute | solution.py:278
  78.3 5.3 %collective-permute-start.4 = (bf16[2,64,2048]{2,1,0:T(8,128)(2,1)S(1)}, bf16[2,64,2048]{2,1,0:T(8,128)(2,1)S(1)}, u32[]{:S(2)}, u32[]{:S(2)}) collective-permute-start(bf16[2,64,2048]{2,1,0:T(8,128)(2,1)S(1)} %collective-permute-done.3.left_ref), channel_id=1, source_target_pairs={{0,128},{128,256},{256,384},{384,512},{512,640},{640,768},{768,896... | collective-permute-start | bytes 1572872 | tf_op jit(solution)/shard_map/ring/ppermute | solution.py:278
  83.6 0.0 collective-permute-done.8.right_ref
  83.7 1.9 %collective-permute-start.9 = (bf16[2,64,2048]{2,1,0:T(8,128)(2,1)S(1)}, bf16[2,64,2048]{2,1,0:T(8,128)(2,1)S(1)}, u32[]{:S(2)}, u32[]{:S(2)}) collective-permute-start(bf16[2,64,2048]{2,1,0:T(8,128)(2,1)S(1)} %collective-permute-done.8.right_ref), channel_id=1, source_target_pairs={{0,4},{4,8},{8,12},{12,16},{16,20},{20,24},{24,28},{28,0},{1,29},{... | collective-permute-start | bytes 1572872 | tf_op jit(solution)/shard_map/ring/ppermute | solution.py:278
  85.6 0.1 hand.4
  85.7 2.1 %collective-permute-start.12 = (bf16[1,64,2048]{2,1,0:T(8,128)(2,1)S(1)}, bf16[1,64,2048]{2,1,0:T(8,128)(2,1)S(1)}, u32[]{:S(2)}, u32[]{:S(2)}) collective-permute-start(bf16[1,64,2048]{2,1,0:T(8,128)(2,1)S(1)} %get-tuple-element.48.rest_4_), channel_id=1, source_target_pairs={{0,256},{128,384},{256,512},{384,640},{512,768},{640,896},{768,0},... | collective-permute-start | bytes 786440 | tf_op jit(solution)/shard_map/ring/ppermute | solution.py:288
  87.8 0.0 collective-permute-done.10.rest_3_
  87.8 1.9 %collective-permute-start.13 = (bf16[1,64,2048]{2,1,0:T(8,128)(2,1)S(1)}, bf16[1,64,2048]{2,1,0:T(8,128)(2,1)S(1)}, u32[]{:S(2)}, u32[]{:S(2)}) collective-permute-start(bf16[1,64,2048]{2,1,0:T(8,128)(2,1)S(1)} %get-tuple-element.49.rest_5_), channel_id=1, source_target_pairs={{0,8},{4,12},{8,16},{12,20},{16,24},{20,28},{24,0},{28,4},{1,25},{... | collective-permute-start | bytes 786440 | tf_op jit(solution)/shard_map/ring/ppermute | solution.py:288
  89.7 0.9 collective-permute-done.4.left_ref
  90.6 4.4 %collective-permute-done.9.right_ref = bf16[2,64,2048]{2,1,0:T(8,128)(2,1)S(1)} collective-permute-done((bf16[2,64,2048]{2,1,0:T(8,128)(2,1)S(1)}, bf16[2,64,2048]{2,1,0:T(8,128)(2,1)S(1)}, u32[]{:S(2)}, u32[]{:S(2)}) %collective-permute-start.9) | collective-permute-done | bytes 524320 | tf_op jit(solution)/shard_map/ring/ppermute | solution.py:278
  94.9 0.0 collective-permute-done.5.p2.rest_13_
  94.9 4.0 %collective-permute-start.6 = (bf16[128,4096]{1,0:T(8,128)(2,1)S(1)}, bf16[128,4096]{1,0:T(8,128)(2,1)S(1)}, u32[]{:S(2)}, u32[]{:S(2)}) collective-permute-start(bf16[128,4096]{1,0:T(8,128)(2,1)S(1)} %collective-permute-done.5.p2.rest_13_), channel_id=1, source_target_pairs={{0,1},{1,0},{2,3},{3,2},{4,5},{5,4},{6,7},{7,6},{8,9},{9,8},{10,11... | collective-permute-start | bytes 3145736 | tf_op jit(solution)/shard_map/other_pools/ppermute | solution.py:293
  98.9 0.0 copy-start
  98.9 0.1 hand.5
  99.0 2.1 %collective-permute-start.11 = (bf16[4,64,2048]{2,1,0:T(8,128)(2,1)S(1)}, bf16[4,64,2048]{2,1,0:T(8,128)(2,1)S(1)}, u32[]{:S(2)}, u32[]{:S(2)}) collective-permute-start(bf16[4,64,2048]{2,1,0:T(8,128)(2,1)S(1)} %get-tuple-element.55), channel_id=1, source_target_pairs={{0,1},{1,0},{2,3},{3,2},{4,5},{5,4},{6,7},{7,6},{8,9},{9,8},{10,11... | collective-permute-start | bytes 3145736 | tf_op jit(solution)/shard_map/ring/ppermute | solution.py:290
  101.1 0.1 collective-permute-done.6.p3.rest_14_
  101.2 0.0 copy-done
  101.2 1.4 %hard.1.hard_ref = f32[128,512]{1,0:T(8,128)S(1)} custom-call(f32[128,512]{1,0:T(8,128)S(1)} %mask.1.mask_ref, bf16[128,4096]{1,0:T(8,128)(2,1)S(1)} %copy-done, bf16[128,4096]{1,0:T(8,128)(2,1)S(1)} %copy-done.1, bf16[128,4096]{1,0:T(8,128)(2,1)S(1)} %collective-permute-done.2.p1.rest_12_, bf16[128,4096]{1,0:T(8,128)(2,1)S(1)} %collective-permute-done.5.p2.rest_13_, ...), custom_call_target="tpu_custom_call" | custom-call | flops 17179869184 | bytes 4194304 | tf_op jit(solution)/shard_map/other_pools/hard/pallas_call | solution.py:189
  102.5 0.0 collective-permute-done.12.rest_9_
  102.5 0.0 collective-permute-done.13.rest_10_
  102.6 1.2 %collective-permute-done.11.rest_8_ = bf16[4,64,2048]{2,1,0:T(8,128)(2,1)S(1)} collective-permute-done((bf16[4,64,2048]{2,1,0:T(8,128)(2,1)S(1)}, bf16[4,64,2048]{2,1,0:T(8,128)(2,1)S(1)}, u32[]{:S(2)}, u32[]{:S(2)}) %collective-permute-start.11) | collective-permute-done | bytes 1048608 | tf_op jit(solution)/shard_map/ring/ppermute | solution.py:290
  103.7 0.0 copy-start.3
  103.7 0.7 copy-done.3
  104.4 5.3 %tail.1 = (bf16[128,4096]{1,0:T(8,128)(2,1)}, f32[1,128]{1,0:T(1,128)}) custom-call(s32[4]{0:T(128)S(1)} %pad_add_fusion.place_ref, s32[1,128]{1,0:T(1,128)S(1)} %bitcast.12, f32[128,512]{1,0:T(8,128)S(1)} %hard.1.hard_ref, bf16[128,4096]{1,0:T(8,128)(2,1)S(1)} %copy-done, bf16[2,64,2048]{2,1,0:T(8,128)(2,1)S(1)} %get-tuple-element.44.rest_0_, ...), custom_call_target="tpu_custom_call" | custom-call | flops 2147483648 | bytes 12582912 | tf_op jit(solution)/shard_map/tail/pallas_call | solution.py:231
  (3 shorter events, 0.1 us)
Async XLA Ops:
  0.6 0.7 copy-start.2
  2.0 24.9 %all-to-all-start = ((bf16[8,2,2048]{2,1,0:T(2,128)(2,1)}), bf16[8,2,2048]{2,1,0:T(2,128)(2,1)S(1)}, u32[]{:S(2)}, u32[]{:S(2)}) async-start(bf16[8,2,2048]{2,1,0:T(2,128)(2,1)} %copies.1), calls=%async_computation | async-start | bytes 131072 | tf_op jit(solution)/shard_map/cross/all_to_all | solution.py:258
  19.4 0.7 copy-start.4
  19.5 0.7 copy-start.5
  19.5 0.7 copy-start.6
  21.1 27.0 %copy-start.1 = (bf16[128,4096]{1,0:T(8,128)(2,1)S(1)}, bf16[128,4096]{1,0:T(8,128)(2,1)}, u32[]{:S(2)}) copy-start(bf16[128,4096]{1,0:T(8,128)(2,1)} %rest_11_) | copy-start | bytes 3145732
  46.2 4.3 %collective-permute-start = (bf16[8,16,2048]{2,1,0:T(8,128)(2,1)S(1)}, bf16[8,16,2048]{2,1,0:T(8,128)(2,1)S(1)}, u32[]{:S(2)}, u32[]{:S(2)}) collective-permute-start(bf16[8,16,2048]{2,1,0:T(8,128)(2,1)S(1)} %all_to_all.10.mine_ref), channel_id=1, source_target_pairs={{0,1},{1,0},{2,3},{3,2},{4,5},{5,4},{6,7},{7,6},{8,9},{9,8},{10,11... | collective-permute-start | bytes 1572872 | tf_op jit(solution)/shard_map/near/ppermute | solution.py:266
  48.1 17.2 %collective-permute-start.2 = (bf16[128,4096]{1,0:T(8,128)(2,1)S(1)}, bf16[128,4096]{1,0:T(8,128)(2,1)S(1)}, u32[]{:S(2)}, u32[]{:S(2)}) collective-permute-start(bf16[128,4096]{1,0:T(8,128)(2,1)S(1)} %copy-done.1), channel_id=1, source_target_pairs={{0,1},{1,0},{2,3},{3,2},{4,5},{5,4},{6,7},{7,6},{8,9},{9,8},{10,11... | collective-permute-start | bytes 3145736 | tf_op jit(solution)/shard_map/ring/ppermute | solution.py:274
  51.2 15.7 %collective-permute-start.1 = (bf16[2,64,2048]{2,1,0:T(8,128)(2,1)S(1)}, bf16[2,64,2048]{2,1,0:T(8,128)(2,1)S(1)}, u32[]{:S(2)}, u32[]{:S(2)}) collective-permute-start(bf16[2,64,2048]{2,1,0:T(8,128)(2,1)S(1)} %get-tuple-element.33), channel_id=1, source_target_pairs={{0,128},{128,256},{256,384},{384,512},{512,640},{640,768},{768,896... | collective-permute-start | bytes 1572872 | tf_op jit(solution)/shard_map/ring/ppermute | solution.py:273
  60.8 11.4 %collective-permute-start.7 = (bf16[2,64,2048]{2,1,0:T(8,128)(2,1)S(1)}, bf16[2,64,2048]{2,1,0:T(8,128)(2,1)S(1)}, u32[]{:S(2)}, u32[]{:S(2)}) collective-permute-start(bf16[2,64,2048]{2,1,0:T(8,128)(2,1)S(1)} %get-tuple-element.36), channel_id=1, source_target_pairs={{0,4},{4,8},{8,12},{12,16},{16,20},{20,24},{24,28},{28,0},{1,29},{... | collective-permute-start | bytes 1572872 | tf_op jit(solution)/shard_map/ring/ppermute | solution.py:273
  62.7 32.2 %collective-permute-start.5 = (bf16[128,4096]{1,0:T(8,128)(2,1)S(1)}, bf16[128,4096]{1,0:T(8,128)(2,1)S(1)}, u32[]{:S(2)}, u32[]{:S(2)}) collective-permute-start(bf16[128,4096]{1,0:T(8,128)(2,1)S(1)} %copy-done.1), channel_id=1, source_target_pairs={{0,2},{1,3},{2,0},{3,1},{4,6},{5,7},{6,4},{7,5},{8,10},{9,11},{10,... | collective-permute-start | bytes 3145736 | tf_op jit(solution)/shard_map/pool_x/ppermute | solution.py:270
  66.9 11.4 %collective-permute-start.3 = (bf16[2,64,2048]{2,1,0:T(8,128)(2,1)S(1)}, bf16[2,64,2048]{2,1,0:T(8,128)(2,1)S(1)}, u32[]{:S(2)}, u32[]{:S(2)}) collective-permute-start(bf16[2,64,2048]{2,1,0:T(8,128)(2,1)S(1)} %collective-permute-done.1.left_ref), channel_id=1, source_target_pairs={{0,128},{128,256},{256,384},{384,512},{512,640},{640,768},{768,896... | collective-permute-start | bytes 1572872 | tf_op jit(solution)/shard_map/ring/ppermute | solution.py:278
  72.2 11.4 %collective-permute-start.8 = (bf16[2,64,2048]{2,1,0:T(8,128)(2,1)S(1)}, bf16[2,64,2048]{2,1,0:T(8,128)(2,1)S(1)}, u32[]{:S(2)}, u32[]{:S(2)}) collective-permute-start(bf16[2,64,2048]{2,1,0:T(8,128)(2,1)S(1)} %collective-permute-done.7.right_ref), channel_id=1, source_target_pairs={{0,4},{4,8},{8,12},{12,16},{16,20},{20,24},{24,28},{28,0},{1,29},{... | collective-permute-start | bytes 1572872 | tf_op jit(solution)/shard_map/ring/ppermute | solution.py:278
  74.2 13.5 %collective-permute-start.10 = (bf16[2,64,2048]{2,1,0:T(8,128)(2,1)S(1)}, bf16[2,64,2048]{2,1,0:T(8,128)(2,1)S(1)}, u32[]{:S(2)}, u32[]{:S(2)}) collective-permute-start(bf16[2,64,2048]{2,1,0:T(8,128)(2,1)S(1)} %get-tuple-element.41), channel_id=1, source_target_pairs={{0,1},{1,0},{2,3},{3,2},{4,5},{5,4},{6,7},{7,6},{8,9},{9,8},{10,11... | collective-permute-start | bytes 1572872 | tf_op jit(solution)/shard_map/ring/ppermute | solution.py:290
  78.3 12.2 %collective-permute-start.4 = (bf16[2,64,2048]{2,1,0:T(8,128)(2,1)S(1)}, bf16[2,64,2048]{2,1,0:T(8,128)(2,1)S(1)}, u32[]{:S(2)}, u32[]{:S(2)}) collective-permute-start(bf16[2,64,2048]{2,1,0:T(8,128)(2,1)S(1)} %collective-permute-done.3.left_ref), channel_id=1, source_target_pairs={{0,128},{128,256},{256,384},{384,512},{512,640},{640,768},{768,896... | collective-permute-start | bytes 1572872 | tf_op jit(solution)/shard_map/ring/ppermute | solution.py:278
  83.7 11.3 %collective-permute-start.9 = (bf16[2,64,2048]{2,1,0:T(8,128)(2,1)S(1)}, bf16[2,64,2048]{2,1,0:T(8,128)(2,1)S(1)}, u32[]{:S(2)}, u32[]{:S(2)}) collective-permute-start(bf16[2,64,2048]{2,1,0:T(8,128)(2,1)S(1)} %collective-permute-done.8.right_ref), channel_id=1, source_target_pairs={{0,4},{4,8},{8,12},{12,16},{16,20},{20,24},{24,28},{28,0},{1,29},{... | collective-permute-start | bytes 1572872 | tf_op jit(solution)/shard_map/ring/ppermute | solution.py:278
  85.7 16.9 %collective-permute-start.12 = (bf16[1,64,2048]{2,1,0:T(8,128)(2,1)S(1)}, bf16[1,64,2048]{2,1,0:T(8,128)(2,1)S(1)}, u32[]{:S(2)}, u32[]{:S(2)}) collective-permute-start(bf16[1,64,2048]{2,1,0:T(8,128)(2,1)S(1)} %get-tuple-element.48.rest_4_), channel_id=1, source_target_pairs={{0,256},{128,384},{256,512},{384,640},{512,768},{640,896},{768,0},... | collective-permute-start | bytes 786440 | tf_op jit(solution)/shard_map/ring/ppermute | solution.py:288
  87.8 14.8 %collective-permute-start.13 = (bf16[1,64,2048]{2,1,0:T(8,128)(2,1)S(1)}, bf16[1,64,2048]{2,1,0:T(8,128)(2,1)S(1)}, u32[]{:S(2)}, u32[]{:S(2)}) collective-permute-start(bf16[1,64,2048]{2,1,0:T(8,128)(2,1)S(1)} %get-tuple-element.49.rest_5_), channel_id=1, source_target_pairs={{0,8},{4,12},{8,16},{12,20},{16,24},{20,28},{24,0},{28,4},{1,25},{... | collective-permute-start | bytes 786440 | tf_op jit(solution)/shard_map/ring/ppermute | solution.py:288
  94.9 6.2 %collective-permute-start.6 = (bf16[128,4096]{1,0:T(8,128)(2,1)S(1)}, bf16[128,4096]{1,0:T(8,128)(2,1)S(1)}, u32[]{:S(2)}, u32[]{:S(2)}) collective-permute-start(bf16[128,4096]{1,0:T(8,128)(2,1)S(1)} %collective-permute-done.5.p2.rest_13_), channel_id=1, source_target_pairs={{0,1},{1,0},{2,3},{3,2},{4,5},{5,4},{6,7},{7,6},{8,9},{9,8},{10,11... | collective-permute-start | bytes 3145736 | tf_op jit(solution)/shard_map/other_pools/ppermute | solution.py:293
  98.9 2.3 %copy-start = (bf16[128,4096]{1,0:T(8,128)(2,1)S(1)}, bf16[128,4096]{1,0:T(8,128)(2,1)}, u32[]{:S(2)}) copy-start(bf16[128,4096]{1,0:T(8,128)(2,1)} %q_ref.3) | copy-start | bytes 3145732
  99.0 4.7 %collective-permute-start.11 = (bf16[4,64,2048]{2,1,0:T(8,128)(2,1)S(1)}, bf16[4,64,2048]{2,1,0:T(8,128)(2,1)S(1)}, u32[]{:S(2)}, u32[]{:S(2)}) collective-permute-start(bf16[4,64,2048]{2,1,0:T(8,128)(2,1)S(1)} %get-tuple-element.55), channel_id=1, source_target_pairs={{0,1},{1,0},{2,3},{3,2},{4,5},{5,4},{6,7},{7,6},{8,9},{9,8},{10,11... | collective-permute-start | bytes 3145736 | tf_op jit(solution)/shard_map/ring/ppermute | solution.py:290
  103.7 0.7 copy-start.3

commit v9 on v8

--- a/solution.py
+++ b/solution.py
@@ -60,7 +60,14 @@
         out_ref[:, i * span : (i + 1) * span] = jnp.where(used > 0, 0.0, -jnp.inf)
 
 
-def hard_kernel(mask_ref, q_ref, p0, p1, p2, p3, out_ref):
+def hard_kernel(place_ref, pos_ref, mask_ref, q_ref, p0, p1, p2, p3, out_ref, order_ref, column_ref):
+    total, rows = order_ref.shape[0], q_ref.shape[0]
+    place = (place_ref[0], place_ref[1], place_ref[2])
+    left_index = passage((1, total), 1, place, True)
+    right_index = passage((total, 1), 0, place, False)
+    order_ref[...] = jnp.where(right_index == left_index, 1.0, 0.0).astype(jnp.bfloat16)
+    eye = lax.broadcasted_iota(jnp.int32, (rows, rows), 0) == lax.broadcasted_iota(jnp.int32, (rows, rows), 1)
+    column_ref[...] = jnp.sum(jnp.where(eye, pos_ref[...].astype(jnp.float32), 0.0), axis=1, keepdims=True)
     span = p0.shape[0]
     for i, pool in enumerate((p0, p1, p2, p3)):
         at = slice(i * span, (i + 1) * span)
@@ -124,7 +131,7 @@
     give_ref[at + 1] = right_ref[1]
 
 
-def tail_kernel(place_ref, pos_ref, hard_ref, q_ref, *rest):
+def tail_kernel(place_ref, column_ref, hard_ref, order_ref, q_ref, *rest):
     blocks, (p0, p1, p2, p3), (grad_ref, loss_ref, left_ref, right_ref) = rest[:11], rest[11:15], rest[15:19]
     out_ref, sems = rest[19:]
     keep, l1, r1, e1, l2, r2, l3, r3, e23, l4, r4 = blocks
@@ -138,8 +145,7 @@
 
     place = (place_ref[0], place_ref[1], place_ref[2])
     left_index = passage((1, total), 1, place, True)
-    right_index = passage((total, 1), 0, place, False)
-    order = jnp.where(right_index == left_index, 1.0, 0.0).astype(jnp.bfloat16)
+    order = order_ref[...]
     right_logits = dots(q_ref[:, half:], right_ref[...])
     high = right_logits.astype(jnp.bfloat16)
     left_over = right_logits - high.astype(jnp.float32)
@@ -157,8 +163,7 @@
     denominator = jnp.sum(cycle_exp, axis=1, keepdims=True) + jnp.sum(hard_exp, axis=1, keepdims=True)
     rows = q_ref.shape[0]
     eye = lax.broadcasted_iota(jnp.int32, (rows, rows), 0) == lax.broadcasted_iota(jnp.int32, (rows, rows), 1)
-    positives = jnp.sum(jnp.where(eye, pos_ref[...].astype(jnp.float32), 0.0), axis=1, keepdims=True)
-    positive = left_index == positives.astype(jnp.int32)
+    positive = left_index == column_ref[...].astype(jnp.int32)
     chosen = jnp.sum(jnp.where(positive, logits, 0.0), axis=1, keepdims=True)
     loss = jnp.log(denominator) + peak - chosen
     loss_ref[...] = jnp.sum(jnp.where(eye, loss, 0.0), axis=0, keepdims=True)
@@ -203,9 +208,13 @@
     return small_call(mask_kernel, out, (place, refs.T, count.reshape(1, rows), lists[0]), "mask", scalars=1)
 
 
-def hard_call(mask, queries, pools):
+def hard_call(place, positive, mask, queries, pools):
+    rows = queries.shape[0]
     out = jax.ShapeDtypeStruct(mask.shape, mask.dtype)
-    return small_call(hard_kernel, out, (mask, queries, *pools), "hard", flops=2**34)
+    order = jax.ShapeDtypeStruct((8 * BLOCK, 8 * BLOCK), jnp.bfloat16)
+    column = jax.ShapeDtypeStruct((rows, 1), jnp.float32)
+    args = (place, positive.reshape(1, rows), mask, queries, *pools)
+    return small_call(hard_kernel, (out, order, column), args, "hard", scalars=1, flops=2**34)
 
 
 def copies_call(passages):
@@ -225,7 +234,7 @@
     return small_call(hand_kernel, (one, one, out), (left, right, *waiting), "hand", flops=flops)
 
 
-def tail_call(place, positive, hard, queries, blocks, pools):
+def tail_call(place, column, hard, order, queries, blocks, pools):
     rows, width = queries.shape
     half = width // 2
     return pl.pallas_call(
@@ -234,7 +243,7 @@
             jax.ShapeDtypeStruct((rows, width), jnp.bfloat16),
             jax.ShapeDtypeStruct((1, rows), jnp.float32),
         ),
-        in_specs=[SMEM()] + [VMEM()] * (3 + len(blocks) + len(pools)),
+        in_specs=[SMEM()] + [VMEM()] * (4 + len(blocks) + len(pools)),
         out_specs=(pl.BlockSpec(memory_space=pl.ANY), VMEM()),
         scratch_shapes=[
             pltpu.VMEM((8 * BLOCK, half), jnp.bfloat16),
@@ -245,7 +254,7 @@
         compiler_params=pltpu.CompilerParams(vmem_limit_bytes=16 * 2**20),
         cost_estimate=pl.CostEstimate(flops=2**31, bytes_accessed=12 * 2**20, transcendentals=2**17),
         name="tail",
-    )(place, positive.reshape(1, rows), hard, queries, *blocks, *pools)
+    )(place, column, hard, order, queries, *blocks, *pools)
 
 
 def body(queries, passages, pool, positive_ids, request_lists, hard_refs, hard_count):
@@ -292,8 +301,8 @@
     with jax.named_scope("other_pools"):
         pool_xc = lax.ppermute(pool_x, "d", OTHER_CORE)
         pools = (pool, pool_c, pool_x, pool_xc)
-        hard = hard_call(mask, queries, pools)
-    grad, loss = tail_call(place, positive_ids, hard, queries, blocks + last, pools)
+        hard, order, column = hard_call(place, positive_ids, mask, queries, pools)
+    grad, loss = tail_call(place, column, hard, order, queries, blocks + last, pools)
     return grad, loss.reshape(-1)
 
 

time: 110 us -> 110 us (level)
  transfers between devices with their start and end apart: 15 -> 15, of which waited for: 7 -> 7; matrix products, arithmetic and copies ran while one was open for 0% -> 0% of each run, Pallas kernels for 3% -> 4%
where the time goes in v9:
time: 110 us; the launch traced here: 109 us
  starting transfers between devices  62.2 us (57%)
  blocking collectives  19.2 us (17%)
  waiting for transfers between devices  15.3 us (14%)
  Pallas kernels  9.73 us (9%)
  local copies, waits for them, and re-layouts  1.54 us (1%)
    ppermute x3, starting transfers between devices, body(): lax.ppermute(left, 'd', RING_Z)  20.2 us
    all_to_all x1, blocking collectives, body(): near = lax.all_to_all(sent, 'd', 0, 0, axis_index_groups=NEAR, tiled=True)  19.2 us
    all_to_all x1, starting transfers between devices, body(): lax.all_to_all(copies_call(passages), 'd', 0, 0, axis_index_groups=CROSS,...  17.4 us
    ppermute x3, starting transfers between devices, body(): lax.ppermute(right, 'd', RING_Y)  5.76 us
    all_to_all x1, waiting for transfers between devices, body(): lax.all_to_all(copies_call(passages), 'd', 0, 0, axis_index_groups=CROSS,...  5.72 us
    pallas_call x1, Pallas kernels, tail_call(): pl.pallas_call(tail_kernel, out_shape=(jax.ShapeDtypeStruct((rows, width)...  5.12 us
    ppermute x3, waiting for transfers between devices, body(): lax.ppermute(left, 'd', RING_Z)  4.64 us
    pallas_call x7, Pallas kernels, small_call(): pl.pallas_call(kernel, out_shape=outs, in_specs=[SMEM()] * scalars + [VME...  4.61 us
  transfers between devices with their start and end apart: 15, of which 7 were waited for; matrix products, arithmetic and copies ran while one was open for 0% of the time, Pallas kernels for 4%

profile of v9, /device:TPU:1, one launch (start us, length us, event | category | flops | bytes accessed | tf_op | source)
XLA Modules:
  0.0 108.8 jit_solution(6837736644045414450)
XLA Ops:
  0.6 0.0 copy-start.2
  0.6 0.7 copy-done.2
  1.3 0.6 copies.1
  2.0 17.4 %all-to-all-start = ((bf16[8,2,2048]{2,1,0:T(2,128)(2,1)}), bf16[8,2,2048]{2,1,0:T(2,128)(2,1)S(1)}, u32[]{:S(2)}, u32[]{:S(2)}) async-start(bf16[8,2,2048]{2,1,0:T(2,128)(2,1)} %copies.1), calls=%async_computation | async-start | bytes 131072 | tf_op jit(solution)/shard_map/cross/all_to_all | solution.py:267
  19.4 0.0 copy-start.3
  19.4 0.1 pad_add_fusion.place_ref
  19.5 0.0 copy-start.4
  19.5 0.0 copy-start.5
  19.5 0.6 copy-done.3
  20.1 0.0 copy-done.4
  20.2 0.0 copy-done.5
  20.2 1.0 mask.1.mask_ref
  21.1 0.0 copy-start.1
  21.1 5.7 %all-to-all-done = bf16[8,2,2048]{2,1,0:T(2,128)(2,1)S(1)} async-done(((bf16[8,2,2048]{2,1,0:T(2,128)(2,1)}), bf16[8,2,2048]{2,1,0:T(2,128)(2,1)S(1)}, u32[]{:S(2)}, u32[]{:S(2)}) %all-to-all-start) | async-done | bytes 65568 | tf_op jit(solution)/shard_map/cross/all_to_all | solution.py:267
  27.0 19.2 %all_to_all.10.mine_ref = bf16[8,16,2048]{2,1,0:T(8,128)(2,1)S(1)} all-to-all(bf16[8,16,2048]{2,1,0:T(8,128)(2,1)S(1)} %broadcast_in_dim.8), channel_id=1, replica_groups={{0,4,8,12,16,20,24,28},{2,6,10,14,18,22,26,30},{32,36,40,44,48,52,56,60..., dimensions={0} | all-to-all | bytes 1048576 | tf_op jit(solution)/shard_map/near/all_to_all | solution.py:274
  46.2 1.9 %collective-permute-start = (bf16[8,16,2048]{2,1,0:T(8,128)(2,1)S(1)}, bf16[8,16,2048]{2,1,0:T(8,128)(2,1)S(1)}, u32[]{:S(2)}, u32[]{:S(2)}) collective-permute-start(bf16[8,16,2048]{2,1,0:T(8,128)(2,1)S(1)} %all_to_all.10.mine_ref), channel_id=1, source_target_pairs={{0,1},{1,0},{2,3},{3,2},{4,5},{5,4},{6,7},{7,6},{8,9},{9,8},{10,11... | collective-permute-start | bytes 1572872 | tf_op jit(solution)/shard_map/near/ppermute | solution.py:275
  48.1 0.0 copy-done.1
  48.1 2.4 %collective-permute-start.2 = (bf16[128,4096]{1,0:T(8,128)(2,1)S(1)}, bf16[128,4096]{1,0:T(8,128)(2,1)S(1)}, u32[]{:S(2)}, u32[]{:S(2)}) collective-permute-start(bf16[128,4096]{1,0:T(8,128)(2,1)S(1)} %copy-done.1), channel_id=1, source_target_pairs={{0,1},{1,0},{2,3},{3,2},{4,5},{5,4},{6,7},{7,6},{8,9},{9,8},{10,11... | collective-permute-start | bytes 3145736 | tf_op jit(solution)/shard_map/ring/ppermute | solution.py:283
  50.5 0.0 collective-permute-done.theirs_ref
  50.5 0.7 sort.1
  51.2 9.6 %collective-permute-start.1 = (bf16[2,64,2048]{2,1,0:T(8,128)(2,1)S(1)}, bf16[2,64,2048]{2,1,0:T(8,128)(2,1)S(1)}, u32[]{:S(2)}, u32[]{:S(2)}) collective-permute-start(bf16[2,64,2048]{2,1,0:T(8,128)(2,1)S(1)} %get-tuple-element.36), channel_id=1, source_target_pairs={{0,128},{128,256},{256,384},{384,512},{512,640},{640,768},{768,896... | collective-permute-start | bytes 1572872 | tf_op jit(solution)/shard_map/ring/ppermute | solution.py:282
  60.8 1.9 %collective-permute-start.7 = (bf16[2,64,2048]{2,1,0:T(8,128)(2,1)S(1)}, bf16[2,64,2048]{2,1,0:T(8,128)(2,1)S(1)}, u32[]{:S(2)}, u32[]{:S(2)}) collective-permute-start(bf16[2,64,2048]{2,1,0:T(8,128)(2,1)S(1)} %get-tuple-element.42), channel_id=1, source_target_pairs={{0,4},{4,8},{8,12},{12,16},{16,20},{20,24},{24,28},{28,0},{1,29},{... | collective-permute-start | bytes 1572872 | tf_op jit(solution)/shard_map/ring/ppermute | solution.py:282
  62.7 2.5 %collective-permute-start.5 = (bf16[128,4096]{1,0:T(8,128)(2,1)S(1)}, bf16[128,4096]{1,0:T(8,128)(2,1)S(1)}, u32[]{:S(2)}, u32[]{:S(2)}) collective-permute-start(bf16[128,4096]{1,0:T(8,128)(2,1)S(1)} %copy-done.1), channel_id=1, source_target_pairs={{0,2},{1,3},{2,0},{3,1},{4,6},{5,7},{6,4},{7,5},{8,10},{9,11},{10,... | collective-permute-start | bytes 3145736 | tf_op jit(solution)/shard_map/pool_x/ppermute | solution.py:279
  65.3 0.0 collective-permute-done.2.p1.rest_12_
  65.3 1.6 %collective-permute-done.1.left_ref = bf16[2,64,2048]{2,1,0:T(8,128)(2,1)S(1)} collective-permute-done((bf16[2,64,2048]{2,1,0:T(8,128)(2,1)S(1)}, bf16[2,64,2048]{2,1,0:T(8,128)(2,1)S(1)}, u32[]{:S(2)}, u32[]{:S(2)}) %collective-permute-start.1) | collective-permute-done | bytes 524320 | tf_op jit(solution)/shard_map/ring/ppermute | solution.py:282
  66.9 5.3 %collective-permute-start.3 = (bf16[2,64,2048]{2,1,0:T(8,128)(2,1)S(1)}, bf16[2,64,2048]{2,1,0:T(8,128)(2,1)S(1)}, u32[]{:S(2)}, u32[]{:S(2)}) collective-permute-start(bf16[2,64,2048]{2,1,0:T(8,128)(2,1)S(1)} %collective-permute-done.1.left_ref), channel_id=1, source_target_pairs={{0,128},{128,256},{256,384},{384,512},{512,640},{640,768},{768,896... | collective-permute-start | bytes 1572872 | tf_op jit(solution)/shard_map/ring/ppermute | solution.py:287
  72.2 0.0 collective-permute-done.7.right_ref
  72.2 1.9 %collective-permute-start.8 = (bf16[2,64,2048]{2,1,0:T(8,128)(2,1)S(1)}, bf16[2,64,2048]{2,1,0:T(8,128)(2,1)S(1)}, u32[]{:S(2)}, u32[]{:S(2)}) collective-permute-start(bf16[2,64,2048]{2,1,0:T(8,128)(2,1)S(1)} %collective-permute-done.7.right_ref), channel_id=1, source_target_pairs={{0,4},{4,8},{8,12},{12,16},{16,20},{20,24},{24,28},{28,0},{1,29},{... | collective-permute-start | bytes 1572872 | tf_op jit(solution)/shard_map/ring/ppermute | solution.py:287
  74.2 0.1 hand.3
  74.2 1.9 %collective-permute-start.10 = (bf16[2,64,2048]{2,1,0:T(8,128)(2,1)S(1)}, bf16[2,64,2048]{2,1,0:T(8,128)(2,1)S(1)}, u32[]{:S(2)}, u32[]{:S(2)}) collective-permute-start(bf16[2,64,2048]{2,1,0:T(8,128)(2,1)S(1)} %get-tuple-element.47), channel_id=1, source_target_pairs={{0,1},{1,0},{2,3},{3,2},{4,5},{5,4},{6,7},{7,6},{8,9},{9,8},{10,11... | collective-permute-start | bytes 1572872 | tf_op jit(solution)/shard_map/ring/ppermute | solution.py:299
  76.2 2.2 %collective-permute-done.3.left_ref = bf16[2,64,2048]{2,1,0:T(8,128)(2,1)S(1)} collective-permute-done((bf16[2,64,2048]{2,1,0:T(8,128)(2,1)S(1)}, bf16[2,64,2048]{2,1,0:T(8,128)(2,1)S(1)}, u32[]{:S(2)}, u32[]{:S(2)}) %collective-permute-start.3) | collective-permute-done | bytes 524320 | tf_op jit(solution)/shard_map/ring/ppermute | solution.py:287
  78.3 5.3 %collective-permute-start.4 = (bf16[2,64,2048]{2,1,0:T(8,128)(2,1)S(1)}, bf16[2,64,2048]{2,1,0:T(8,128)(2,1)S(1)}, u32[]{:S(2)}, u32[]{:S(2)}) collective-permute-start(bf16[2,64,2048]{2,1,0:T(8,128)(2,1)S(1)} %collective-permute-done.3.left_ref), channel_id=1, source_target_pairs={{0,128},{128,256},{256,384},{384,512},{512,640},{640,768},{768,896... | collective-permute-start | bytes 1572872 | tf_op jit(solution)/shard_map/ring/ppermute | solution.py:287
  83.6 0.0 collective-permute-done.8.right_ref
  83.7 1.9 %collective-permute-start.9 = (bf16[2,64,2048]{2,1,0:T(8,128)(2,1)S(1)}, bf16[2,64,2048]{2,1,0:T(8,128)(2,1)S(1)}, u32[]{:S(2)}, u32[]{:S(2)}) collective-permute-start(bf16[2,64,2048]{2,1,0:T(8,128)(2,1)S(1)} %collective-permute-done.8.right_ref), channel_id=1, source_target_pairs={{0,4},{4,8},{8,12},{12,16},{16,20},{20,24},{24,28},{28,0},{1,29},{... | collective-permute-start | bytes 1572872 | tf_op jit(solution)/shard_map/ring/ppermute | solution.py:287
  85.6 0.1 hand.4
  85.7 2.1 %collective-permute-start.12 = (bf16[1,64,2048]{2,1,0:T(8,128)(2,1)S(1)}, bf16[1,64,2048]{2,1,0:T(8,128)(2,1)S(1)}, u32[]{:S(2)}, u32[]{:S(2)}) collective-permute-start(bf16[1,64,2048]{2,1,0:T(8,128)(2,1)S(1)} %get-tuple-element.54.rest_4_), channel_id=1, source_target_pairs={{0,256},{128,384},{256,512},{384,640},{512,768},{640,896},{768,0},... | collective-permute-start | bytes 786440 | tf_op jit(solution)/shard_map/ring/ppermute | solution.py:297
  87.8 0.0 collective-permute-done.10.rest_3_
  87.8 1.9 %collective-permute-start.13 = (bf16[1,64,2048]{2,1,0:T(8,128)(2,1)S(1)}, bf16[1,64,2048]{2,1,0:T(8,128)(2,1)S(1)}, u32[]{:S(2)}, u32[]{:S(2)}) collective-permute-start(bf16[1,64,2048]{2,1,0:T(8,128)(2,1)S(1)} %get-tuple-element.55.rest_5_), channel_id=1, source_target_pairs={{0,8},{4,12},{8,16},{12,20},{16,24},{20,28},{24,0},{28,4},{1,25},{... | collective-permute-start | bytes 786440 | tf_op jit(solution)/shard_map/ring/ppermute | solution.py:297
  89.7 0.9 collective-permute-done.4.left_ref
  90.6 4.4 %collective-permute-done.9.right_ref = bf16[2,64,2048]{2,1,0:T(8,128)(2,1)S(1)} collective-permute-done((bf16[2,64,2048]{2,1,0:T(8,128)(2,1)S(1)}, bf16[2,64,2048]{2,1,0:T(8,128)(2,1)S(1)}, u32[]{:S(2)}, u32[]{:S(2)}) %collective-permute-start.9) | collective-permute-done | bytes 524320 | tf_op jit(solution)/shard_map/ring/ppermute | solution.py:287
  94.9 0.0 collective-permute-done.5.p2.rest_13_
  94.9 4.0 %collective-permute-start.6 = (bf16[128,4096]{1,0:T(8,128)(2,1)S(1)}, bf16[128,4096]{1,0:T(8,128)(2,1)S(1)}, u32[]{:S(2)}, u32[]{:S(2)}) collective-permute-start(bf16[128,4096]{1,0:T(8,128)(2,1)S(1)} %collective-permute-done.5.p2.rest_13_), channel_id=1, source_target_pairs={{0,1},{1,0},{2,3},{3,2},{4,5},{5,4},{6,7},{7,6},{8,9},{9,8},{10,11... | collective-permute-start | bytes 3145736 | tf_op jit(solution)/shard_map/other_pools/ppermute | solution.py:302
  98.9 0.0 copy-start
  98.9 0.1 hand.5
  99.0 0.0 copy-start.6
  99.0 2.1 %collective-permute-start.11 = (bf16[4,64,2048]{2,1,0:T(8,128)(2,1)S(1)}, bf16[4,64,2048]{2,1,0:T(8,128)(2,1)S(1)}, u32[]{:S(2)}, u32[]{:S(2)}) collective-permute-start(bf16[4,64,2048]{2,1,0:T(8,128)(2,1)S(1)} %get-tuple-element.61), channel_id=1, source_target_pairs={{0,1},{1,0},{2,3},{3,2},{4,5},{5,4},{6,7},{7,6},{8,9},{9,8},{10,11... | collective-permute-start | bytes 3145736 | tf_op jit(solution)/shard_map/ring/ppermute | solution.py:299
  101.1 0.1 collective-permute-done.6.p3.rest_14_
  101.2 0.0 copy-done
  101.2 0.0 copy-done.6
  101.2 2.1 %hard.1 = (f32[128,512]{1,0:T(8,128)S(1)}, bf16[512,512]{1,0:T(8,128)(2,1)S(1)}, f32[128,1]{1,0:T(8,128)S(1)}) custom-call(s32[4]{0:T(128)S(1)} %pad_add_fusion.place_ref, s32[1,128]{1,0:T(1,128)S(1)} %bitcast.15, f32[128,512]{1,0:T(8,128)S(1)} %mask.1.mask_ref, bf16[128,4096]{1,0:T(8,128)(2,1)S(1)} %copy-done, bf16[128,4096]{1,0:T(8,128)(2,1)S(1)} %copy-done.1, ...), custom_call_target="tpu_custom_call" | custom-call | flops 17179869184 | bytes 4194304 | tf_op jit(solution)/shard_map/other_pools/hard/pallas_call | solution.py:194
  103.3 0.0 collective-permute-done.12.rest_9_
  103.3 0.0 collective-permute-done.13.rest_10_
  103.3 0.4 collective-permute-done.11.rest_8_
  103.7 5.1 %tail.1 = (bf16[128,4096]{1,0:T(8,128)(2,1)}, f32[1,128]{1,0:T(1,128)}) custom-call(s32[4]{0:T(128)S(1)} %pad_add_fusion.place_ref, f32[128,1]{1,0:T(8,128)S(1)} %get-tuple-element.39.column_ref, f32[128,512]{1,0:T(8,128)S(1)} %get-tuple-element.40.hard_ref, bf16[512,512]{1,0:T(8,128)(2,1)S(1)} %get-tuple-element.41.order_ref, ...), custom_call_target="tpu_custom_call" | custom-call | flops 2147483648 | bytes 12582912 | tf_op jit(solution)/shard_map/tail/pallas_call | solution.py:240
  (3 shorter events, 0.1 us)
Async XLA Ops:
  0.6 0.7 copy-start.2
  2.0 24.9 %all-to-all-start = ((bf16[8,2,2048]{2,1,0:T(2,128)(2,1)}), bf16[8,2,2048]{2,1,0:T(2,128)(2,1)S(1)}, u32[]{:S(2)}, u32[]{:S(2)}) async-start(bf16[8,2,2048]{2,1,0:T(2,128)(2,1)} %copies.1), calls=%async_computation | async-start | bytes 131072 | tf_op jit(solution)/shard_map/cross/all_to_all | solution.py:267
  19.4 0.7 copy-start.3
  19.5 0.7 copy-start.4
  19.5 0.7 copy-start.5
  21.1 27.0 %copy-start.1 = (bf16[128,4096]{1,0:T(8,128)(2,1)S(1)}, bf16[128,4096]{1,0:T(8,128)(2,1)}, u32[]{:S(2)}) copy-start(bf16[128,4096]{1,0:T(8,128)(2,1)} %rest_11_) | copy-start | bytes 3145732
  46.2 4.3 %collective-permute-start = (bf16[8,16,2048]{2,1,0:T(8,128)(2,1)S(1)}, bf16[8,16,2048]{2,1,0:T(8,128)(2,1)S(1)}, u32[]{:S(2)}, u32[]{:S(2)}) collective-permute-start(bf16[8,16,2048]{2,1,0:T(8,128)(2,1)S(1)} %all_to_all.10.mine_ref), channel_id=1, source_target_pairs={{0,1},{1,0},{2,3},{3,2},{4,5},{5,4},{6,7},{7,6},{8,9},{9,8},{10,11... | collective-permute-start | bytes 1572872 | tf_op jit(solution)/shard_map/near/ppermute | solution.py:275
  48.1 17.2 %collective-permute-start.2 = (bf16[128,4096]{1,0:T(8,128)(2,1)S(1)}, bf16[128,4096]{1,0:T(8,128)(2,1)S(1)}, u32[]{:S(2)}, u32[]{:S(2)}) collective-permute-start(bf16[128,4096]{1,0:T(8,128)(2,1)S(1)} %copy-done.1), channel_id=1, source_target_pairs={{0,1},{1,0},{2,3},{3,2},{4,5},{5,4},{6,7},{7,6},{8,9},{9,8},{10,11... | collective-permute-start | bytes 3145736 | tf_op jit(solution)/shard_map/ring/ppermute | solution.py:283
  51.2 15.7 %collective-permute-start.1 = (bf16[2,64,2048]{2,1,0:T(8,128)(2,1)S(1)}, bf16[2,64,2048]{2,1,0:T(8,128)(2,1)S(1)}, u32[]{:S(2)}, u32[]{:S(2)}) collective-permute-start(bf16[2,64,2048]{2,1,0:T(8,128)(2,1)S(1)} %get-tuple-element.36), channel_id=1, source_target_pairs={{0,128},{128,256},{256,384},{384,512},{512,640},{640,768},{768,896... | collective-permute-start | bytes 1572872 | tf_op jit(solution)/shard_map/ring/ppermute | solution.py:282
  60.8 11.4 %collective-permute-start.7 = (bf16[2,64,2048]{2,1,0:T(8,128)(2,1)S(1)}, bf16[2,64,2048]{2,1,0:T(8,128)(2,1)S(1)}, u32[]{:S(2)}, u32[]{:S(2)}) collective-permute-start(bf16[2,64,2048]{2,1,0:T(8,128)(2,1)S(1)} %get-tuple-element.42), channel_id=1, source_target_pairs={{0,4},{4,8},{8,12},{12,16},{16,20},{20,24},{24,28},{28,0},{1,29},{... | collective-permute-start | bytes 1572872 | tf_op jit(solution)/shard_map/ring/ppermute | solution.py:282
  62.7 32.2 %collective-permute-start.5 = (bf16[128,4096]{1,0:T(8,128)(2,1)S(1)}, bf16[128,4096]{1,0:T(8,128)(2,1)S(1)}, u32[]{:S(2)}, u32[]{:S(2)}) collective-permute-start(bf16[128,4096]{1,0:T(8,128)(2,1)S(1)} %copy-done.1), channel_id=1, source_target_pairs={{0,2},{1,3},{2,0},{3,1},{4,6},{5,7},{6,4},{7,5},{8,10},{9,11},{10,... | collective-permute-start | bytes 3145736 | tf_op jit(solution)/shard_map/pool_x/ppermute | solution.py:279
  66.9 11.4 %collective-permute-start.3 = (bf16[2,64,2048]{2,1,0:T(8,128)(2,1)S(1)}, bf16[2,64,2048]{2,1,0:T(8,128)(2,1)S(1)}, u32[]{:S(2)}, u32[]{:S(2)}) collective-permute-start(bf16[2,64,2048]{2,1,0:T(8,128)(2,1)S(1)} %collective-permute-done.1.left_ref), channel_id=1, source_target_pairs={{0,128},{128,256},{256,384},{384,512},{512,640},{640,768},{768,896... | collective-permute-start | bytes 1572872 | tf_op jit(solution)/shard_map/ring/ppermute | solution.py:287
  72.2 11.4 %collective-permute-start.8 = (bf16[2,64,2048]{2,1,0:T(8,128)(2,1)S(1)}, bf16[2,64,2048]{2,1,0:T(8,128)(2,1)S(1)}, u32[]{:S(2)}, u32[]{:S(2)}) collective-permute-start(bf16[2,64,2048]{2,1,0:T(8,128)(2,1)S(1)} %collective-permute-done.7.right_ref), channel_id=1, source_target_pairs={{0,4},{4,8},{8,12},{12,16},{16,20},{20,24},{24,28},{28,0},{1,29},{... | collective-permute-start | bytes 1572872 | tf_op jit(solution)/shard_map/ring/ppermute | solution.py:287
  74.2 13.5 %collective-permute-start.10 = (bf16[2,64,2048]{2,1,0:T(8,128)(2,1)S(1)}, bf16[2,64,2048]{2,1,0:T(8,128)(2,1)S(1)}, u32[]{:S(2)}, u32[]{:S(2)}) collective-permute-start(bf16[2,64,2048]{2,1,0:T(8,128)(2,1)S(1)} %get-tuple-element.47), channel_id=1, source_target_pairs={{0,1},{1,0},{2,3},{3,2},{4,5},{5,4},{6,7},{7,6},{8,9},{9,8},{10,11... | collective-permute-start | bytes 1572872 | tf_op jit(solution)/shard_map/ring/ppermute | solution.py:299
  78.3 12.2 %collective-permute-start.4 = (bf16[2,64,2048]{2,1,0:T(8,128)(2,1)S(1)}, bf16[2,64,2048]{2,1,0:T(8,128)(2,1)S(1)}, u32[]{:S(2)}, u32[]{:S(2)}) collective-permute-start(bf16[2,64,2048]{2,1,0:T(8,128)(2,1)S(1)} %collective-permute-done.3.left_ref), channel_id=1, source_target_pairs={{0,128},{128,256},{256,384},{384,512},{512,640},{640,768},{768,896... | collective-permute-start | bytes 1572872 | tf_op jit(solution)/shard_map/ring/ppermute | solution.py:287
  83.7 11.3 %collective-permute-start.9 = (bf16[2,64,2048]{2,1,0:T(8,128)(2,1)S(1)}, bf16[2,64,2048]{2,1,0:T(8,128)(2,1)S(1)}, u32[]{:S(2)}, u32[]{:S(2)}) collective-permute-start(bf16[2,64,2048]{2,1,0:T(8,128)(2,1)S(1)} %collective-permute-done.8.right_ref), channel_id=1, source_target_pairs={{0,4},{4,8},{8,12},{12,16},{16,20},{20,24},{24,28},{28,0},{1,29},{... | collective-permute-start | bytes 1572872 | tf_op jit(solution)/shard_map/ring/ppermute | solution.py:287
  85.7 17.6 %collective-permute-start.12 = (bf16[1,64,2048]{2,1,0:T(8,128)(2,1)S(1)}, bf16[1,64,2048]{2,1,0:T(8,128)(2,1)S(1)}, u32[]{:S(2)}, u32[]{:S(2)}) collective-permute-start(bf16[1,64,2048]{2,1,0:T(8,128)(2,1)S(1)} %get-tuple-element.54.rest_4_), channel_id=1, source_target_pairs={{0,256},{128,384},{256,512},{384,640},{512,768},{640,896},{768,0},... | collective-permute-start | bytes 786440 | tf_op jit(solution)/shard_map/ring/ppermute | solution.py:297
  87.8 15.5 %collective-permute-start.13 = (bf16[1,64,2048]{2,1,0:T(8,128)(2,1)S(1)}, bf16[1,64,2048]{2,1,0:T(8,128)(2,1)S(1)}, u32[]{:S(2)}, u32[]{:S(2)}) collective-permute-start(bf16[1,64,2048]{2,1,0:T(8,128)(2,1)S(1)} %get-tuple-element.55.rest_5_), channel_id=1, source_target_pairs={{0,8},{4,12},{8,16},{12,20},{16,24},{20,28},{24,0},{28,4},{1,25},{... | collective-permute-start | bytes 786440 | tf_op jit(solution)/shard_map/ring/ppermute | solution.py:297
  94.9 6.2 %collective-permute-start.6 = (bf16[128,4096]{1,0:T(8,128)(2,1)S(1)}, bf16[128,4096]{1,0:T(8,128)(2,1)S(1)}, u32[]{:S(2)}, u32[]{:S(2)}) collective-permute-start(bf16[128,4096]{1,0:T(8,128)(2,1)S(1)} %collective-permute-done.5.p2.rest_13_), channel_id=1, source_target_pairs={{0,1},{1,0},{2,3},{3,2},{4,5},{5,4},{6,7},{7,6},{8,9},{9,8},{10,11... | collective-permute-start | bytes 3145736 | tf_op jit(solution)/shard_map/other_pools/ppermute | solution.py:302
  98.9 2.3 %copy-start = (bf16[128,4096]{1,0:T(8,128)(2,1)S(1)}, bf16[128,4096]{1,0:T(8,128)(2,1)}, u32[]{:S(2)}) copy-start(bf16[128,4096]{1,0:T(8,128)(2,1)} %q_ref.3) | copy-start | bytes 3145732
  99.0 2.1 %copy-start.6 = (s32[128]{0:T(128)S(1)}, s32[128]{0:T(128)}, u32[]{:S(2)}) copy-start(s32[128]{0:T(128)} %param.10) | copy-start | bytes 1540
  99.0 4.7 %collective-permute-start.11 = (bf16[4,64,2048]{2,1,0:T(8,128)(2,1)S(1)}, bf16[4,64,2048]{2,1,0:T(8,128)(2,1)S(1)}, u32[]{:S(2)}, u32[]{:S(2)}) collective-permute-start(bf16[4,64,2048]{2,1,0:T(8,128)(2,1)S(1)} %get-tuple-element.61), channel_id=1, source_target_pairs={{0,1},{1,0},{2,3},{3,2},{4,5},{5,4},{6,7},{7,6},{8,9},{9,8},{10,11... | collective-permute-start | bytes 3145736 | tf_op jit(solution)/shard_map/ring/ppermute | solution.py:299
